TPU v7x, 32 devices: a whole 2x2x4 slice. The times are simulated.
32 devices in a mesh: groups: 2 (over y), gx: 4 (over z), gy: 2 (over x), ta: 2 (over core).
Axes of the slice: x: 2, y: 2, z: 4, core: 2. Of those that a mesh axis runs over, the one named last changes fastest.
Arguments:
- frames: bfloat16 [4, 128, 16, 4, 512], P('gx', ('groups', 'ta'), None, 'gy'), parts along dimension 1, may hold values from -6 to 6
- start_state: float32 [128, 16, 4, 256], P(('groups', 'ta'), 'gx', 'gy'), parts along dimension 0, may hold values from -0.9 to 0.9
- tile_index: int32 [16, 4, 5], P('gx', 'gy'), may hold values from 0 to 7, as said below
- tile_bank: bfloat16 [8, 256, 256], replicated, may hold values from -1.25 to 1.25
- inlet_coupler: bfloat16 [512, 256], replicated, may hold values from -0.0546875 to 0.0546875
- readout_operator: bfloat16 [512, 512], replicated, may hold values from -0.25 to 0.25
Outputs:
- predicted_field: bfloat16 [128, 16, 4, 512], P(('groups', 'ta'), 'gx', 'gy'), parts along dimension 0
- final_state: float32 [128, 16, 4, 256], P(('groups', 'ta'), 'gx', 'gy'), parts along dimension 0
There are 2 independent parts, one for each index of `groups`. A program takes and returns all parts, laid end to end along the dimension named above; an argument that names none is the same for every part. Nothing has to cross between parts.
Inputs may be any that keep to these rules, and one draw needn't show every extreme that they name: tile_index[x, y, 0], the tile that joins a block to itself, is below 4; the four neighbour entries are 4 or more.
All inputs are finite; a program needn't handle non-finite values.
Results may differ from a plain program's by a relative error of at most 0.0067.
Values may be sent and summed in bfloat16 or wider, within the bound.
No kernel may reach another device: no remote copies, remote signals or barrier semaphores. Data moves between devices by JAX's collectives and lax.ppermute only.
A program may use at most 64 MiB of HBM per device.

v0:
```python
import jax
import jax.numpy as jnp
from jax import lax
from jax.sharding import PartitionSpec as P


def with_halo(cells, sides, width):
    for axis, dim in sides:
        count = lax.axis_size(axis)
        head = lax.slice_in_dim(cells, 0, width, axis=dim)
        tail = lax.slice_in_dim(cells, cells.shape[dim] - width, cells.shape[dim], axis=dim)
        cells = jnp.concatenate(
            [
                lax.ppermute(tail, axis, [(i, (i + 1) % count) for i in range(count)]),
                cells,
                lax.ppermute(head, axis, [((i + 1) % count, i) for i in range(count)]),
            ],
            axis=dim,
        )
    return cells


def shards(frames, start_state, tile_index, tile_bank, inlet_coupler, readout_operator):
    patch_site_total = inlet_coupler.shape[0]
    hidden_node_total = inlet_coupler.shape[1]
    prediction_span = frames.shape[:-1]
    unrolled = jnp.dot(
        frames.reshape(-1, patch_site_total), inlet_coupler, preferred_element_type=jnp.float32
    )
    projected = unrolled.astype(jnp.bfloat16).reshape(prediction_span + (hidden_node_total,))
    input_signal = lax.all_to_all(projected, "gx", split_axis=2, concat_axis=0, tiled=True)
    chosen_tiles = tile_bank[tile_index]

    def advance(step_index, echo_system):
        state_half = echo_system.astype(jnp.bfloat16)
        extended = with_halo(state_half, (("gx", 1), ("gy", 2)), 1)
        adjacent_blocks = jnp.stack(
            [
                extended[:, 1:-1, 1:-1],
                extended[:, :-2, 1:-1],
                extended[:, 2:, 1:-1],
                extended[:, 1:-1, :-2],
                extended[:, 1:-1, 2:],
            ],
            axis=0,
        )
        coupled = jnp.einsum(
            "kcxyu,xykuv->cxyv", adjacent_blocks, chosen_tiles, preferred_element_type=jnp.float32
        )
        drive_now = lax.dynamic_index_in_dim(input_signal, step_index, 0, keepdims=False)
        return jnp.tanh(coupled + drive_now.astype(jnp.float32))

    echo_system = lax.fori_loop(0, input_signal.shape[0], advance, start_state)
    readout_basis = jnp.concatenate([echo_system, echo_system * echo_system], axis=-1).astype(
        jnp.bfloat16
    )
    prediction_span = readout_basis.shape[:-1]
    predicted_field = jnp.dot(
        readout_basis.reshape(-1, 2 * hidden_node_total),
        readout_operator,
        preferred_element_type=jnp.float32,
    )
    predicted_field = predicted_field.astype(jnp.bfloat16).reshape(
        prediction_span + (patch_site_total,)
    )
    return (predicted_field, echo_system)


def solution(mesh):
    placed = (
        P("gx", ("groups", "ta"), None, "gy", None),
        P(("groups", "ta"), "gx", "gy", None),
        P("gx", "gy", None),
        P(),
        P(),
        P(),
    )
    return jax.shard_map(
        shards,
        mesh=mesh,
        in_specs=placed,
        out_specs=(P(("groups", "ta"), "gx", "gy", None), P(("groups", "ta"), "gx", "gy", None)),
        check_vma=False,
    )
```

profile of v0, /device:TPU:0, one launch (start us, length us, event | category | flops | bytes accessed | tf_op | source)
XLA Modules:
  0.0 89.4 jit_solution(13063251913147973936)
XLA Ops:
  0.6 0.0 copy-start
  0.6 0.0 copy-start.2
  0.7 0.0 copy-start.1
  0.7 1.6 %reshape.20 = bf16[1024,512]{1,0:T(8,128)(2,1)S(1)} reshape(bf16[1,32,16,2,512]{4,3,2,1,0:T(2,128)(2,1)} %param.8) | data formatting | bytes 2097152 | tf_op jit(solution)/shard_map/reshape | solution.py:28
  2.2 1.4 %convolution_convert_fusion = bf16[1024,256]{1,0:T(8,128)(2,1)S(1)} fusion(bf16[1024,512]{1,0:T(8,128)(2,1)S(1)} %reshape.20, bf16[512,256]{1,0:T(8,128)(2,1)} %param.12), kind=kOutput, calls=%fused_computation.22 | convolution fusion | flops 268697600 | bytes 1835008 | tf_op jit(solution)/shard_map/dot_general | solution.py:27
  3.6 0.2 reshape.21
  3.8 1.3 %copy.28 = bf16[1,32,16,2,256]{4,3,1,0,2:T(2,128)(2,1)} copy(bf16[1,32,16,2,256]{4,3,2,1,0:T(2,128)(2,1)S(1)} %reshape.21) | data formatting | bytes 1048576 | tf_op jit(solution)/shard_map/reshape | solution.py:30
  5.2 6.3 %all-to-all-start = ((bf16[1,32,16,2,256]{4,3,1,0,2:T(2,128)(2,1)}), bf16[1,32,16,2,256]{4,3,1,0,2:T(2,128)(2,1)S(1)}, u32[]{:S(2)}, u32[]{:S(2)}) async-start(bf16[1,32,16,2,256]{4,3,1,0,2:T(2,128)(2,1)} %copy.28), calls=%async_computation | async-start | bytes 1048576 | tf_op jit(solution)/shard_map/all_to_all | solution.py:31
  11.5 0.0 copy-done.2
  11.5 0.1 reshape.26
  11.6 0.0 copy-done.1
  11.6 0.1 copy.30
  11.7 0.0 copy-done
  11.7 4.6 %gather_fusion = bf16[40,256,256]{2,1,0:T(8,128)(2,1)} fusion(bf16[8,256,256]{2,1,0:T(8,128)(2,1)S(1)} %copy-done, s32[1024]{0:T(1024)S(1)} %pad_clamp_fusion), kind=kCustom, calls=%fused_computation | custom fusion | bytes 10485920 | tf_op jit(solution)/shard_map/gather | solution.py:32
  16.3 9.7 %all-to-all-done = bf16[1,32,16,2,256]{4,3,1,0,2:T(2,128)(2,1)S(1)} async-done(((bf16[1,32,16,2,256]{4,3,1,0,2:T(2,128)(2,1)}), bf16[1,32,16,2,256]{4,3,1,0,2:T(2,128)(2,1)S(1)}, u32[]{:S(2)}, u32[]{:S(2)}) %all-to-all-start) | async-done | bytes 524320 | tf_op jit(solution)/shard_map/all_to_all | solution.py:31
  26.0 0.1 copy.36
  26.1 0.0 copy-start.3
  26.1 60.9 %while.13 = (s32[]{:T(128)}, f32[32,4,2,256]{3,0,2,1:T(8,128)S(1)}, bf16[4,2,5,256,256]{4,3,2,1,0:T(8,128)(2,1)}, bf16[4,32,4,2,256]{4,1,3,2,0:T(8,128)(2,1)S(1)}, s32[]{:T(128)}) while((s32[]{:T(128)}, f32[32,4,2,256]{3,0,2,1:T(8,128)S(1)}, bf16[4,2,5,256,256]{4,3,2,1,0:T(8,128)(2,1)}, bf16[4,32,4,2,256]{4,1,3,2,0:T(8,128)(2,1)S(1)}, ...), condition=%wide.region_1.2_spmd, body=%wide.region_0.1_spmd.sunk | while | flops 169738240 | bytes 10223849 | solution.py:53
  26.1 0.1 collective-permute-start
  26.2 3.8 %collective-permute-start.1 = (bf16[32,1,2,256]{3,0,2,1:T(8,128)(2,1)S(1)}, bf16[32,1,2,256]{3,0,2,1:T(8,128)(2,1)S(1)}, u32[]{:S(2)}, u32[]{:S(2)}) collective-permute-start(bf16[32,1,2,256]{3,0,2,1:T(8,128)(2,1)S(1)} %get-tuple-element.150), channel_id=1, source_target_pairs={{4,0},{8,4},{12,8},{0,12},{5,1},{9,5},{13,9},{1,13},{6,2},{10,6},{... | collective-permute-start | bytes 98312 | tf_op jit(solution)/shard_map/while/body/eval_jaxpr/ppermute | solution.py:16
  30.0 1.9 %collective-permute-done = bf16[32,1,2,256]{3,0,2,1:T(8,128)(2,1)S(1)} collective-permute-done((bf16[32,1,2,256]{3,0,2,1:T(8,128)(2,1)S(1)}, bf16[32,1,2,256]{3,0,2,1:T(8,128)(2,1)S(1)}, u32[]{:S(2)}, u32[]{:S(2)}) %collective-permute-start) | collective-permute-done | bytes 32800 | tf_op jit(solution)/shard_map/while/body/eval_jaxpr/ppermute | solution.py:14
  31.9 0.0 collective-permute-done.1
  32.0 1.6 %collective-permute-start.2 = (bf16[32,6,1,256]{3,0,2,1:T(8,128)(2,1)S(1)}, bf16[32,6,1,256]{3,0,2,1:T(8,128)(2,1)S(1)}, u32[]{:S(2)}, u32[]{:S(2)}) collective-permute-start(bf16[32,6,1,256]{3,0,2,1:T(8,128)(2,1)S(1)} %get-tuple-element.151), channel_id=1, source_target_pairs={{0,2},{2,0},{1,3},{3,1},{4,6},{6,4},{5,7},{7,5},{8,10},{10,8},{9,1... | collective-permute-start | bytes 294920 | tf_op jit(solution)/shard_map/while/body/eval_jaxpr/ppermute | solution.py:14
  33.5 0.5 collective-permute-start.3
  34.1 2.6 %collective-permute-done.2 = bf16[32,6,1,256]{3,0,2,1:T(8,128)(2,1)S(1)} collective-permute-done((bf16[32,6,1,256]{3,0,2,1:T(8,128)(2,1)S(1)}, bf16[32,6,1,256]{3,0,2,1:T(8,128)(2,1)S(1)}, u32[]{:S(2)}, u32[]{:S(2)}) %collective-permute-start.2) | collective-permute-done | bytes 98336 | tf_op jit(solution)/shard_map/while/body/eval_jaxpr/ppermute | solution.py:14
  36.7 1.5 %collective-permute-done.3 = bf16[32,6,1,256]{3,0,2,1:T(8,128)(2,1)S(1)} collective-permute-done((bf16[32,6,1,256]{3,0,2,1:T(8,128)(2,1)S(1)}, bf16[32,6,1,256]{3,0,2,1:T(8,128)(2,1)S(1)}, u32[]{:S(2)}, u32[]{:S(2)}) %collective-permute-start.3) | collective-permute-done | bytes 98336 | tf_op jit(solution)/shard_map/while/body/eval_jaxpr/ppermute | solution.py:16
  38.2 3.4 %fusion.39 = f32[32,4,2,256]{3,0,2,1:T(8,128)S(1)} fusion(bf16[5,32,4,2,256]{4,1,0,3,2:T(8,128)(2,1)S(1)} %fusion.38, bf16[4,2,5,256,256]{4,3,2,1,0:T(8,128)(2,1)} %get-tuple-element.165, bf16[4,32,4,2,256]{4,1,3,2,0:T(8,128)(2,1)S(1)} %get-tuple-element.166, s32[]{:T(128)S(6)} %copy.43), kind=kOutput, calls=%fused_computation.3.clone.1 | convolution fusion | flops 167903232 | bytes 6291460 | tf_op jit(solution)/shard_map/while/body/eval_jaxpr/kcxyu,xykuv->cxyv/dot_general | solution.py:47
  41.7 0.1 collective-permute-start
  41.7 3.9 %collective-permute-start.1 = (bf16[32,1,2,256]{3,0,2,1:T(8,128)(2,1)S(1)}, bf16[32,1,2,256]{3,0,2,1:T(8,128)(2,1)S(1)}, u32[]{:S(2)}, u32[]{:S(2)}) collective-permute-start(bf16[32,1,2,256]{3,0,2,1:T(8,128)(2,1)S(1)} %get-tuple-element.150), channel_id=1, source_target_pairs={{4,0},{8,4},{12,8},{0,12},{5,1},{9,5},{13,9},{1,13},{6,2},{10,6},{... | collective-permute-start | bytes 98312 | tf_op jit(solution)/shard_map/while/body/eval_jaxpr/ppermute | solution.py:16
  45.6 1.8 %collective-permute-done = bf16[32,1,2,256]{3,0,2,1:T(8,128)(2,1)S(1)} collective-permute-done((bf16[32,1,2,256]{3,0,2,1:T(8,128)(2,1)S(1)}, bf16[32,1,2,256]{3,0,2,1:T(8,128)(2,1)S(1)}, u32[]{:S(2)}, u32[]{:S(2)}) %collective-permute-start) | collective-permute-done | bytes 32800 | tf_op jit(solution)/shard_map/while/body/eval_jaxpr/ppermute | solution.py:14
  47.4 0.0 collective-permute-done.1
  47.5 1.1 %collective-permute-start.2 = (bf16[32,6,1,256]{3,0,2,1:T(8,128)(2,1)S(1)}, bf16[32,6,1,256]{3,0,2,1:T(8,128)(2,1)S(1)}, u32[]{:S(2)}, u32[]{:S(2)}) collective-permute-start(bf16[32,6,1,256]{3,0,2,1:T(8,128)(2,1)S(1)} %get-tuple-element.151), channel_id=1, source_target_pairs={{0,2},{2,0},{1,3},{3,1},{4,6},{6,4},{5,7},{7,5},{8,10},{10,8},{9,1... | collective-permute-start | bytes 294920 | tf_op jit(solution)/shard_map/while/body/eval_jaxpr/ppermute | solution.py:14
  48.6 1.0 %collective-permute-start.3 = (bf16[32,6,1,256]{3,0,2,1:T(8,128)(2,1)S(1)}, bf16[32,6,1,256]{3,0,2,1:T(8,128)(2,1)S(1)}, u32[]{:S(2)}, u32[]{:S(2)}) collective-permute-start(bf16[32,6,1,256]{3,0,2,1:T(8,128)(2,1)S(1)} %get-tuple-element.152), channel_id=1, source_target_pairs={{2,0},{0,2},{3,1},{1,3},{6,4},{4,6},{7,5},{5,7},{10,8},{8,10},{11,... | collective-permute-start | bytes 294920 | tf_op jit(solution)/shard_map/while/body/eval_jaxpr/ppermute | solution.py:16
  49.6 2.6 %collective-permute-done.2 = bf16[32,6,1,256]{3,0,2,1:T(8,128)(2,1)S(1)} collective-permute-done((bf16[32,6,1,256]{3,0,2,1:T(8,128)(2,1)S(1)}, bf16[32,6,1,256]{3,0,2,1:T(8,128)(2,1)S(1)}, u32[]{:S(2)}, u32[]{:S(2)}) %collective-permute-start.2) | collective-permute-done | bytes 98336 | tf_op jit(solution)/shard_map/while/body/eval_jaxpr/ppermute | solution.py:14
  52.2 1.0 %collective-permute-done.3 = bf16[32,6,1,256]{3,0,2,1:T(8,128)(2,1)S(1)} collective-permute-done((bf16[32,6,1,256]{3,0,2,1:T(8,128)(2,1)S(1)}, bf16[32,6,1,256]{3,0,2,1:T(8,128)(2,1)S(1)}, u32[]{:S(2)}, u32[]{:S(2)}) %collective-permute-start.3) | collective-permute-done | bytes 98336 | tf_op jit(solution)/shard_map/while/body/eval_jaxpr/ppermute | solution.py:16
  53.2 3.4 %fusion.39 = f32[32,4,2,256]{3,0,2,1:T(8,128)S(1)} fusion(bf16[5,32,4,2,256]{4,1,0,3,2:T(8,128)(2,1)S(1)} %fusion.38, bf16[4,2,5,256,256]{4,3,2,1,0:T(8,128)(2,1)} %get-tuple-element.165, bf16[4,32,4,2,256]{4,1,3,2,0:T(8,128)(2,1)S(1)} %get-tuple-element.166, s32[]{:T(128)S(6)} %copy.43), kind=kOutput, calls=%fused_computation.3.clone.1 | convolution fusion | flops 167903232 | bytes 6291460 | tf_op jit(solution)/shard_map/while/body/eval_jaxpr/kcxyu,xykuv->cxyv/dot_general | solution.py:47
  56.7 1.2 %collective-permute-start = (bf16[32,1,2,256]{3,0,2,1:T(8,128)(2,1)S(1)}, bf16[32,1,2,256]{3,0,2,1:T(8,128)(2,1)S(1)}, u32[]{:S(2)}, u32[]{:S(2)}) collective-permute-start(bf16[32,1,2,256]{3,0,2,1:T(8,128)(2,1)S(1)} %get-tuple-element.149), channel_id=1, source_target_pairs={{0,4},{4,8},{8,12},{12,0},{1,5},{5,9},{9,13},{13,1},{2,6},{6,10},{... | collective-permute-start | bytes 98312 | tf_op jit(solution)/shard_map/while/body/eval_jaxpr/ppermute | solution.py:14
  57.9 2.8 %collective-permute-start.1 = (bf16[32,1,2,256]{3,0,2,1:T(8,128)(2,1)S(1)}, bf16[32,1,2,256]{3,0,2,1:T(8,128)(2,1)S(1)}, u32[]{:S(2)}, u32[]{:S(2)}) collective-permute-start(bf16[32,1,2,256]{3,0,2,1:T(8,128)(2,1)S(1)} %get-tuple-element.150), channel_id=1, source_target_pairs={{4,0},{8,4},{12,8},{0,12},{5,1},{9,5},{13,9},{1,13},{6,2},{10,6},{... | collective-permute-start | bytes 98312 | tf_op jit(solution)/shard_map/while/body/eval_jaxpr/ppermute | solution.py:16
  60.7 1.8 %collective-permute-done = bf16[32,1,2,256]{3,0,2,1:T(8,128)(2,1)S(1)} collective-permute-done((bf16[32,1,2,256]{3,0,2,1:T(8,128)(2,1)S(1)}, bf16[32,1,2,256]{3,0,2,1:T(8,128)(2,1)S(1)}, u32[]{:S(2)}, u32[]{:S(2)}) %collective-permute-start) | collective-permute-done | bytes 32800 | tf_op jit(solution)/shard_map/while/body/eval_jaxpr/ppermute | solution.py:14
  62.6 0.0 collective-permute-done.1
  62.6 1.1 %collective-permute-start.2 = (bf16[32,6,1,256]{3,0,2,1:T(8,128)(2,1)S(1)}, bf16[32,6,1,256]{3,0,2,1:T(8,128)(2,1)S(1)}, u32[]{:S(2)}, u32[]{:S(2)}) collective-permute-start(bf16[32,6,1,256]{3,0,2,1:T(8,128)(2,1)S(1)} %get-tuple-element.151), channel_id=1, source_target_pairs={{0,2},{2,0},{1,3},{3,1},{4,6},{6,4},{5,7},{7,5},{8,10},{10,8},{9,1... | collective-permute-start | bytes 294920 | tf_op jit(solution)/shard_map/while/body/eval_jaxpr/ppermute | solution.py:14
  63.7 1.0 %collective-permute-start.3 = (bf16[32,6,1,256]{3,0,2,1:T(8,128)(2,1)S(1)}, bf16[32,6,1,256]{3,0,2,1:T(8,128)(2,1)S(1)}, u32[]{:S(2)}, u32[]{:S(2)}) collective-permute-start(bf16[32,6,1,256]{3,0,2,1:T(8,128)(2,1)S(1)} %get-tuple-element.152), channel_id=1, source_target_pairs={{2,0},{0,2},{3,1},{1,3},{6,4},{4,6},{7,5},{5,7},{10,8},{8,10},{11,... | collective-permute-start | bytes 294920 | tf_op jit(solution)/shard_map/while/body/eval_jaxpr/ppermute | solution.py:16
  64.7 2.6 %collective-permute-done.2 = bf16[32,6,1,256]{3,0,2,1:T(8,128)(2,1)S(1)} collective-permute-done((bf16[32,6,1,256]{3,0,2,1:T(8,128)(2,1)S(1)}, bf16[32,6,1,256]{3,0,2,1:T(8,128)(2,1)S(1)}, u32[]{:S(2)}, u32[]{:S(2)}) %collective-permute-start.2) | collective-permute-done | bytes 98336 | tf_op jit(solution)/shard_map/while/body/eval_jaxpr/ppermute | solution.py:14
  67.3 1.0 %collective-permute-done.3 = bf16[32,6,1,256]{3,0,2,1:T(8,128)(2,1)S(1)} collective-permute-done((bf16[32,6,1,256]{3,0,2,1:T(8,128)(2,1)S(1)}, bf16[32,6,1,256]{3,0,2,1:T(8,128)(2,1)S(1)}, u32[]{:S(2)}, u32[]{:S(2)}) %collective-permute-start.3) | collective-permute-done | bytes 98336 | tf_op jit(solution)/shard_map/while/body/eval_jaxpr/ppermute | solution.py:16
  68.4 3.4 %fusion.39 = f32[32,4,2,256]{3,0,2,1:T(8,128)S(1)} fusion(bf16[5,32,4,2,256]{4,1,0,3,2:T(8,128)(2,1)S(1)} %fusion.38, bf16[4,2,5,256,256]{4,3,2,1,0:T(8,128)(2,1)} %get-tuple-element.165, bf16[4,32,4,2,256]{4,1,3,2,0:T(8,128)(2,1)S(1)} %get-tuple-element.166, s32[]{:T(128)S(6)} %copy.43), kind=kOutput, calls=%fused_computation.3.clone.1 | convolution fusion | flops 167903232 | bytes 6291460 | tf_op jit(solution)/shard_map/while/body/eval_jaxpr/kcxyu,xykuv->cxyv/dot_general | solution.py:47
  71.9 1.3 %collective-permute-start = (bf16[32,1,2,256]{3,0,2,1:T(8,128)(2,1)S(1)}, bf16[32,1,2,256]{3,0,2,1:T(8,128)(2,1)S(1)}, u32[]{:S(2)}, u32[]{:S(2)}) collective-permute-start(bf16[32,1,2,256]{3,0,2,1:T(8,128)(2,1)S(1)} %get-tuple-element.149), channel_id=1, source_target_pairs={{0,4},{4,8},{8,12},{12,0},{1,5},{5,9},{9,13},{13,1},{2,6},{6,10},{... | collective-permute-start | bytes 98312 | tf_op jit(solution)/shard_map/while/body/eval_jaxpr/ppermute | solution.py:14
  73.2 2.7 %collective-permute-start.1 = (bf16[32,1,2,256]{3,0,2,1:T(8,128)(2,1)S(1)}, bf16[32,1,2,256]{3,0,2,1:T(8,128)(2,1)S(1)}, u32[]{:S(2)}, u32[]{:S(2)}) collective-permute-start(bf16[32,1,2,256]{3,0,2,1:T(8,128)(2,1)S(1)} %get-tuple-element.150), channel_id=1, source_target_pairs={{4,0},{8,4},{12,8},{0,12},{5,1},{9,5},{13,9},{1,13},{6,2},{10,6},{... | collective-permute-start | bytes 98312 | tf_op jit(solution)/shard_map/while/body/eval_jaxpr/ppermute | solution.py:16
  75.9 1.8 %collective-permute-done = bf16[32,1,2,256]{3,0,2,1:T(8,128)(2,1)S(1)} collective-permute-done((bf16[32,1,2,256]{3,0,2,1:T(8,128)(2,1)S(1)}, bf16[32,1,2,256]{3,0,2,1:T(8,128)(2,1)S(1)}, u32[]{:S(2)}, u32[]{:S(2)}) %collective-permute-start) | collective-permute-done | bytes 32800 | tf_op jit(solution)/shard_map/while/body/eval_jaxpr/ppermute | solution.py:14
  77.7 0.0 collective-permute-done.1
  77.8 1.1 %collective-permute-start.2 = (bf16[32,6,1,256]{3,0,2,1:T(8,128)(2,1)S(1)}, bf16[32,6,1,256]{3,0,2,1:T(8,128)(2,1)S(1)}, u32[]{:S(2)}, u32[]{:S(2)}) collective-permute-start(bf16[32,6,1,256]{3,0,2,1:T(8,128)(2,1)S(1)} %get-tuple-element.151), channel_id=1, source_target_pairs={{0,2},{2,0},{1,3},{3,1},{4,6},{6,4},{5,7},{7,5},{8,10},{10,8},{9,1... | collective-permute-start | bytes 294920 | tf_op jit(solution)/shard_map/while/body/eval_jaxpr/ppermute | solution.py:14
  78.9 1.0 %collective-permute-start.3 = (bf16[32,6,1,256]{3,0,2,1:T(8,128)(2,1)S(1)}, bf16[32,6,1,256]{3,0,2,1:T(8,128)(2,1)S(1)}, u32[]{:S(2)}, u32[]{:S(2)}) collective-permute-start(bf16[32,6,1,256]{3,0,2,1:T(8,128)(2,1)S(1)} %get-tuple-element.152), channel_id=1, source_target_pairs={{2,0},{0,2},{3,1},{1,3},{6,4},{4,6},{7,5},{5,7},{10,8},{8,10},{11,... | collective-permute-start | bytes 294920 | tf_op jit(solution)/shard_map/while/body/eval_jaxpr/ppermute | solution.py:16
  79.9 2.6 %collective-permute-done.2 = bf16[32,6,1,256]{3,0,2,1:T(8,128)(2,1)S(1)} collective-permute-done((bf16[32,6,1,256]{3,0,2,1:T(8,128)(2,1)S(1)}, bf16[32,6,1,256]{3,0,2,1:T(8,128)(2,1)S(1)}, u32[]{:S(2)}, u32[]{:S(2)}) %collective-permute-start.2) | collective-permute-done | bytes 98336 | tf_op jit(solution)/shard_map/while/body/eval_jaxpr/ppermute | solution.py:14
  82.5 1.0 %collective-permute-done.3 = bf16[32,6,1,256]{3,0,2,1:T(8,128)(2,1)S(1)} collective-permute-done((bf16[32,6,1,256]{3,0,2,1:T(8,128)(2,1)S(1)}, bf16[32,6,1,256]{3,0,2,1:T(8,128)(2,1)S(1)}, u32[]{:S(2)}, u32[]{:S(2)}) %collective-permute-start.3) | collective-permute-done | bytes 98336 | tf_op jit(solution)/shard_map/while/body/eval_jaxpr/ppermute | solution.py:16
  83.5 3.4 %fusion.39 = f32[32,4,2,256]{3,0,2,1:T(8,128)S(1)} fusion(bf16[5,32,4,2,256]{4,1,0,3,2:T(8,128)(2,1)S(1)} %fusion.38, bf16[4,2,5,256,256]{4,3,2,1,0:T(8,128)(2,1)} %get-tuple-element.165, bf16[4,32,4,2,256]{4,1,3,2,0:T(8,128)(2,1)S(1)} %get-tuple-element.166, s32[]{:T(128)S(6)} %copy.43), kind=kOutput, calls=%fused_computation.3.clone.1 | convolution fusion | flops 167903232 | bytes 6291460 | tf_op jit(solution)/shard_map/while/body/eval_jaxpr/kcxyu,xykuv->cxyv/dot_general | solution.py:47
  87.0 0.9 %copy.33 = f32[32,4,2,256]{3,2,1,0:T(2,128)} copy(f32[32,4,2,256]{3,0,2,1:T(8,128)S(1)} %get-tuple-element.99) | data formatting | bytes 524288
  87.9 0.1 copy.31
  88.0 0.1 concatenate.39
  88.1 0.1 copy.32
  88.3 0.1 concatenate.40
  88.3 0.0 copy-done.3
  88.3 0.3 convolution_convert_fusion.1
  88.6 0.8 reshape.22
  (35 shorter events, 0.5 us)
Async XLA Ops:
  0.6 11.1 %copy-start = (bf16[8,256,256]{2,1,0:T(8,128)(2,1)S(1)}, bf16[8,256,256]{2,1,0:T(8,128)(2,1)}, u32[]{:S(2)}) copy-start(bf16[8,256,256]{2,1,0:T(8,128)(2,1)} %param.11) | copy-start | bytes 3145732
  0.6 10.8 %copy-start.2 = (s32[4,2,5]{2,1,0:T(2,128)S(1)}, s32[4,2,5]{2,1,0:T(2,128)}, u32[]{:S(2)}) copy-start(s32[4,2,5]{2,1,0:T(2,128)} %param.10) | copy-start | bytes 484
  0.7 10.9 %copy-start.1 = (f32[32,4,2,256]{3,2,1,0:T(2,128)S(1)}, f32[32,4,2,256]{3,2,1,0:T(2,128)}, u32[]{:S(2)}) copy-start(f32[32,4,2,256]{3,2,1,0:T(2,128)} %param.9) | copy-start | bytes 786436
  5.2 20.8 %all-to-all-start = ((bf16[1,32,16,2,256]{4,3,1,0,2:T(2,128)(2,1)}), bf16[1,32,16,2,256]{4,3,1,0,2:T(2,128)(2,1)S(1)}, u32[]{:S(2)}, u32[]{:S(2)}) async-start(bf16[1,32,16,2,256]{4,3,1,0,2:T(2,128)(2,1)} %copy.28), calls=%async_computation | async-start | bytes 1048576 | tf_op jit(solution)/shard_map/all_to_all | solution.py:31
  26.1 62.2 %copy-start.3 = (bf16[512,512]{1,0:T(8,128)(2,1)S(1)}, bf16[512,512]{1,0:T(8,128)(2,1)}, u32[]{:S(2)}) copy-start(bf16[512,512]{1,0:T(8,128)(2,1)} %param.13) | copy-start | bytes 1572868
  26.1 5.8 %collective-permute-start = (bf16[32,1,2,256]{3,0,2,1:T(8,128)(2,1)S(1)}, bf16[32,1,2,256]{3,0,2,1:T(8,128)(2,1)S(1)}, u32[]{:S(2)}, u32[]{:S(2)}) collective-permute-start(bf16[32,1,2,256]{3,0,2,1:T(8,128)(2,1)S(1)} %get-tuple-element.149), channel_id=1, source_target_pairs={{0,4},{4,8},{8,12},{12,0},{1,5},{5,9},{9,13},{13,1},{2,6},{6,10},{... | collective-permute-start | bytes 98312 | tf_op jit(solution)/shard_map/while/body/eval_jaxpr/ppermute | solution.py:14
  26.2 5.7 %collective-permute-start.1 = (bf16[32,1,2,256]{3,0,2,1:T(8,128)(2,1)S(1)}, bf16[32,1,2,256]{3,0,2,1:T(8,128)(2,1)S(1)}, u32[]{:S(2)}, u32[]{:S(2)}) collective-permute-start(bf16[32,1,2,256]{3,0,2,1:T(8,128)(2,1)S(1)} %get-tuple-element.150), channel_id=1, source_target_pairs={{4,0},{8,4},{12,8},{0,12},{5,1},{9,5},{13,9},{1,13},{6,2},{10,6},{... | collective-permute-start | bytes 98312 | tf_op jit(solution)/shard_map/while/body/eval_jaxpr/ppermute | solution.py:16
  32.0 4.7 %collective-permute-start.2 = (bf16[32,6,1,256]{3,0,2,1:T(8,128)(2,1)S(1)}, bf16[32,6,1,256]{3,0,2,1:T(8,128)(2,1)S(1)}, u32[]{:S(2)}, u32[]{:S(2)}) collective-permute-start(bf16[32,6,1,256]{3,0,2,1:T(8,128)(2,1)S(1)} %get-tuple-element.151), channel_id=1, source_target_pairs={{0,2},{2,0},{1,3},{3,1},{4,6},{6,4},{5,7},{7,5},{8,10},{10,8},{9,1... | collective-permute-start | bytes 294920 | tf_op jit(solution)/shard_map/while/body/eval_jaxpr/ppermute | solution.py:14
  33.5 4.6 %collective-permute-start.3 = (bf16[32,6,1,256]{3,0,2,1:T(8,128)(2,1)S(1)}, bf16[32,6,1,256]{3,0,2,1:T(8,128)(2,1)S(1)}, u32[]{:S(2)}, u32[]{:S(2)}) collective-permute-start(bf16[32,6,1,256]{3,0,2,1:T(8,128)(2,1)S(1)} %get-tuple-element.152), channel_id=1, source_target_pairs={{2,0},{0,2},{3,1},{1,3},{6,4},{4,6},{7,5},{5,7},{10,8},{8,10},{11,... | collective-permute-start | bytes 294920 | tf_op jit(solution)/shard_map/while/body/eval_jaxpr/ppermute | solution.py:16
  41.7 5.8 %collective-permute-start = (bf16[32,1,2,256]{3,0,2,1:T(8,128)(2,1)S(1)}, bf16[32,1,2,256]{3,0,2,1:T(8,128)(2,1)S(1)}, u32[]{:S(2)}, u32[]{:S(2)}) collective-permute-start(bf16[32,1,2,256]{3,0,2,1:T(8,128)(2,1)S(1)} %get-tuple-element.149), channel_id=1, source_target_pairs={{0,4},{4,8},{8,12},{12,0},{1,5},{5,9},{9,13},{13,1},{2,6},{6,10},{... | collective-permute-start | bytes 98312 | tf_op jit(solution)/shard_map/while/body/eval_jaxpr/ppermute | solution.py:14
  41.7 5.7 %collective-permute-start.1 = (bf16[32,1,2,256]{3,0,2,1:T(8,128)(2,1)S(1)}, bf16[32,1,2,256]{3,0,2,1:T(8,128)(2,1)S(1)}, u32[]{:S(2)}, u32[]{:S(2)}) collective-permute-start(bf16[32,1,2,256]{3,0,2,1:T(8,128)(2,1)S(1)} %get-tuple-element.150), channel_id=1, source_target_pairs={{4,0},{8,4},{12,8},{0,12},{5,1},{9,5},{13,9},{1,13},{6,2},{10,6},{... | collective-permute-start | bytes 98312 | tf_op jit(solution)/shard_map/while/body/eval_jaxpr/ppermute | solution.py:16
  47.5 4.7 %collective-permute-start.2 = (bf16[32,6,1,256]{3,0,2,1:T(8,128)(2,1)S(1)}, bf16[32,6,1,256]{3,0,2,1:T(8,128)(2,1)S(1)}, u32[]{:S(2)}, u32[]{:S(2)}) collective-permute-start(bf16[32,6,1,256]{3,0,2,1:T(8,128)(2,1)S(1)} %get-tuple-element.151), channel_id=1, source_target_pairs={{0,2},{2,0},{1,3},{3,1},{4,6},{6,4},{5,7},{7,5},{8,10},{10,8},{9,1... | collective-permute-start | bytes 294920 | tf_op jit(solution)/shard_map/while/body/eval_jaxpr/ppermute | solution.py:14
  48.6 4.6 %collective-permute-start.3 = (bf16[32,6,1,256]{3,0,2,1:T(8,128)(2,1)S(1)}, bf16[32,6,1,256]{3,0,2,1:T(8,128)(2,1)S(1)}, u32[]{:S(2)}, u32[]{:S(2)}) collective-permute-start(bf16[32,6,1,256]{3,0,2,1:T(8,128)(2,1)S(1)} %get-tuple-element.152), channel_id=1, source_target_pairs={{2,0},{0,2},{3,1},{1,3},{6,4},{4,6},{7,5},{5,7},{10,8},{8,10},{11,... | collective-permute-start | bytes 294920 | tf_op jit(solution)/shard_map/while/body/eval_jaxpr/ppermute | solution.py:16
  56.7 5.8 %collective-permute-start = (bf16[32,1,2,256]{3,0,2,1:T(8,128)(2,1)S(1)}, bf16[32,1,2,256]{3,0,2,1:T(8,128)(2,1)S(1)}, u32[]{:S(2)}, u32[]{:S(2)}) collective-permute-start(bf16[32,1,2,256]{3,0,2,1:T(8,128)(2,1)S(1)} %get-tuple-element.149), channel_id=1, source_target_pairs={{0,4},{4,8},{8,12},{12,0},{1,5},{5,9},{9,13},{13,1},{2,6},{6,10},{... | collective-permute-start | bytes 98312 | tf_op jit(solution)/shard_map/while/body/eval_jaxpr/ppermute | solution.py:14
  57.9 4.7 %collective-permute-start.1 = (bf16[32,1,2,256]{3,0,2,1:T(8,128)(2,1)S(1)}, bf16[32,1,2,256]{3,0,2,1:T(8,128)(2,1)S(1)}, u32[]{:S(2)}, u32[]{:S(2)}) collective-permute-start(bf16[32,1,2,256]{3,0,2,1:T(8,128)(2,1)S(1)} %get-tuple-element.150), channel_id=1, source_target_pairs={{4,0},{8,4},{12,8},{0,12},{5,1},{9,5},{13,9},{1,13},{6,2},{10,6},{... | collective-permute-start | bytes 98312 | tf_op jit(solution)/shard_map/while/body/eval_jaxpr/ppermute | solution.py:16
  62.6 4.7 %collective-permute-start.2 = (bf16[32,6,1,256]{3,0,2,1:T(8,128)(2,1)S(1)}, bf16[32,6,1,256]{3,0,2,1:T(8,128)(2,1)S(1)}, u32[]{:S(2)}, u32[]{:S(2)}) collective-permute-start(bf16[32,6,1,256]{3,0,2,1:T(8,128)(2,1)S(1)} %get-tuple-element.151), channel_id=1, source_target_pairs={{0,2},{2,0},{1,3},{3,1},{4,6},{6,4},{5,7},{7,5},{8,10},{10,8},{9,1... | collective-permute-start | bytes 294920 | tf_op jit(solution)/shard_map/while/body/eval_jaxpr/ppermute | solution.py:14
  63.7 4.6 %collective-permute-start.3 = (bf16[32,6,1,256]{3,0,2,1:T(8,128)(2,1)S(1)}, bf16[32,6,1,256]{3,0,2,1:T(8,128)(2,1)S(1)}, u32[]{:S(2)}, u32[]{:S(2)}) collective-permute-start(bf16[32,6,1,256]{3,0,2,1:T(8,128)(2,1)S(1)} %get-tuple-element.152), channel_id=1, source_target_pairs={{2,0},{0,2},{3,1},{1,3},{6,4},{4,6},{7,5},{5,7},{10,8},{8,10},{11,... | collective-permute-start | bytes 294920 | tf_op jit(solution)/shard_map/while/body/eval_jaxpr/ppermute | solution.py:16
  71.9 5.8 %collective-permute-start = (bf16[32,1,2,256]{3,0,2,1:T(8,128)(2,1)S(1)}, bf16[32,1,2,256]{3,0,2,1:T(8,128)(2,1)S(1)}, u32[]{:S(2)}, u32[]{:S(2)}) collective-permute-start(bf16[32,1,2,256]{3,0,2,1:T(8,128)(2,1)S(1)} %get-tuple-element.149), channel_id=1, source_target_pairs={{0,4},{4,8},{8,12},{12,0},{1,5},{5,9},{9,13},{13,1},{2,6},{6,10},{... | collective-permute-start | bytes 98312 | tf_op jit(solution)/shard_map/while/body/eval_jaxpr/ppermute | solution.py:14
  73.2 4.5 %collective-permute-start.1 = (bf16[32,1,2,256]{3,0,2,1:T(8,128)(2,1)S(1)}, bf16[32,1,2,256]{3,0,2,1:T(8,128)(2,1)S(1)}, u32[]{:S(2)}, u32[]{:S(2)}) collective-permute-start(bf16[32,1,2,256]{3,0,2,1:T(8,128)(2,1)S(1)} %get-tuple-element.150), channel_id=1, source_target_pairs={{4,0},{8,4},{12,8},{0,12},{5,1},{9,5},{13,9},{1,13},{6,2},{10,6},{... | collective-permute-start | bytes 98312 | tf_op jit(solution)/shard_map/while/body/eval_jaxpr/ppermute | solution.py:16
  77.8 4.7 %collective-permute-start.2 = (bf16[32,6,1,256]{3,0,2,1:T(8,128)(2,1)S(1)}, bf16[32,6,1,256]{3,0,2,1:T(8,128)(2,1)S(1)}, u32[]{:S(2)}, u32[]{:S(2)}) collective-permute-start(bf16[32,6,1,256]{3,0,2,1:T(8,128)(2,1)S(1)} %get-tuple-element.151), channel_id=1, source_target_pairs={{0,2},{2,0},{1,3},{3,1},{4,6},{6,4},{5,7},{7,5},{8,10},{10,8},{9,1... | collective-permute-start | bytes 294920 | tf_op jit(solution)/shard_map/while/body/eval_jaxpr/ppermute | solution.py:14
  78.9 4.6 %collective-permute-start.3 = (bf16[32,6,1,256]{3,0,2,1:T(8,128)(2,1)S(1)}, bf16[32,6,1,256]{3,0,2,1:T(8,128)(2,1)S(1)}, u32[]{:S(2)}, u32[]{:S(2)}) collective-permute-start(bf16[32,6,1,256]{3,0,2,1:T(8,128)(2,1)S(1)} %get-tuple-element.152), channel_id=1, source_target_pairs={{2,0},{0,2},{3,1},{1,3},{6,4},{4,6},{7,5},{5,7},{10,8},{8,10},{11,... | collective-permute-start | bytes 294920 | tf_op jit(solution)/shard_map/while/body/eval_jaxpr/ppermute | solution.py:16
where the time goes:
time: 89.8 us; the launch traced here: 89.4 us
  waiting for transfers between devices  31.9 us (36%)
  starting transfers between devices  30.5 us (34%)
  matrix products  15.4 us (17%)
  local copies, waits for them, and re-layouts  10.1 us (11%)
    ppermute x8, waiting for transfers between devices, with_halo(): lax.ppermute(tail, axis, [(i, (i + 1) % count) for i in range(count)])  17.6 us
    ppermute x8, starting transfers between devices, with_halo(): lax.ppermute(head, axis, [((i + 1) % count, i) for i in range(count)])  16.6 us
    dot_general x4, matrix products, advance(): jnp.einsum('kcxyu,xykuv->cxyv', adjacent_blocks, chosen_tiles, preferred_...  13.7 us
    all_to_all x1, waiting for transfers between devices, shards(): lax.all_to_all(projected, 'gx', split_axis=2, concat_axis=0, tiled=True)  9.71 us
    ppermute x8, starting transfers between devices, with_halo(): lax.ppermute(tail, axis, [(i, (i + 1) % count) for i in range(count)])  7.52 us
    all_to_all x1, starting transfers between devices, shards(): lax.all_to_all(projected, 'gx', split_axis=2, concat_axis=0, tiled=True)  6.31 us
    ppermute x8, waiting for transfers between devices, with_halo(): lax.ppermute(head, axis, [((i + 1) % count, i) for i in range(count)])  4.6 us
    gather x1, local copies, waits for them, and re-layouts, shards(): chosen_tiles = tile_bank[tile_index]  4.57 us
  transfers between devices with their start and end apart: 17, of which 13 were waited for; matrix products, arithmetic and copies ran while one was open for 5% of the time, Pallas kernels for 0%

commit v1 on v0

--- a/solution.py
+++ b/solution.py
@@ -1,7 +1,178 @@
 import jax
 import jax.numpy as jnp
 from jax import lax
+from jax.experimental import pallas as pl
+from jax.experimental.pallas import tpu as pltpu
 from jax.sharding import PartitionSpec as P
+
+PLANE = ("gx", "gy")
+VMEM_LIMIT = 40 * 1024 * 1024
+
+
+def whole(shape):
+    return pl.BlockSpec(shape, lambda *_: (0,) * len(shape))
+
+
+def inlet_kernel(frames_ref, start_ref, inlet_ref, packed_ref):
+    peers, rows, units = packed_ref.shape
+    cells = frames_ref[...].reshape(-1, frames_ref.shape[-1])
+    drive = jnp.dot(cells, inlet_ref[...], preferred_element_type=jnp.float32)
+    drive_rows = drive.shape[0] // peers
+    packed_ref[:, :drive_rows, :] = drive.astype(jnp.bfloat16).reshape(peers, drive_rows, units)
+    state = start_ref[...].reshape(peers, rows - drive_rows, units)
+    packed_ref[:, drive_rows:, :] = state.astype(jnp.bfloat16)
+
+
+def pack_for_peers(frames, start_state, inlet_coupler, peers):
+    units = inlet_coupler.shape[1]
+    drive_rows = frames.size // frames.shape[-1] // peers
+    state_rows = start_state.size // units // peers
+    return pl.pallas_call(
+        inlet_kernel,
+        out_shape=jax.ShapeDtypeStruct((peers, drive_rows + state_rows, units), jnp.bfloat16),
+        compiler_params=pltpu.CompilerParams(vmem_limit_bytes=VMEM_LIMIT),
+    )(frames, start_state, inlet_coupler)
+
+
+def steps_kernel(count_x, count_y, packed_ref, own_ref, from_ref, bank_ref, sent_ref):
+    peers, rows, units = packed_ref.shape
+    torus_rows = own_ref.shape[1]
+    home_rows = torus_rows // count_x
+    trajectories = sent_ref.shape[1] // home_rows
+    drive_rows = trajectories * torus_rows
+    halves = bank_ref.shape[0] // 2
+    groups = [(j, t) for j in range(count_y) for t in range(trajectories)]
+
+    def home_slice(t, base=0):
+        return slice(base + t * home_rows, base + (t + 1) * home_rows)
+
+    def choose(index, products):
+        chosen = products[-1]
+        for tile in range(halves - 2, -1, -1):
+            chosen = jnp.where(index == tile, products[tile], chosen)
+        return chosen
+
+    column = lax.broadcasted_iota(jnp.int32, (torus_rows, units), 0) % 2
+    low = column == 0
+    state = []
+    for j, t in groups:
+        for i in range(count_x):
+            piece = packed_ref[i * count_y + j, drive_rows : rows, :].astype(jnp.float32)
+            state.append(piece[home_slice(t)])
+    state = jnp.concatenate(state, axis=0)
+    for step in range(count_x):
+        state_half = state.astype(jnp.bfloat16)
+        own = [
+            jnp.dot(state_half, bank_ref[tile], preferred_element_type=jnp.float32)
+            for tile in range(halves)
+        ]
+        other = [
+            jnp.dot(state_half, bank_ref[halves + tile], preferred_element_type=jnp.float32)
+            for tile in range(halves)
+        ]
+        kept, after_x, left, right = {}, {}, {}, {}
+        for g, (j, t) in enumerate(groups):
+            span = slice(g * torus_rows, (g + 1) * torus_rows)
+            others = [product[span] for product in other]
+            total = choose(own_ref[j], [product[span] for product in own])
+            total += pltpu.roll(choose(from_ref[0, j], others), 2, axis=0)
+            total += pltpu.roll(choose(from_ref[1, j], others), torus_rows - 2, axis=0)
+            kept[j, t] = total
+            left[j, t] = choose(from_ref[2, j], others)
+            right[j, t] = choose(from_ref[3, j], others)
+        fresh = []
+        for j, t in groups:
+            before, behind = (j - 1) % count_y, (j + 1) % count_y
+            total = kept[j, t]
+            total += jnp.where(
+                low,
+                pltpu.roll(left[before, t], torus_rows - 1, axis=0),
+                pltpu.roll(left[j, t], 1, axis=0),
+            )
+            total += jnp.where(
+                low,
+                pltpu.roll(right[j, t], torus_rows - 1, axis=0),
+                pltpu.roll(right[behind, t], 1, axis=0),
+            )
+            drive = packed_ref[
+                step * count_y + j, t * torus_rows : (t + 1) * torus_rows, :
+            ].astype(jnp.float32)
+            fresh.append(jnp.tanh(total + drive))
+        state = jnp.concatenate(fresh, axis=0)
+    for i in range(count_x):
+        for j in range(count_y):
+            pieces = []
+            for t in range(trajectories):
+                base = (j * trajectories + t) * torus_rows + i * home_rows
+                pieces.append(state[base : base + home_rows])
+            sent_ref[i * count_y + j] = jnp.concatenate(pieces, axis=0).astype(jnp.bfloat16)
+
+
+def run_steps(packed, own_index, from_index, tile_bank, count_x, count_y, home_rows):
+    peers, _, units = packed.shape
+
+    def kernel(*refs):
+        steps_kernel(count_x, count_y, *refs)
+
+    return pl.pallas_call(
+        kernel,
+        out_shape=jax.ShapeDtypeStruct((peers, home_rows, units), jnp.bfloat16),
+        compiler_params=pltpu.CompilerParams(vmem_limit_bytes=VMEM_LIMIT),
+    )(packed, own_index, from_index, tile_bank)
+
+
+def readout_kernel(state_ref, readout_ref, field_ref, final_ref):
+    units = state_ref.shape[-1]
+    half = state_ref[...].reshape(-1, units)
+    final = half.astype(jnp.float32)
+    squares = (final * final).astype(jnp.bfloat16)
+    field = jnp.dot(half, readout_ref[:units], preferred_element_type=jnp.float32)
+    field += jnp.dot(squares, readout_ref[units:], preferred_element_type=jnp.float32)
+    final_ref[...] = final.reshape(final_ref.shape)
+    field_ref[...] = field.astype(jnp.bfloat16).reshape(field_ref.shape)
+
+
+def read_out(state, readout_operator, block_shape):
+    return pl.pallas_call(
+        readout_kernel,
+        out_shape=(
+            jax.ShapeDtypeStruct(block_shape + readout_operator.shape[1:], jnp.bfloat16),
+            jax.ShapeDtypeStruct(block_shape + state.shape[-1:], jnp.float32),
+        ),
+        compiler_params=pltpu.CompilerParams(vmem_limit_bytes=VMEM_LIMIT),
+    )(state, readout_operator)
+
+
+def tile_choices(tile_index, first_other, units):
+    everywhere = lax.all_gather(tile_index, "gx", axis=0, tiled=True)
+    everywhere = lax.all_gather(everywhere, "gy", axis=1, tiled=True)
+
+    def by_row(index):
+        pairs = index.reshape(index.shape[0], -1, 2).transpose(1, 0, 2)
+        pairs = pairs.reshape(pairs.shape[0], -1, 1)
+        return jnp.broadcast_to(pairs, pairs.shape[:2] + (units,))
+
+    leaving = [
+        jnp.roll(everywhere[..., 1], -1, 0),
+        jnp.roll(everywhere[..., 2], 1, 0),
+        jnp.roll(everywhere[..., 3], -1, 1),
+        jnp.roll(everywhere[..., 4], 1, 1),
+    ]
+    return by_row(everywhere[..., 0]), jnp.stack([by_row(v) for v in leaving]) - first_other
+
+
+def by_trajectory(frames, start_state, tile_index, tile_bank, inlet_coupler, readout_operator):
+    count_x, count_y = lax.axis_size("gx"), lax.axis_size("gy")
+    peers = count_x * count_y
+    units = inlet_coupler.shape[1]
+    block_shape = start_state.shape[:-1]
+    packed = pack_for_peers(frames, start_state, inlet_coupler, peers)
+    own_index, from_index = tile_choices(tile_index, tile_bank.shape[0] // 2, units)
+    packed = lax.all_to_all(packed, PLANE, 0, 0, tiled=True)
+    home_rows = start_state.size // units // peers
+    sent = run_steps(packed, own_index, from_index, tile_bank, count_x, count_y, home_rows)
+    state = lax.all_to_all(sent, PLANE, 0, 0, tiled=True)
+    return read_out(state, readout_operator, block_shape)
 
 
 def with_halo(cells, sides, width):
@@ -20,7 +191,7 @@
     return cells
 
 
-def shards(frames, start_state, tile_index, tile_bank, inlet_coupler, readout_operator):
+def by_block(frames, start_state, tile_index, tile_bank, inlet_coupler, readout_operator):
     patch_site_total = inlet_coupler.shape[0]
     hidden_node_total = inlet_coupler.shape[1]
     prediction_span = frames.shape[:-1]
@@ -75,6 +246,13 @@
         P(),
         P(),
     )
+    def shards(frames, start_state, *rest):
+        peers = mesh.shape["gx"] * mesh.shape["gy"]
+        fits = start_state.shape[0] % peers == 0 and start_state.shape[2] == 2
+        fits = fits and start_state.shape[1] % 4 == 0
+        body = by_trajectory if fits and frames.shape[0] == 1 else by_block
+        return body(frames, start_state, *rest)
+
     return jax.shard_map(
         shards,
         mesh=mesh,

time: 89.8 us -> 57.5 us (0.64)
  blocking collectives: 0 us -> 38.7 us
  waiting for transfers between devices: 31.9 us -> 0.01 us
  starting transfers between devices: 30.5 us -> 7.38 us
  matrix products: 15.4 us -> 0 us
  local copies, waits for them, and re-layouts: 10.1 us -> 4.66 us
  Pallas kernels: 0 us -> 5.42 us
    all_gather x0 -> x2, blocking collectives: none -> 26.8 us  [the longest x1 22.4 us: tile_choices(): everywhere = lax.all_gather(tile_index, 'gx', axis=0, tiled=True)]
    ppermute x16 -> x0, starting transfers between devices: 24.2 us -> none  [the longest x8 16.6 us: with_halo(): lax.ppermute(head, axis, [((i + 1) % count, i) for i in range(count)])]
    ppermute x16 -> x0, waiting for transfers between devices: 22.2 us -> none  [the longest x8 17.6 us: with_halo(): lax.ppermute(tail, axis, [(i, (i + 1) % count) for i in range(count)])]
    dot_general x6 -> x0, matrix products: 15.4 us -> none  [the longest x4 13.7 us: advance(): jnp.einsum('kcxyu,xykuv->cxyv', adjacent_blocks, chosen_tiles, preferred_...]
    all_to_all x0 -> x1, blocking collectives: none -> 12 us  [by_trajectory(): state = lax.all_to_all(sent, PLANE, 0, 0, tiled=True)]
    all_to_all x1, waiting for transfers between devices: 9.71 us -> 0.01 us  [by_trajectory(): packed = lax.all_to_all(packed, PLANE, 0, 0, tiled=True)]
    pallas_call x0 -> x3, Pallas kernels: none -> 5.42 us  [the longest x1 3.12 us: run_steps(): pl.pallas_call(kernel, out_shape=jax.ShapeDtypeStruct((peers, home_rows,...]
    gather x1 -> x0, local copies, waits for them, and re-layouts: 4.57 us -> none  [shards(): chosen_tiles = tile_bank[tile_index]]
  transfers between devices with their start and end apart: 17 -> 1, of which waited for: 13 -> 0; matrix products, arithmetic and copies ran while one was open for 5% -> 3% of each run, Pallas kernels for 0% -> 0%
where the time goes in v1:
time: 57.5 us; the launch traced here: 57.1 us
  blocking collectives  38.7 us (67%)
  starting transfers between devices  7.38 us (13%)
  Pallas kernels  5.42 us (9%)
  local copies, waits for them, and re-layouts  4.66 us (8%)
  between operations  0.72 us (1%)
    all_gather x1, blocking collectives, tile_choices(): everywhere = lax.all_gather(tile_index, 'gx', axis=0, tiled=True)  22.4 us
    all_to_all x1, blocking collectives, by_trajectory(): state = lax.all_to_all(sent, PLANE, 0, 0, tiled=True)  12 us
    all_to_all x1, starting transfers between devices, by_trajectory(): packed = lax.all_to_all(packed, PLANE, 0, 0, tiled=True)  7.38 us
    all_gather x1, blocking collectives, tile_choices(): everywhere = lax.all_gather(everywhere, 'gy', axis=1, tiled=True)  4.35 us
    unnamed x12, local copies, waits for them, and re-layouts  3.13 us
    pallas_call x1, Pallas kernels, run_steps(): pl.pallas_call(kernel, out_shape=jax.ShapeDtypeStruct((peers, home_rows,...  3.12 us
    pallas_call x1, Pallas kernels, pack_for_peers(): pl.pallas_call(inlet_kernel, out_shape=jax.ShapeDtypeStruct((peers, drive...  1.29 us
  transfers between devices with their start and end apart: 1, of which 0 were waited for; matrix products, arithmetic and copies ran while one was open for 3% of the time, Pallas kernels for 0%

profile of v1, /device:TPU:0, one launch (start us, length us, event | category | flops | bytes accessed | tf_op | source)
XLA Modules:
  0.0 57.1 jit_solution(17607450365652887753)
XLA Ops:
  0.6 0.0 copy-start
  0.6 1.2 %copy-done = bf16[1,32,16,2,512]{4,3,2,1,0:T(2,128)(2,1)S(1)} copy-done((bf16[1,32,16,2,512]{4,3,2,1,0:T(2,128)(2,1)S(1)}, bf16[1,32,16,2,512]{4,3,2,1,0:T(2,128)(2,1)}, u32[]{:S(2)}) %copy-start) | copy-done | bytes 1048600
  1.9 0.0 copy-start.3
  1.9 0.9 %copy-done.3 = f32[32,4,2,256]{3,2,1,0:T(2,128)S(1)} copy-done((f32[32,4,2,256]{3,2,1,0:T(2,128)S(1)}, f32[32,4,2,256]{3,2,1,0:T(2,128)}, u32[]{:S(2)}) %copy-start.3) | copy-done | bytes 262168
  2.8 0.0 copy-start.4
  2.8 0.9 %copy-done.4 = bf16[512,256]{1,0:T(8,128)(2,1)S(1)} copy-done((bf16[512,256]{1,0:T(8,128)(2,1)S(1)}, bf16[512,256]{1,0:T(8,128)(2,1)}, u32[]{:S(2)}) %copy-start.4) | copy-done | bytes 262168
  3.8 1.3 %shard_map.77 = bf16[8,160,256]{2,1,0:T(8,128)(2,1)} custom-call(bf16[1,32,16,2,512]{4,3,2,1,0:T(2,128)(2,1)S(1)} %copy-done, f32[32,4,2,256]{3,2,1,0:T(2,128)S(1)} %copy-done.3, bf16[512,256]{1,0:T(8,128)(2,1)S(1)} %copy-done.4), custom_call_target="tpu_custom_call" | custom-call | tf_op jit(solution)/shard_map/pallas_call | solution.py:30
  5.0 0.0 copy-start.5
  5.0 0.0 copy-start.1
  5.1 7.4 %all-to-all-start = ((bf16[8,160,256]{2,1,0:T(8,128)(2,1)}), bf16[8,160,256]{2,1,0:T(8,128)(2,1)S(1)}, u32[]{:S(2)}, u32[]{:S(2)}) async-start(bf16[8,160,256]{2,1,0:T(8,128)(2,1)} %shard_map.77), calls=%async_computation | async-start | bytes 1310720 | tf_op jit(solution)/shard_map/all_to_all | solution.py:171
  12.4 0.0 copy-done.5
  12.4 22.4 %all_gather.6 = s32[16,2,5]{2,1,0:T(2,128)S(1)} all-gather(s32[4,2,5]{2,1,0:T(2,128)S(1)} %copy-done.5), channel_id=1, replica_groups=mesh['groups'=2,'gx'=4,'gy'=2,'ta'=2] {'gx'}, dimensions={0}, use_global_device_ids=true | all-gather | bytes 800 | tf_op jit(solution)/shard_map/all_gather | solution.py:147
  34.8 0.1 copy.32
  34.9 4.4 %all_gather.7 = s32[16,4,5]{0,2,1:T(8,128)S(1)} all-gather(s32[16,2,5]{0,2,1:T(8,128)S(1)} %copy.32), channel_id=1, replica_groups=mesh['groups'=2,'gx'=4,'gy'=2,'ta'=2] {'gy'}, dimensions={1}, use_global_device_ids=true | all-gather | bytes 1920 | tf_op jit(solution)/shard_map/all_gather | solution.py:148
  39.3 0.1 copy.33
  39.4 0.1 broadcast_in_dim.7
  39.5 0.1 copy.39
  39.6 0.1 stack_broadcast_in_dim.34
  39.7 0.1 copy.38
  39.8 0.1 stack_broadcast_in_dim.32
  39.9 0.1 fusion
  40.0 0.1 fusion.1
  40.0 0.1 add_bitcast_fusion.1
  40.1 0.1 copy.37
  40.2 0.1 stack_broadcast_in_dim.30
  40.3 0.1 add_bitcast_fusion
  40.4 0.1 copy.35
  40.5 0.1 stack_broadcast_in_dim.28
  40.6 0.1 stack_broadcast_in_dim.35
  40.6 0.1 stack_broadcast_in_dim.33
  40.7 0.1 stack_broadcast_in_dim.31
  40.8 0.1 stack_broadcast_in_dim.29
  40.9 0.0 all-to-all-done.refs_0_
  40.9 0.1 broadcast_in_dim.8.refs_1_
  41.0 0.0 copy-done.1
  41.0 0.0 copy-start.2
  41.0 3.1 %shard_map.78 = bf16[8,32,256]{2,1,0:T(8,128)(2,1)S(1)} custom-call(bf16[8,160,256]{2,1,0:T(8,128)(2,1)S(1)} %all-to-all-done.refs_0_, s32[2,32,256]{2,1,0:T(8,128)S(1)} %broadcast_in_dim.8.refs_1_, s32[4,2,32,256]{3,2,1,0:T(8,128)S(1)} %add_add_fusion.refs_2_, bf16[8,256,256]{2,1,0:T(8,128)(2,1)S(1)} %copy-done.1), custom_call_target="tpu_custom_call" | custom-call | tf_op jit(solution)/shard_map/pallas_call | solution.py:117
  44.1 12.0 %all_to_all.10.state_ref = bf16[8,32,256]{2,1,0:T(8,128)(2,1)S(1)} all-to-all(bf16[8,32,256]{2,1,0:T(8,128)(2,1)S(1)} %shard_map.78), channel_id=1, replica_groups=mesh['groups'=2,'gx'=4,'gy'=2,'ta'=2] {'gx','gy'}, dimensions={0} | all-to-all | bytes 262144 | tf_op jit(solution)/shard_map/all_to_all | solution.py:174
  56.1 0.0 copy-done.2
  56.1 1.0 %shard_map.79 = (bf16[32,4,2,512]{3,2,1,0:T(2,128)(2,1)}, f32[32,4,2,256]{3,2,1,0:T(2,128)}) custom-call(bf16[8,32,256]{2,1,0:T(8,128)(2,1)S(1)} %all_to_all.10.state_ref, bf16[512,512]{1,0:T(8,128)(2,1)S(1)} %copy-done.2), custom_call_target="tpu_custom_call" | custom-call | tf_op jit(solution)/shard_map/pallas_call | solution.py:136
  (7 shorter events, 0.1 us)
Async XLA Ops:
  0.6 1.2 %copy-start = (bf16[1,32,16,2,512]{4,3,2,1,0:T(2,128)(2,1)S(1)}, bf16[1,32,16,2,512]{4,3,2,1,0:T(2,128)(2,1)}, u32[]{:S(2)}) copy-start(bf16[1,32,16,2,512]{4,3,2,1,0:T(2,128)(2,1)} %frames_ref.1) | copy-start | bytes 3145732
  1.9 0.9 %copy-start.3 = (f32[32,4,2,256]{3,2,1,0:T(2,128)S(1)}, f32[32,4,2,256]{3,2,1,0:T(2,128)}, u32[]{:S(2)}) copy-start(f32[32,4,2,256]{3,2,1,0:T(2,128)} %start_ref.1) | copy-start | bytes 786436
  2.8 0.9 %copy-start.4 = (bf16[512,256]{1,0:T(8,128)(2,1)S(1)}, bf16[512,256]{1,0:T(8,128)(2,1)}, u32[]{:S(2)}) copy-start(bf16[512,256]{1,0:T(8,128)(2,1)} %inlet_ref.1) | copy-start | bytes 786436
  5.0 7.4 %copy-start.5 = (s32[4,2,5]{2,1,0:T(2,128)S(1)}, s32[4,2,5]{2,1,0:T(2,128)}, u32[]{:S(2)}) copy-start(s32[4,2,5]{2,1,0:T(2,128)} %param.8) | copy-start | bytes 484
  5.0 35.9 %copy-start.1 = (bf16[8,256,256]{2,1,0:T(8,128)(2,1)S(1)}, bf16[8,256,256]{2,1,0:T(8,128)(2,1)}, u32[]{:S(2)}) copy-start(bf16[8,256,256]{2,1,0:T(8,128)(2,1)} %refs_3_.1) | copy-start | bytes 3145732
  5.1 35.9 %all-to-all-start = ((bf16[8,160,256]{2,1,0:T(8,128)(2,1)}), bf16[8,160,256]{2,1,0:T(8,128)(2,1)S(1)}, u32[]{:S(2)}, u32[]{:S(2)}) async-start(bf16[8,160,256]{2,1,0:T(8,128)(2,1)} %shard_map.77), calls=%async_computation | async-start | bytes 1310720 | tf_op jit(solution)/shard_map/all_to_all | solution.py:171
  41.0 15.1 %copy-start.2 = (bf16[512,512]{1,0:T(8,128)(2,1)S(1)}, bf16[512,512]{1,0:T(8,128)(2,1)}, u32[]{:S(2)}) copy-start(bf16[512,512]{1,0:T(8,128)(2,1)} %readout_ref.1) | copy-start | bytes 1572868

commit v2 on v1

--- a/solution.py
+++ b/solution.py
@@ -7,44 +7,90 @@
 
 PLANE = ("gx", "gy")
 VMEM_LIMIT = 40 * 1024 * 1024
+WIDE_VMEM_LIMIT = 60 * 1024 * 1024
 
 
 def whole(shape):
     return pl.BlockSpec(shape, lambda *_: (0,) * len(shape))
 
 
-def inlet_kernel(frames_ref, start_ref, inlet_ref, packed_ref):
+def inlet_kernel(frames_ref, start_ref, index_ref, inlet_ref, packed_ref):
     peers, rows, units = packed_ref.shape
+    entries = index_ref.shape[-1]
     cells = frames_ref[...].reshape(-1, frames_ref.shape[-1])
     drive = jnp.dot(cells, inlet_ref[...], preferred_element_type=jnp.float32)
     drive_rows = drive.shape[0] // peers
     packed_ref[:, :drive_rows, :] = drive.astype(jnp.bfloat16).reshape(peers, drive_rows, units)
-    state = start_ref[...].reshape(peers, rows - drive_rows, units)
-    packed_ref[:, drive_rows:, :] = state.astype(jnp.bfloat16)
-
-
-def pack_for_peers(frames, start_state, inlet_coupler, peers):
+    state_rows = start_ref.shape[0] * index_ref.shape[0] // peers
+    state = start_ref[...].reshape(peers, state_rows, units)
+    packed_ref[:, drive_rows : drive_rows + state_rows, :] = state.astype(jnp.bfloat16)
+    index = jnp.broadcast_to(index_ref[...].astype(jnp.bfloat16)[None], (peers,) + index_ref.shape)
+    packed_ref[:, drive_rows + state_rows :, :] = jnp.zeros((peers, index_ref.shape[0], units), jnp.bfloat16)
+    packed_ref[:, drive_rows + state_rows :, :entries] = index
+
+
+def pack_for_peers(frames, start_state, tile_index, inlet_coupler, peers):
     units = inlet_coupler.shape[1]
+    blocks = tile_index.shape[0] * tile_index.shape[1]
     drive_rows = frames.size // frames.shape[-1] // peers
     state_rows = start_state.size // units // peers
+    index = tile_index.reshape(blocks, -1)
+    out_shape = (peers, drive_rows + state_rows + blocks, units)
     return pl.pallas_call(
         inlet_kernel,
-        out_shape=jax.ShapeDtypeStruct((peers, drive_rows + state_rows, units), jnp.bfloat16),
-        compiler_params=pltpu.CompilerParams(vmem_limit_bytes=VMEM_LIMIT),
-    )(frames, start_state, inlet_coupler)
-
-
-def steps_kernel(count_x, count_y, packed_ref, own_ref, from_ref, bank_ref, sent_ref):
+        grid=(1,),
+        in_specs=[whole(v.shape) for v in (frames, start_state, index, inlet_coupler)],
+        out_specs=whole(out_shape),
+        out_shape=jax.ShapeDtypeStruct(out_shape, jnp.bfloat16),
+        compiler_params=pltpu.CompilerParams(vmem_limit_bytes=WIDE_VMEM_LIMIT),
+    )(frames, start_state, index, inlet_coupler)
+
+
+def neighbour_choices(packed_ref, base, count_x, count_y, first_other):
+    units = packed_ref.shape[-1]
+
+    def entry(j, k):
+        parts = []
+        for i in range(count_x):
+            rows = packed_ref[i * count_y + j, base:, :].astype(jnp.float32)
+            parts.append(jnp.broadcast_to(rows[:, k : k + 1], (rows.shape[0], units)))
+        return jnp.concatenate(parts, axis=0)
+
+    columns = range(count_y)
+    own = [entry(j, 0) for j in columns]
+    torus_rows = own[0].shape[0]
+    low = lax.broadcasted_iota(jnp.int32, own[0].shape, 0) % 2 == 0
+    left = [entry(j, 3) for j in columns]
+    right = [entry(j, 4) for j in columns]
+    other = []
+    for j in columns:
+        other.append(
+            [
+                pltpu.roll(entry(j, 1), torus_rows - 2, axis=0),
+                pltpu.roll(entry(j, 2), 2, axis=0),
+                jnp.where(
+                    low,
+                    pltpu.roll(left[j], torus_rows - 1, axis=0),
+                    pltpu.roll(left[(j + 1) % count_y], 1, axis=0),
+                ),
+                jnp.where(
+                    low,
+                    pltpu.roll(right[j - 1], torus_rows - 1, axis=0),
+                    pltpu.roll(right[j], 1, axis=0),
+                ),
+            ]
+        )
+    return own, [[v - first_other for v in choices] for choices in other], low
+
+
+def steps_kernel(count_x, count_y, torus_rows, packed_ref, bank_ref, sent_ref):
     peers, rows, units = packed_ref.shape
-    torus_rows = own_ref.shape[1]
     home_rows = torus_rows // count_x
     trajectories = sent_ref.shape[1] // home_rows
     drive_rows = trajectories * torus_rows
+    state_rows = trajectories * home_rows
     halves = bank_ref.shape[0] // 2
     groups = [(j, t) for j in range(count_y) for t in range(trajectories)]
-
-    def home_slice(t, base=0):
-        return slice(base + t * home_rows, base + (t + 1) * home_rows)
 
     def choose(index, products):
         chosen = products[-1]
@@ -52,34 +98,32 @@
             chosen = jnp.where(index == tile, products[tile], chosen)
         return chosen
 
-    column = lax.broadcasted_iota(jnp.int32, (torus_rows, units), 0) % 2
-    low = column == 0
+    own_index, other_index, low = neighbour_choices(
+        packed_ref, drive_rows + state_rows, count_x, count_y, halves
+    )
     state = []
     for j, t in groups:
         for i in range(count_x):
-            piece = packed_ref[i * count_y + j, drive_rows : rows, :].astype(jnp.float32)
-            state.append(piece[home_slice(t)])
+            piece = packed_ref[i * count_y + j, drive_rows : drive_rows + state_rows, :]
+            piece = piece.astype(jnp.float32)
+            state.append(piece[t * home_rows : (t + 1) * home_rows])
     state = jnp.concatenate(state, axis=0)
     for step in range(count_x):
         state_half = state.astype(jnp.bfloat16)
-        own = [
+        products = [
             jnp.dot(state_half, bank_ref[tile], preferred_element_type=jnp.float32)
-            for tile in range(halves)
+            for tile in range(2 * halves)
         ]
-        other = [
-            jnp.dot(state_half, bank_ref[halves + tile], preferred_element_type=jnp.float32)
-            for tile in range(halves)
-        ]
-        kept, after_x, left, right = {}, {}, {}, {}
+        kept, left, right = {}, {}, {}
         for g, (j, t) in enumerate(groups):
             span = slice(g * torus_rows, (g + 1) * torus_rows)
-            others = [product[span] for product in other]
-            total = choose(own_ref[j], [product[span] for product in own])
-            total += pltpu.roll(choose(from_ref[0, j], others), 2, axis=0)
-            total += pltpu.roll(choose(from_ref[1, j], others), torus_rows - 2, axis=0)
+            others = [product[span] for product in products[halves:]]
+            total = choose(own_index[j], [product[span] for product in products[:halves]])
+            total += pltpu.roll(choose(other_index[j][0], others), 2, axis=0)
+            total += pltpu.roll(choose(other_index[j][1], others), torus_rows - 2, axis=0)
             kept[j, t] = total
-            left[j, t] = choose(from_ref[2, j], others)
-            right[j, t] = choose(from_ref[3, j], others)
+            left[j, t] = choose(other_index[j][2], others)
+            right[j, t] = choose(other_index[j][3], others)
         fresh = []
         for j, t in groups:
             before, behind = (j - 1) % count_y, (j + 1) % count_y
@@ -108,17 +152,17 @@
             sent_ref[i * count_y + j] = jnp.concatenate(pieces, axis=0).astype(jnp.bfloat16)
 
 
-def run_steps(packed, own_index, from_index, tile_bank, count_x, count_y, home_rows):
+def run_steps(packed, tile_bank, count_x, count_y, torus_rows, home_rows):
     peers, _, units = packed.shape
 
     def kernel(*refs):
-        steps_kernel(count_x, count_y, *refs)
+        steps_kernel(count_x, count_y, torus_rows, *refs)
 
     return pl.pallas_call(
         kernel,
         out_shape=jax.ShapeDtypeStruct((peers, home_rows, units), jnp.bfloat16),
         compiler_params=pltpu.CompilerParams(vmem_limit_bytes=VMEM_LIMIT),
-    )(packed, own_index, from_index, tile_bank)
+    )(packed, tile_bank)
 
 
 def readout_kernel(state_ref, readout_ref, field_ref, final_ref):
@@ -143,34 +187,16 @@
     )(state, readout_operator)
 
 
-def tile_choices(tile_index, first_other, units):
-    everywhere = lax.all_gather(tile_index, "gx", axis=0, tiled=True)
-    everywhere = lax.all_gather(everywhere, "gy", axis=1, tiled=True)
-
-    def by_row(index):
-        pairs = index.reshape(index.shape[0], -1, 2).transpose(1, 0, 2)
-        pairs = pairs.reshape(pairs.shape[0], -1, 1)
-        return jnp.broadcast_to(pairs, pairs.shape[:2] + (units,))
-
-    leaving = [
-        jnp.roll(everywhere[..., 1], -1, 0),
-        jnp.roll(everywhere[..., 2], 1, 0),
-        jnp.roll(everywhere[..., 3], -1, 1),
-        jnp.roll(everywhere[..., 4], 1, 1),
-    ]
-    return by_row(everywhere[..., 0]), jnp.stack([by_row(v) for v in leaving]) - first_other
-
-
 def by_trajectory(frames, start_state, tile_index, tile_bank, inlet_coupler, readout_operator):
     count_x, count_y = lax.axis_size("gx"), lax.axis_size("gy")
     peers = count_x * count_y
     units = inlet_coupler.shape[1]
     block_shape = start_state.shape[:-1]
-    packed = pack_for_peers(frames, start_state, inlet_coupler, peers)
-    own_index, from_index = tile_choices(tile_index, tile_bank.shape[0] // 2, units)
+    packed = pack_for_peers(frames, start_state, tile_index, inlet_coupler, peers)
     packed = lax.all_to_all(packed, PLANE, 0, 0, tiled=True)
+    torus_rows = frames.shape[2] * frames.shape[3]
     home_rows = start_state.size // units // peers
-    sent = run_steps(packed, own_index, from_index, tile_bank, count_x, count_y, home_rows)
+    sent = run_steps(packed, tile_bank, count_x, count_y, torus_rows, home_rows)
     state = lax.all_to_all(sent, PLANE, 0, 0, tiled=True)
     return read_out(state, readout_operator, block_shape)
 

time: 57.5 us -> 43.7 us (0.76)
  starting transfers between devices: 7.38 us -> 0 us
  local copies, waits for them, and re-layouts: 4.66 us -> 0.01 us
  blocking collectives: 38.7 us -> 36.2 us
  Pallas kernels: 5.42 us -> 6.62 us
    all_gather x2 -> x0, blocking collectives: 26.8 us -> none  [the longest x1 22.4 us: tile_choices(): everywhere = lax.all_gather(tile_index, 'gx', axis=0, tiled=True)]
    all_to_all x0 -> x1, blocking collectives: none -> 25.7 us  [by_trajectory(): packed = lax.all_to_all(packed, PLANE, 0, 0, tiled=True)]
    all_to_all x1 -> x0, starting transfers between devices: 7.38 us -> none  [by_trajectory(): packed = lax.all_to_all(packed, PLANE, 0, 0, tiled=True)]
    unnamed x12 -> x4, local copies, waits for them, and re-layouts: 3.13 us -> 0.01 us
    all_to_all x1, blocking collectives: 12 us -> 10.5 us  [by_trajectory(): state = lax.all_to_all(sent, PLANE, 0, 0, tiled=True)]
    pallas_call x1, Pallas kernels: 1.29 us -> 2.65 us  [pack_for_peers(): pl.pallas_call(inlet_kernel, grid=(1,), in_specs=[whole(v.shape) for v in...]
    another operation x8 -> x0, local copies, waits for them, and re-layouts: 0.66 us -> none  [tile_choices(): jnp.stack([by_row(v) for v in leaving]) - first_other]
  transfers between devices with their start and end apart: 1 -> 0, of which waited for: 0 -> 0; matrix products, arithmetic and copies ran while one was open for 3% -> 0% of each run, Pallas kernels for 0% -> 0%
where the time goes in v2:
time: 43.7 us; the launch traced here: 43.4 us
  blocking collectives  36.2 us (83%)
  Pallas kernels  6.62 us (15%)
  between operations  0.64 us (1%)
    all_to_all x1, blocking collectives, by_trajectory(): packed = lax.all_to_all(packed, PLANE, 0, 0, tiled=True)  25.7 us
    all_to_all x1, blocking collectives, by_trajectory(): state = lax.all_to_all(sent, PLANE, 0, 0, tiled=True)  10.5 us
    pallas_call x1, Pallas kernels, run_steps(): pl.pallas_call(kernel, out_shape=jax.ShapeDtypeStruct((peers, home_rows,...  2.95 us
    pallas_call x1, Pallas kernels, pack_for_peers(): pl.pallas_call(inlet_kernel, grid=(1,), in_specs=[whole(v.shape) for v in...  2.65 us
    pallas_call x1, Pallas kernels, read_out(): pl.pallas_call(readout_kernel, out_shape=(jax.ShapeDtypeStruct(block_shap...  1.01 us

profile of v2, /device:TPU:0, one launch (start us, length us, event | category | flops | bytes accessed | tf_op | source)
XLA Modules:
  0.0 43.4 jit_solution(2818231926764215468)
XLA Ops:
  0.6 2.6 %shard_map.77 = bf16[8,168,256]{2,1,0:T(8,128)(2,1)} custom-call(bf16[1,32,16,2,512]{4,3,2,1,0:T(2,128)(2,1)} %frames_ref.1, f32[32,4,2,256]{3,2,1,0:T(2,128)} %start_ref.1, s32[8,5]{1,0:T(8,128)} %bitcast.1, bf16[512,256]{1,0:T(8,128)(2,1)} %inlet_ref.1), custom_call_target="tpu_custom_call" | custom-call | tf_op jit(solution)/shard_map/pallas_call | solution.py:39
  3.3 0.0 copy-start
  3.3 25.7 %all_to_all.10.refs_0_ = bf16[8,168,256]{2,1,0:T(8,128)(2,1)S(1)} all-to-all(bf16[8,168,256]{2,1,0:T(8,128)(2,1)} %shard_map.77), channel_id=1, replica_groups=mesh['groups'=2,'gx'=4,'gy'=2,'ta'=2] {'gx','gy'}, dimensions={0} | all-to-all | bytes 1376256 | tf_op jit(solution)/shard_map/all_to_all | solution.py:196
  28.9 0.0 copy-done
  28.9 0.0 copy-start.1
  28.9 3.0 %shard_map.78 = bf16[8,32,256]{2,1,0:T(8,128)(2,1)S(1)} custom-call(bf16[8,168,256]{2,1,0:T(8,128)(2,1)S(1)} %all_to_all.10.refs_0_, bf16[8,256,256]{2,1,0:T(8,128)(2,1)S(1)} %copy-done), custom_call_target="tpu_custom_call" | custom-call | tf_op jit(solution)/shard_map/pallas_call | solution.py:161
  31.9 10.5 %all_to_all.11.state_ref = bf16[8,32,256]{2,1,0:T(8,128)(2,1)S(1)} all-to-all(bf16[8,32,256]{2,1,0:T(8,128)(2,1)S(1)} %shard_map.78), channel_id=1, replica_groups=mesh['groups'=2,'gx'=4,'gy'=2,'ta'=2] {'gx','gy'}, dimensions={0} | all-to-all | bytes 262144 | tf_op jit(solution)/shard_map/all_to_all | solution.py:200
  42.4 0.0 copy-done.1
  42.4 1.0 %shard_map.79 = (bf16[32,4,2,512]{3,2,1,0:T(2,128)(2,1)}, f32[32,4,2,256]{3,2,1,0:T(2,128)}) custom-call(bf16[8,32,256]{2,1,0:T(8,128)(2,1)S(1)} %all_to_all.11.state_ref, bf16[512,512]{1,0:T(8,128)(2,1)S(1)} %copy-done.1), custom_call_target="tpu_custom_call" | custom-call | tf_op jit(solution)/shard_map/pallas_call | solution.py:180
Async XLA Ops:
  3.3 25.7 %copy-start = (bf16[8,256,256]{2,1,0:T(8,128)(2,1)S(1)}, bf16[8,256,256]{2,1,0:T(8,128)(2,1)}, u32[]{:S(2)}) copy-start(bf16[8,256,256]{2,1,0:T(8,128)(2,1)} %refs_1_.1) | copy-start | bytes 3145732
  28.9 13.5 %copy-start.1 = (bf16[512,512]{1,0:T(8,128)(2,1)S(1)}, bf16[512,512]{1,0:T(8,128)(2,1)}, u32[]{:S(2)}) copy-start(bf16[512,512]{1,0:T(8,128)(2,1)} %readout_ref.1) | copy-start | bytes 1572868

commit v3 on v2

--- a/solution.py
+++ b/solution.py
@@ -14,36 +14,95 @@
     return pl.BlockSpec(shape, lambda *_: (0,) * len(shape))
 
 
-def inlet_kernel(frames_ref, start_ref, index_ref, inlet_ref, packed_ref):
-    peers, rows, units = packed_ref.shape
+def place_in_plane():
+    return lax.axis_index("gx") * lax.axis_size("gy") + lax.axis_index("gy")
+
+
+def place_in_plane():
+    return lax.axis_index("gx") * lax.axis_size("gy") + lax.axis_index("gy")
+
+
+def partners(peers):
+    return list(range(peers - 1, -1, -1))
+
+
+def inlet_kernel(peers, order, frames_hbm, start_hbm, index_ref, inlet_hbm, *refs):
+    packed_refs, (frames_ref, start_ref, inlet_ref, arrived) = refs[:-4], refs[-4:]
+    units = inlet_ref.shape[1]
+    place = place_in_plane()
+    share = frames_ref.shape[1]
     entries = index_ref.shape[-1]
-    cells = frames_ref[...].reshape(-1, frames_ref.shape[-1])
-    drive = jnp.dot(cells, inlet_ref[...], preferred_element_type=jnp.float32)
-    drive_rows = drive.shape[0] // peers
-    packed_ref[:, :drive_rows, :] = drive.astype(jnp.bfloat16).reshape(peers, drive_rows, units)
-    state_rows = start_ref.shape[0] * index_ref.shape[0] // peers
-    state = start_ref[...].reshape(peers, state_rows, units)
-    packed_ref[:, drive_rows : drive_rows + state_rows, :] = state.astype(jnp.bfloat16)
-    index = jnp.broadcast_to(index_ref[...].astype(jnp.bfloat16)[None], (peers,) + index_ref.shape)
-    packed_ref[:, drive_rows + state_rows :, :] = jnp.zeros((peers, index_ref.shape[0], units), jnp.bfloat16)
-    packed_ref[:, drive_rows + state_rows :, :entries] = index
-
-
-def pack_for_peers(frames, start_state, tile_index, inlet_coupler, peers):
+    inlet_copy = pltpu.make_async_copy(inlet_hbm, inlet_ref, arrived.at[0, len(order)])
+    inlet_copy.start()
+    cell_copies, state_copies = [], []
+    for slot, k in enumerate(order):
+        mine = pl.ds((place ^ k) * share, share)
+        cell_copies.append(
+            pltpu.make_async_copy(frames_hbm.at[0, mine], frames_ref.at[slot], arrived.at[0, slot])
+        )
+        state_copies.append(
+            pltpu.make_async_copy(start_hbm.at[mine], start_ref.at[slot], arrived.at[1, slot])
+        )
+    for copy in cell_copies + state_copies:
+        copy.start()
+    index = index_ref[...].astype(jnp.bfloat16)
+    blank = jnp.zeros((index.shape[0], units), jnp.bfloat16)
+    inlet_copy.wait()
+    for slot, packed_ref in enumerate(packed_refs):
+        cell_copies[slot].wait()
+        cells = frames_ref[slot].reshape(-1, frames_ref.shape[-1])
+        drive = jnp.dot(cells, inlet_ref[...], preferred_element_type=jnp.float32)
+        drive_rows = drive.shape[0]
+        packed_ref[:drive_rows, :] = drive.astype(jnp.bfloat16)
+        state_copies[slot].wait()
+        state = start_ref[slot].reshape(-1, units)
+        after = drive_rows + state.shape[0]
+        packed_ref[drive_rows:after, :] = state.astype(jnp.bfloat16)
+        packed_ref[after:, :] = blank
+        packed_ref[after:, :entries] = index
+
+
+def pack_for_peers(frames, start_state, tile_index, inlet_coupler, peers, order, vmem_limit):
     units = inlet_coupler.shape[1]
     blocks = tile_index.shape[0] * tile_index.shape[1]
     drive_rows = frames.size // frames.shape[-1] // peers
     state_rows = start_state.size // units // peers
     index = tile_index.reshape(blocks, -1)
-    out_shape = (peers, drive_rows + state_rows + blocks, units)
+    out_shape = (drive_rows + state_rows + blocks, units)
+    share = frames.shape[1] // peers
+    far = pl.BlockSpec(memory_space=pltpu.HBM)
+
+    def kernel(*refs):
+        inlet_kernel(peers, order, *refs)
+
     return pl.pallas_call(
-        inlet_kernel,
-        grid=(1,),
-        in_specs=[whole(v.shape) for v in (frames, start_state, index, inlet_coupler)],
-        out_specs=whole(out_shape),
-        out_shape=jax.ShapeDtypeStruct(out_shape, jnp.bfloat16),
-        compiler_params=pltpu.CompilerParams(vmem_limit_bytes=WIDE_VMEM_LIMIT),
+        kernel,
+        in_specs=[far, far, pl.BlockSpec(memory_space=pltpu.VMEM), far],
+        out_shape=[jax.ShapeDtypeStruct(out_shape, jnp.bfloat16)] * len(order),
+        scratch_shapes=[
+            pltpu.VMEM((len(order), share) + frames.shape[2:], frames.dtype),
+            pltpu.VMEM((len(order), share) + start_state.shape[1:], start_state.dtype),
+            pltpu.VMEM(inlet_coupler.shape, inlet_coupler.dtype),
+            pltpu.SemaphoreType.DMA((2, len(order) + 1)),
+        ],
+        compiler_params=pltpu.CompilerParams(vmem_limit_bytes=vmem_limit),
     )(frames, start_state, index, inlet_coupler)
+
+
+def exchange(frames, start_state, tile_index, inlet_coupler, peers):
+    order = partners(peers)
+    half = peers // 2
+    got = []
+    for part, limit in ((order[:half], WIDE_VMEM_LIMIT), (order[half:], VMEM_LIMIT)):
+        packed = list(
+            pack_for_peers(frames, start_state, tile_index, inlet_coupler, peers, part, limit)
+        )
+        tile_index, packed[0] = lax.optimization_barrier((tile_index, packed[0]))
+        for k, block in zip(part, packed):
+            if k:
+                block = lax.ppermute(block, PLANE, [(p, p ^ k) for p in range(peers)])
+            got.append(block)
+    return got
 
 
 def neighbour_choices(packed_ref, base, count_x, count_y, first_other):
@@ -83,8 +142,12 @@
     return own, [[v - first_other for v in choices] for choices in other], low
 
 
-def steps_kernel(count_x, count_y, torus_rows, packed_ref, bank_ref, sent_ref):
+def steps_kernel(count_x, count_y, torus_rows, *refs):
+    got_refs, (bank_ref, sent_ref, packed_ref) = refs[:-3], refs[-3:]
     peers, rows, units = packed_ref.shape
+    place = place_in_plane()
+    for k, got_ref in zip(partners(peers), got_refs):
+        packed_ref[place ^ k] = got_ref[...]
     home_rows = torus_rows // count_x
     trajectories = sent_ref.shape[1] // home_rows
     drive_rows = trajectories * torus_rows
@@ -153,7 +216,8 @@
 
 
 def run_steps(packed, tile_bank, count_x, count_y, torus_rows, home_rows):
-    peers, _, units = packed.shape
+    peers = len(packed)
+    rows, units = packed[0].shape
 
     def kernel(*refs):
         steps_kernel(count_x, count_y, torus_rows, *refs)
@@ -161,8 +225,9 @@
     return pl.pallas_call(
         kernel,
         out_shape=jax.ShapeDtypeStruct((peers, home_rows, units), jnp.bfloat16),
+        scratch_shapes=[pltpu.VMEM((peers, rows, units), jnp.bfloat16)],
         compiler_params=pltpu.CompilerParams(vmem_limit_bytes=VMEM_LIMIT),
-    )(packed, tile_bank)
+    )(*packed, tile_bank)
 
 
 def readout_kernel(state_ref, readout_ref, field_ref, final_ref):
@@ -192,8 +257,7 @@
     peers = count_x * count_y
     units = inlet_coupler.shape[1]
     block_shape = start_state.shape[:-1]
-    packed = pack_for_peers(frames, start_state, tile_index, inlet_coupler, peers)
-    packed = lax.all_to_all(packed, PLANE, 0, 0, tiled=True)
+    packed = exchange(frames, start_state, tile_index, inlet_coupler, peers)
     torus_rows = frames.shape[2] * frames.shape[3]
     home_rows = start_state.size // units // peers
     sent = run_steps(packed, tile_bank, count_x, count_y, torus_rows, home_rows)
@@ -274,7 +338,7 @@
     )
     def shards(frames, start_state, *rest):
         peers = mesh.shape["gx"] * mesh.shape["gy"]
-        fits = start_state.shape[0] % peers == 0 and start_state.shape[2] == 2
+        fits = start_state.shape[0] % peers == 0 and peers & (peers - 1) == 0 and start_state.shape[2] == 2
         fits = fits and start_state.shape[1] % 4 == 0
         body = by_trajectory if fits and frames.shape[0] == 1 else by_block
         return body(frames, start_state, *rest)

time: 43.7 us -> 41.7 us (0.954)
  blocking collectives: 36.2 us -> 11.8 us
  starting transfers between devices: 0 us -> 15.6 us
  waiting for transfers between devices: 0 us -> 3.95 us
  Pallas kernels: 6.62 us -> 9.42 us
    all_to_all x1 -> x0, blocking collectives: 25.7 us -> none  [by_trajectory(): packed = lax.all_to_all(packed, PLANE, 0, 0, tiled=True)]
    ppermute x0 -> x7, starting transfers between devices: none -> 15.6 us  [exchange(): block = lax.ppermute(block, PLANE, [(p, p ^ k) for p in range(peers)])]
    ppermute x0 -> x7, waiting for transfers between devices: none -> 3.95 us  [exchange(): block = lax.ppermute(block, PLANE, [(p, p ^ k) for p in range(peers)])]
    pallas_call x1 -> x2, Pallas kernels: 2.65 us -> 5.35 us  [pack_for_peers(): pl.pallas_call(kernel, in_specs=[far, far, pl.BlockSpec(memory_space=pltp...]
    all_to_all x1, blocking collectives: 10.5 us -> 11.8 us  [by_trajectory(): state = lax.all_to_all(sent, PLANE, 0, 0, tiled=True)]
  transfers between devices with their start and end apart: 0 -> 7, of which waited for: 0 -> 3; matrix products, arithmetic and copies ran while one was open for 0% -> 0% of each run, Pallas kernels for 0% -> 5%
where the time goes in v3:
time: 41.7 us; the launch traced here: 41.5 us
  starting transfers between devices  15.6 us (37%)
  blocking collectives  11.8 us (28%)
  Pallas kernels  9.42 us (23%)
  waiting for transfers between devices  3.95 us (9%)
  between operations  0.71 us (2%)
    ppermute x7, starting transfers between devices, exchange(): block = lax.ppermute(block, PLANE, [(p, p ^ k) for p in range(peers)])  15.6 us
    all_to_all x1, blocking collectives, by_trajectory(): state = lax.all_to_all(sent, PLANE, 0, 0, tiled=True)  11.8 us
    pallas_call x2, Pallas kernels, pack_for_peers(): pl.pallas_call(kernel, in_specs=[far, far, pl.BlockSpec(memory_space=pltp...  5.35 us
    ppermute x7, waiting for transfers between devices, exchange(): block = lax.ppermute(block, PLANE, [(p, p ^ k) for p in range(peers)])  3.95 us
    pallas_call x1, Pallas kernels, run_steps(): pl.pallas_call(kernel, out_shape=jax.ShapeDtypeStruct((peers, home_rows,...  3.06 us
    pallas_call x1, Pallas kernels, read_out(): pl.pallas_call(readout_kernel, out_shape=(jax.ShapeDtypeStruct(block_shap...  1.01 us
  transfers between devices with their start and end apart: 7, of which 3 were waited for; matrix products, arithmetic and copies ran while one was open for 0% of the time, Pallas kernels for 5%

profile of v3, /device:TPU:0, one launch (start us, length us, event | category | flops | bytes accessed | tf_op | source)
XLA Modules:
  0.0 41.5 jit_solution(12686759235710465599)
XLA Ops:
  0.6 0.0 copy-start
  0.6 0.0 copy-start.2
  0.7 0.0 copy-start.3
  0.7 0.0 copy-start.5
  0.7 3.5 %shard_map.77 = (bf16[168,256]{1,0:T(8,128)(2,1)}, bf16[168,256]{1,0:T(8,128)(2,1)}, bf16[168,256]{1,0:T(8,128)(2,1)}, bf16[168,256]{1,0:T(8,128)(2,1)}) custom-call(bf16[1,32,16,2,512]{4,3,2,1,0:T(2,128)(2,1)} %refs_0_.3, f32[32,4,2,256]{3,2,1,0:T(2,128)} %refs_1_.3, s32[8,5]{1,0:T(8,128)} %bitcast.2, bf16[512,256]{1,0:T(8,128)(2,1)} %refs_3_.3), custom_call_target="tpu_custom_call" | custom-call | tf_op jit(solution)/shard_map/pallas_call | solution.py:78
  4.2 0.0 copy-start.1
  4.2 6.0 %collective-permute-start = (bf16[168,256]{1,0:T(8,128)(2,1)}, bf16[168,256]{1,0:T(8,128)(2,1)S(1)}, u32[]{:S(2)}, u32[]{:S(2)}) collective-permute-start(bf16[168,256]{1,0:T(8,128)(2,1)} %get-tuple-element.14), channel_id=1, source_target_pairs={{0,14},{2,12},{4,10},{6,8},{8,6},{10,4},{12,2},{14,0},{1,15},{3,13... | collective-permute-start | bytes 258056 | tf_op jit(solution)/shard_map/ppermute | solution.py:103
  10.2 0.2 collective-permute-start.1
  10.4 0.8 %collective-permute-start.2 = (bf16[168,256]{1,0:T(8,128)(2,1)}, bf16[168,256]{1,0:T(8,128)(2,1)S(1)}, u32[]{:S(2)}, u32[]{:S(2)}) collective-permute-start(bf16[168,256]{1,0:T(8,128)(2,1)} %get-tuple-element.16), channel_id=1, source_target_pairs={{0,10},{2,8},{4,14},{6,12},{8,2},{10,0},{12,6},{14,4},{1,11},{3,9}... | collective-permute-start | bytes 258056 | tf_op jit(solution)/shard_map/ppermute | solution.py:103
  11.2 2.0 %collective-permute-start.3 = (bf16[168,256]{1,0:T(8,128)(2,1)}, bf16[168,256]{1,0:T(8,128)(2,1)S(1)}, u32[]{:S(2)}, u32[]{:S(2)}) collective-permute-start(bf16[168,256]{1,0:T(8,128)(2,1)} %get-tuple-element.17), channel_id=1, source_target_pairs={{0,8},{2,10},{4,12},{6,14},{8,0},{10,2},{12,4},{14,6},{1,9},{3,11}... | collective-permute-start | bytes 258056 | tf_op jit(solution)/shard_map/ppermute | solution.py:103
  13.2 0.0 copy-done
  13.2 0.0 copy-done.2
  13.2 0.0 copy-done.3
  13.2 0.0 copy-done.5
  13.2 1.9 %shard_map.78 = (bf16[168,256]{1,0:T(8,128)(2,1)S(1)}, bf16[168,256]{1,0:T(8,128)(2,1)S(1)}, bf16[168,256]{1,0:T(8,128)(2,1)S(1)}, bf16[168,256]{1,0:T(8,128)(2,1)S(1)}) custom-call(bf16[1,32,16,2,512]{4,3,2,1,0:T(2,128)(2,1)S(1)} %copy-done, f32[32,4,2,256]{3,2,1,0:T(2,128)S(1)} %copy-done.2, s32[8,5]{1,0:T(8,128)S(1)} %bitcast.3, ...), custom_call_target="tpu_custom_call" | custom-call | tf_op jit(solution)/shard_map/pallas_call | solution.py:78
  15.1 2.4 %collective-permute-start.4 = (bf16[168,256]{1,0:T(8,128)(2,1)S(1)}, bf16[168,256]{1,0:T(8,128)(2,1)S(1)}, u32[]{:S(2)}, u32[]{:S(2)}) collective-permute-start(bf16[168,256]{1,0:T(8,128)(2,1)S(1)} %get-tuple-element.20), channel_id=1, source_target_pairs={{0,6},{2,4},{4,2},{6,0},{8,14},{10,12},{12,10},{14,8},{1,7},{3,5},... | collective-permute-start | bytes 258056 | tf_op jit(solution)/shard_map/ppermute | solution.py:103
  17.5 0.0 collective-permute-done.refs_0_
  17.5 2.5 %collective-permute-start.5 = (bf16[168,256]{1,0:T(8,128)(2,1)S(1)}, bf16[168,256]{1,0:T(8,128)(2,1)S(1)}, u32[]{:S(2)}, u32[]{:S(2)}) collective-permute-start(bf16[168,256]{1,0:T(8,128)(2,1)S(1)} %get-tuple-element.21), channel_id=1, source_target_pairs={{0,4},{2,6},{4,0},{6,2},{8,12},{10,14},{12,8},{14,10},{1,5},{3,7},... | collective-permute-start | bytes 258056 | tf_op jit(solution)/shard_map/ppermute | solution.py:103
  20.0 0.0 collective-permute-done.1.refs_1_
  20.0 1.6 %collective-permute-start.6 = (bf16[168,256]{1,0:T(8,128)(2,1)S(1)}, bf16[168,256]{1,0:T(8,128)(2,1)S(1)}, u32[]{:S(2)}, u32[]{:S(2)}) collective-permute-start(bf16[168,256]{1,0:T(8,128)(2,1)S(1)} %get-tuple-element.22), channel_id=1, source_target_pairs={{0,2},{2,0},{4,6},{6,4},{8,10},{10,8},{12,14},{14,12},{1,3},{3,1},... | collective-permute-start | bytes 258056 | tf_op jit(solution)/shard_map/ppermute | solution.py:103
  21.6 2.5 %collective-permute-done.2.refs_2_ = bf16[168,256]{1,0:T(8,128)(2,1)S(1)} collective-permute-done((bf16[168,256]{1,0:T(8,128)(2,1)}, bf16[168,256]{1,0:T(8,128)(2,1)S(1)}, u32[]{:S(2)}, u32[]{:S(2)}) %collective-permute-start.2) | collective-permute-done | bytes 86048 | tf_op jit(solution)/shard_map/ppermute | solution.py:103
  24.1 1.0 %collective-permute-done.3.refs_3_ = bf16[168,256]{1,0:T(8,128)(2,1)S(1)} collective-permute-done((bf16[168,256]{1,0:T(8,128)(2,1)}, bf16[168,256]{1,0:T(8,128)(2,1)S(1)}, u32[]{:S(2)}, u32[]{:S(2)}) %collective-permute-start.3) | collective-permute-done | bytes 86048 | tf_op jit(solution)/shard_map/ppermute | solution.py:103
  25.1 0.0 collective-permute-done.4.refs_4_
  25.1 0.5 %collective-permute-done.5.refs_5_ = bf16[168,256]{1,0:T(8,128)(2,1)S(1)} collective-permute-done((bf16[168,256]{1,0:T(8,128)(2,1)S(1)}, bf16[168,256]{1,0:T(8,128)(2,1)S(1)}, u32[]{:S(2)}, u32[]{:S(2)}) %collective-permute-start.5) | collective-permute-done | bytes 86048 | tf_op jit(solution)/shard_map/ppermute | solution.py:103
  25.6 0.0 collective-permute-done.6.refs_6_
  25.6 0.0 copy-done.1
  25.6 0.0 copy-start.4
  25.6 3.1 %shard_map.79 = bf16[8,32,256]{2,1,0:T(8,128)(2,1)S(1)} custom-call(bf16[168,256]{1,0:T(8,128)(2,1)S(1)} %collective-permute-done.refs_0_, bf16[168,256]{1,0:T(8,128)(2,1)S(1)} %collective-permute-done.1.refs_1_, bf16[168,256]{1,0:T(8,128)(2,1)S(1)} %collective-permute-done.2.refs_2_, bf16[168,256]{1,0:T(8,128)(2,1)S(1)} %collective-permute-done.3.refs_3_, ...), custom_call_target="tpu_custom_call" | custom-call | tf_op jit(solution)/shard_map/pallas_call | solution.py:225
  28.7 11.8 %all_to_all.5.state_ref = bf16[8,32,256]{2,1,0:T(8,128)(2,1)S(1)} all-to-all(bf16[8,32,256]{2,1,0:T(8,128)(2,1)S(1)} %shard_map.79), channel_id=1, replica_groups=mesh['groups'=2,'gx'=4,'gy'=2,'ta'=2] {'gx','gy'}, dimensions={0} | all-to-all | bytes 262144 | tf_op jit(solution)/shard_map/all_to_all | solution.py:264
  40.5 0.0 copy-done.4
  40.5 1.0 %shard_map.80 = (bf16[32,4,2,512]{3,2,1,0:T(2,128)(2,1)}, f32[32,4,2,256]{3,2,1,0:T(2,128)}) custom-call(bf16[8,32,256]{2,1,0:T(8,128)(2,1)S(1)} %all_to_all.5.state_ref, bf16[512,512]{1,0:T(8,128)(2,1)S(1)} %copy-done.4), custom_call_target="tpu_custom_call" | custom-call | tf_op jit(solution)/shard_map/pallas_call | solution.py:245
Async XLA Ops:
  0.6 12.6 %copy-start = (bf16[1,32,16,2,512]{4,3,2,1,0:T(2,128)(2,1)S(1)}, bf16[1,32,16,2,512]{4,3,2,1,0:T(2,128)(2,1)}, u32[]{:S(2)}) copy-start(bf16[1,32,16,2,512]{4,3,2,1,0:T(2,128)(2,1)} %refs_0_.3) | copy-start | bytes 3145732
  0.6 12.6 %copy-start.2 = (f32[32,4,2,256]{3,2,1,0:T(2,128)S(1)}, f32[32,4,2,256]{3,2,1,0:T(2,128)}, u32[]{:S(2)}) copy-start(f32[32,4,2,256]{3,2,1,0:T(2,128)} %refs_1_.3) | copy-start | bytes 786436
  0.7 12.6 %copy-start.3 = (bf16[512,256]{1,0:T(8,128)(2,1)S(1)}, bf16[512,256]{1,0:T(8,128)(2,1)}, u32[]{:S(2)}) copy-start(bf16[512,256]{1,0:T(8,128)(2,1)} %refs_3_.3) | copy-start | bytes 786436
  0.7 12.6 %copy-start.5 = (s32[4,2,5]{2,1,0:T(2,128)S(1)}, s32[4,2,5]{2,1,0:T(2,128)}, u32[]{:S(2)}) copy-start(s32[4,2,5]{2,1,0:T(2,128)} %param.8) | copy-start | bytes 484
  4.2 21.4 %copy-start.1 = (bf16[8,256,256]{2,1,0:T(8,128)(2,1)S(1)}, bf16[8,256,256]{2,1,0:T(8,128)(2,1)}, u32[]{:S(2)}) copy-start(bf16[8,256,256]{2,1,0:T(8,128)(2,1)} %refs_8_.1) | copy-start | bytes 3145732
  4.2 13.3 %collective-permute-start = (bf16[168,256]{1,0:T(8,128)(2,1)}, bf16[168,256]{1,0:T(8,128)(2,1)S(1)}, u32[]{:S(2)}, u32[]{:S(2)}) collective-permute-start(bf16[168,256]{1,0:T(8,128)(2,1)} %get-tuple-element.14), channel_id=1, source_target_pairs={{0,14},{2,12},{4,10},{6,8},{8,6},{10,4},{12,2},{14,0},{1,15},{3,13... | collective-permute-start | bytes 258056 | tf_op jit(solution)/shard_map/ppermute | solution.py:103
  10.2 9.8 %collective-permute-start.1 = (bf16[168,256]{1,0:T(8,128)(2,1)}, bf16[168,256]{1,0:T(8,128)(2,1)S(1)}, u32[]{:S(2)}, u32[]{:S(2)}) collective-permute-start(bf16[168,256]{1,0:T(8,128)(2,1)} %get-tuple-element.15), channel_id=1, source_target_pairs={{0,12},{2,14},{4,8},{6,10},{8,4},{10,6},{12,0},{14,2},{1,13},{3,15... | collective-permute-start | bytes 258056 | tf_op jit(solution)/shard_map/ppermute | solution.py:103
  10.4 13.7 %collective-permute-start.2 = (bf16[168,256]{1,0:T(8,128)(2,1)}, bf16[168,256]{1,0:T(8,128)(2,1)S(1)}, u32[]{:S(2)}, u32[]{:S(2)}) collective-permute-start(bf16[168,256]{1,0:T(8,128)(2,1)} %get-tuple-element.16), channel_id=1, source_target_pairs={{0,10},{2,8},{4,14},{6,12},{8,2},{10,0},{12,6},{14,4},{1,11},{3,9}... | collective-permute-start | bytes 258056 | tf_op jit(solution)/shard_map/ppermute | solution.py:103
  11.2 13.9 %collective-permute-start.3 = (bf16[168,256]{1,0:T(8,128)(2,1)}, bf16[168,256]{1,0:T(8,128)(2,1)S(1)}, u32[]{:S(2)}, u32[]{:S(2)}) collective-permute-start(bf16[168,256]{1,0:T(8,128)(2,1)} %get-tuple-element.17), channel_id=1, source_target_pairs={{0,8},{2,10},{4,12},{6,14},{8,0},{10,2},{12,4},{14,6},{1,9},{3,11}... | collective-permute-start | bytes 258056 | tf_op jit(solution)/shard_map/ppermute | solution.py:103
  15.1 10.0 %collective-permute-start.4 = (bf16[168,256]{1,0:T(8,128)(2,1)S(1)}, bf16[168,256]{1,0:T(8,128)(2,1)S(1)}, u32[]{:S(2)}, u32[]{:S(2)}) collective-permute-start(bf16[168,256]{1,0:T(8,128)(2,1)S(1)} %get-tuple-element.20), channel_id=1, source_target_pairs={{0,6},{2,4},{4,2},{6,0},{8,14},{10,12},{12,10},{14,8},{1,7},{3,5},... | collective-permute-start | bytes 258056 | tf_op jit(solution)/shard_map/ppermute | solution.py:103
  17.5 8.1 %collective-permute-start.5 = (bf16[168,256]{1,0:T(8,128)(2,1)S(1)}, bf16[168,256]{1,0:T(8,128)(2,1)S(1)}, u32[]{:S(2)}, u32[]{:S(2)}) collective-permute-start(bf16[168,256]{1,0:T(8,128)(2,1)S(1)} %get-tuple-element.21), channel_id=1, source_target_pairs={{0,4},{2,6},{4,0},{6,2},{8,12},{10,14},{12,8},{14,10},{1,5},{3,7},... | collective-permute-start | bytes 258056 | tf_op jit(solution)/shard_map/ppermute | solution.py:103
  20.0 5.6 %collective-permute-start.6 = (bf16[168,256]{1,0:T(8,128)(2,1)S(1)}, bf16[168,256]{1,0:T(8,128)(2,1)S(1)}, u32[]{:S(2)}, u32[]{:S(2)}) collective-permute-start(bf16[168,256]{1,0:T(8,128)(2,1)S(1)} %get-tuple-element.22), channel_id=1, source_target_pairs={{0,2},{2,0},{4,6},{6,4},{8,10},{10,8},{12,14},{14,12},{1,3},{3,1},... | collective-permute-start | bytes 258056 | tf_op jit(solution)/shard_map/ppermute | solution.py:103
  25.6 14.9 %copy-start.4 = (bf16[512,512]{1,0:T(8,128)(2,1)S(1)}, bf16[512,512]{1,0:T(8,128)(2,1)}, u32[]{:S(2)}) copy-start(bf16[512,512]{1,0:T(8,128)(2,1)} %readout_ref.1) | copy-start | bytes 1572868

commit v4 on v3

--- a/solution.py
+++ b/solution.py
@@ -6,8 +6,7 @@
 from jax.sharding import PartitionSpec as P
 
 PLANE = ("gx", "gy")
-VMEM_LIMIT = 40 * 1024 * 1024
-WIDE_VMEM_LIMIT = 60 * 1024 * 1024
+VMEM_LIMIT = 24 * 1024 * 1024
 
 
 def whole(shape):
@@ -23,17 +22,16 @@
 
 
 def partners(peers):
-    return list(range(peers - 1, -1, -1))
-
-
-def inlet_kernel(peers, order, frames_hbm, start_hbm, index_ref, inlet_hbm, *refs):
-    packed_refs, (frames_ref, start_ref, inlet_ref, arrived) = refs[:-4], refs[-4:]
+    return sorted(range(peers), key=lambda k: (-k.bit_count(), -k))
+
+
+def inlet_kernel(order, frames_hbm, start_hbm, index_hbm, inlet_hbm, *refs):
+    count = len(order)
+    packed_refs, (frames_ref, start_ref, index_ref, inlet_ref, arrived) = refs[:count], refs[count:]
     units = inlet_ref.shape[1]
     place = place_in_plane()
     share = frames_ref.shape[1]
     entries = index_ref.shape[-1]
-    inlet_copy = pltpu.make_async_copy(inlet_hbm, inlet_ref, arrived.at[0, len(order)])
-    inlet_copy.start()
     cell_copies, state_copies = [], []
     for slot, k in enumerate(order):
         mine = pl.ds((place ^ k) * share, share)
@@ -43,10 +41,14 @@
         state_copies.append(
             pltpu.make_async_copy(start_hbm.at[mine], start_ref.at[slot], arrived.at[1, slot])
         )
-    for copy in cell_copies + state_copies:
+    inlet_copy = pltpu.make_async_copy(inlet_hbm, inlet_ref, arrived.at[0, count])
+    index_copy = pltpu.make_async_copy(index_hbm, index_ref, arrived.at[1, count])
+    inlet_copy.start()
+    for copy in cell_copies:
         copy.start()
-    index = index_ref[...].astype(jnp.bfloat16)
-    blank = jnp.zeros((index.shape[0], units), jnp.bfloat16)
+    index_copy.start()
+    for copy in state_copies:
+        copy.start()
     inlet_copy.wait()
     for slot, packed_ref in enumerate(packed_refs):
         cell_copies[slot].wait()
@@ -54,6 +56,10 @@
         drive = jnp.dot(cells, inlet_ref[...], preferred_element_type=jnp.float32)
         drive_rows = drive.shape[0]
         packed_ref[:drive_rows, :] = drive.astype(jnp.bfloat16)
+        if slot == 0:
+            index_copy.wait()
+            index = index_ref[...].astype(jnp.bfloat16)
+            blank = jnp.zeros((index.shape[0], units), jnp.bfloat16)
         state_copies[slot].wait()
         state = start_ref[slot].reshape(-1, units)
         after = drive_rows + state.shape[0]
@@ -62,7 +68,7 @@
         packed_ref[after:, :entries] = index
 
 
-def pack_for_peers(frames, start_state, tile_index, inlet_coupler, peers, order, vmem_limit):
+def pack_for_peers(frames, start_state, tile_index, inlet_coupler, peers, order):
     units = inlet_coupler.shape[1]
     blocks = tile_index.shape[0] * tile_index.shape[1]
     drive_rows = frames.size // frames.shape[-1] // peers
@@ -70,33 +76,37 @@
     index = tile_index.reshape(blocks, -1)
     out_shape = (drive_rows + state_rows + blocks, units)
     share = frames.shape[1] // peers
-    far = pl.BlockSpec(memory_space=pltpu.HBM)
+    count = len(order)
+    operands = [
+        pltpu.with_memory_space_constraint(v, pltpu.HBM)
+        for v in (frames, start_state, index, inlet_coupler)
+    ]
 
     def kernel(*refs):
-        inlet_kernel(peers, order, *refs)
+        inlet_kernel(order, *refs)
 
     return pl.pallas_call(
         kernel,
-        in_specs=[far, far, pl.BlockSpec(memory_space=pltpu.VMEM), far],
-        out_shape=[jax.ShapeDtypeStruct(out_shape, jnp.bfloat16)] * len(order),
+        in_specs=[pl.BlockSpec(memory_space=pltpu.HBM)] * len(operands),
+        out_specs=[pl.BlockSpec(memory_space=pltpu.VMEM)] * count,
+        out_shape=[pltpu.VMEM(out_shape, jnp.bfloat16)] * count,
         scratch_shapes=[
-            pltpu.VMEM((len(order), share) + frames.shape[2:], frames.dtype),
-            pltpu.VMEM((len(order), share) + start_state.shape[1:], start_state.dtype),
+            pltpu.VMEM((count, share) + frames.shape[2:], frames.dtype),
+            pltpu.VMEM((count, share) + start_state.shape[1:], start_state.dtype),
+            pltpu.VMEM(index.shape, index.dtype),
             pltpu.VMEM(inlet_coupler.shape, inlet_coupler.dtype),
-            pltpu.SemaphoreType.DMA((2, len(order) + 1)),
+            pltpu.SemaphoreType.DMA((2, count + 1)),
         ],
-        compiler_params=pltpu.CompilerParams(vmem_limit_bytes=vmem_limit),
-    )(frames, start_state, index, inlet_coupler)
+        compiler_params=pltpu.CompilerParams(vmem_limit_bytes=VMEM_LIMIT),
+    )(*operands)
 
 
 def exchange(frames, start_state, tile_index, inlet_coupler, peers):
     order = partners(peers)
-    half = peers // 2
+    first = 1
     got = []
-    for part, limit in ((order[:half], WIDE_VMEM_LIMIT), (order[half:], VMEM_LIMIT)):
-        packed = list(
-            pack_for_peers(frames, start_state, tile_index, inlet_coupler, peers, part, limit)
-        )
+    for part in (order[:first], order[first:]):
+        packed = list(pack_for_peers(frames, start_state, tile_index, inlet_coupler, peers, part))
         tile_index, packed[0] = lax.optimization_barrier((tile_index, packed[0]))
         for k, block in zip(part, packed):
             if k:

time: 41.7 us -> 38 us (0.911)
  starting transfers between devices: 15.6 us -> 12.8 us
  waiting for transfers between devices: 3.95 us -> 6.02 us
  Pallas kernels: 9.42 us -> 7.91 us
  blocking collectives: 11.8 us -> 10.4 us
    ppermute x7, starting transfers between devices: 15.6 us -> 12.8 us  [exchange(): block = lax.ppermute(block, PLANE, [(p, p ^ k) for p in range(peers)])]
    ppermute x7, waiting for transfers between devices: 3.95 us -> 6.02 us  [exchange(): block = lax.ppermute(block, PLANE, [(p, p ^ k) for p in range(peers)])]
    pallas_call x2, Pallas kernels: 5.35 us -> 3.9 us  [pack_for_peers(): pl.pallas_call(kernel, in_specs=[pl.BlockSpec(memory_space=pltpu.HBM)] *...]
    all_to_all x1, blocking collectives: 11.8 us -> 10.4 us  [by_trajectory(): state = lax.all_to_all(sent, PLANE, 0, 0, tiled=True)]
  transfers between devices with their start and end apart: 7 -> 7, of which waited for: 3 -> 4; matrix products, arithmetic and copies ran while one was open for 0% -> 0% of each run, Pallas kernels for 5% -> 7%
where the time goes in v4:
time: 38 us; the launch traced here: 37.9 us
  starting transfers between devices  12.8 us (34%)
  blocking collectives  10.4 us (27%)
  Pallas kernels  7.91 us (21%)
  waiting for transfers between devices  6.02 us (16%)
  between operations  0.68 us (2%)
    ppermute x7, starting transfers between devices, exchange(): block = lax.ppermute(block, PLANE, [(p, p ^ k) for p in range(peers)])  12.8 us
    all_to_all x1, blocking collectives, by_trajectory(): state = lax.all_to_all(sent, PLANE, 0, 0, tiled=True)  10.4 us
    ppermute x7, waiting for transfers between devices, exchange(): block = lax.ppermute(block, PLANE, [(p, p ^ k) for p in range(peers)])  6.02 us
    pallas_call x2, Pallas kernels, pack_for_peers(): pl.pallas_call(kernel, in_specs=[pl.BlockSpec(memory_space=pltpu.HBM)] *...  3.9 us
    pallas_call x1, Pallas kernels, run_steps(): pl.pallas_call(kernel, out_shape=jax.ShapeDtypeStruct((peers, home_rows,...  3 us
    pallas_call x1, Pallas kernels, read_out(): pl.pallas_call(readout_kernel, out_shape=(jax.ShapeDtypeStruct(block_shap...  1.01 us
  transfers between devices with their start and end apart: 7, of which 4 were waited for; matrix products, arithmetic and copies ran while one was open for 0% of the time, Pallas kernels for 7%

profile of v4, /device:TPU:0, one launch (start us, length us, event | category | flops | bytes accessed | tf_op | source)
XLA Modules:
  0.0 37.9 jit_solution(15505105053387512557)
XLA Ops:
  0.6 1.2 %shard_map.77 = bf16[168,256]{1,0:T(8,128)(2,1)S(1)} custom-call(bf16[1,32,16,2,512]{4,3,2,1,0:T(2,128)(2,1)} %refs_0_.3, f32[32,4,2,256]{3,2,1,0:T(2,128)} %refs_1_.3, s32[8,5]{1,0:T(8,128)} %bitcast.2, bf16[512,256]{1,0:T(8,128)(2,1)} %refs_3_.3), custom_call_target="tpu_custom_call" | custom-call | tf_op jit(solution)/shard_map/pallas_call | solution.py:88
  1.9 0.0 copy-start
  1.9 6.0 %collective-permute-start = (bf16[168,256]{1,0:T(8,128)(2,1)S(1)}, bf16[168,256]{1,0:T(8,128)(2,1)S(1)}, u32[]{:S(2)}, u32[]{:S(2)}) collective-permute-start(bf16[168,256]{1,0:T(8,128)(2,1)S(1)} %shard_map.77), channel_id=1, source_target_pairs={{0,14},{2,12},{4,10},{6,8},{8,6},{10,4},{12,2},{14,0},{1,15},{3,13... | collective-permute-start | bytes 258056 | tf_op jit(solution)/shard_map/ppermute | solution.py:113
  7.9 2.7 %shard_map.78 = (bf16[168,256]{1,0:T(8,128)(2,1)S(1)}, bf16[168,256]{1,0:T(8,128)(2,1)S(1)}, bf16[168,256]{1,0:T(8,128)(2,1)S(1)}, bf16[168,256]{1,0:T(8,128)(2,...) custom-call(bf16[1,32,16,2,512]{4,3,2,1,0:T(2,128)(2,1)} %refs_0_.3, ...), custom_call_target="tpu_custom_call" | custom-call | tf_op jit(solution)/shard_map/pallas_call | solution.py:88
  10.6 0.3 collective-permute-start.1
  10.9 0.8 %collective-permute-start.2 = (bf16[168,256]{1,0:T(8,128)(2,1)S(1)}, bf16[168,256]{1,0:T(8,128)(2,1)S(1)}, u32[]{:S(2)}, u32[]{:S(2)}) collective-permute-start(bf16[168,256]{1,0:T(8,128)(2,1)S(1)} %get-tuple-element.16), channel_id=1, source_target_pairs={{0,10},{2,8},{4,14},{6,12},{8,2},{10,0},{12,6},{14,4},{1,11},{3,9}... | collective-permute-start | bytes 258056 | tf_op jit(solution)/shard_map/ppermute | solution.py:113
  11.6 4.3 %collective-permute-start.3 = (bf16[168,256]{1,0:T(8,128)(2,1)S(1)}, bf16[168,256]{1,0:T(8,128)(2,1)S(1)}, u32[]{:S(2)}, u32[]{:S(2)}) collective-permute-start(bf16[168,256]{1,0:T(8,128)(2,1)S(1)} %get-tuple-element.17), channel_id=1, source_target_pairs={{0,6},{2,4},{4,2},{6,0},{8,14},{10,12},{12,10},{14,8},{1,7},{3,5},... | collective-permute-start | bytes 258056 | tf_op jit(solution)/shard_map/ppermute | solution.py:113
  15.9 0.0 collective-permute-start.4
  16.0 0.0 collective-permute-done.refs_0_
  16.0 0.8 %collective-permute-start.5 = (bf16[168,256]{1,0:T(8,128)(2,1)S(1)}, bf16[168,256]{1,0:T(8,128)(2,1)S(1)}, u32[]{:S(2)}, u32[]{:S(2)}) collective-permute-start(bf16[168,256]{1,0:T(8,128)(2,1)S(1)} %get-tuple-element.19), channel_id=1, source_target_pairs={{0,4},{2,6},{4,0},{6,2},{8,12},{10,14},{12,8},{14,10},{1,5},{3,7},... | collective-permute-start | bytes 258056 | tf_op jit(solution)/shard_map/ppermute | solution.py:113
  16.7 1.2 %collective-permute-done.1.refs_1_ = bf16[168,256]{1,0:T(8,128)(2,1)S(1)} collective-permute-done((bf16[168,256]{1,0:T(8,128)(2,1)S(1)}, bf16[168,256]{1,0:T(8,128)(2,1)S(1)}, u32[]{:S(2)}, u32[]{:S(2)}) %collective-permute-start.1) | collective-permute-done | bytes 86048 | tf_op jit(solution)/shard_map/ppermute | solution.py:113
  17.9 0.6 %collective-permute-start.6 = (bf16[168,256]{1,0:T(8,128)(2,1)S(1)}, bf16[168,256]{1,0:T(8,128)(2,1)S(1)}, u32[]{:S(2)}, u32[]{:S(2)}) collective-permute-start(bf16[168,256]{1,0:T(8,128)(2,1)S(1)} %get-tuple-element.20), channel_id=1, source_target_pairs={{0,2},{2,0},{4,6},{6,4},{8,10},{10,8},{12,14},{14,12},{1,3},{3,1},... | collective-permute-start | bytes 258056 | tf_op jit(solution)/shard_map/ppermute | solution.py:113
  18.6 2.7 %collective-permute-done.2.refs_2_ = bf16[168,256]{1,0:T(8,128)(2,1)S(1)} collective-permute-done((bf16[168,256]{1,0:T(8,128)(2,1)S(1)}, bf16[168,256]{1,0:T(8,128)(2,1)S(1)}, u32[]{:S(2)}, u32[]{:S(2)}) %collective-permute-start.2) | collective-permute-done | bytes 86048 | tf_op jit(solution)/shard_map/ppermute | solution.py:113
  21.3 0.5 %collective-permute-done.3.refs_3_ = bf16[168,256]{1,0:T(8,128)(2,1)S(1)} collective-permute-done((bf16[168,256]{1,0:T(8,128)(2,1)S(1)}, bf16[168,256]{1,0:T(8,128)(2,1)S(1)}, u32[]{:S(2)}, u32[]{:S(2)}) %collective-permute-start.3) | collective-permute-done | bytes 86048 | tf_op jit(solution)/shard_map/ppermute | solution.py:113
  21.8 1.6 %collective-permute-done.4.refs_4_ = bf16[168,256]{1,0:T(8,128)(2,1)S(1)} collective-permute-done((bf16[168,256]{1,0:T(8,128)(2,1)S(1)}, bf16[168,256]{1,0:T(8,128)(2,1)S(1)}, u32[]{:S(2)}, u32[]{:S(2)}) %collective-permute-start.4) | collective-permute-done | bytes 86048 | tf_op jit(solution)/shard_map/ppermute | solution.py:113
  23.4 0.0 collective-permute-done.5.refs_5_
  23.4 0.0 collective-permute-done.6.refs_6_
  23.4 0.0 copy-done
  23.4 0.0 copy-start.1
  23.4 3.0 %shard_map.79 = bf16[8,32,256]{2,1,0:T(8,128)(2,1)S(1)} custom-call(bf16[168,256]{1,0:T(8,128)(2,1)S(1)} %collective-permute-done.refs_0_, bf16[168,256]{1,0:T(8,128)(2,1)S(1)} %collective-permute-done.1.refs_1_, bf16[168,256]{1,0:T(8,128)(2,1)S(1)} %collective-permute-done.2.refs_2_, bf16[168,256]{1,0:T(8,128)(2,1)S(1)} %collective-permute-done.3.refs_3_, ...), custom_call_target="tpu_custom_call" | custom-call | tf_op jit(solution)/shard_map/pallas_call | solution.py:235
  26.4 10.4 %all_to_all.5.state_ref = bf16[8,32,256]{2,1,0:T(8,128)(2,1)S(1)} all-to-all(bf16[8,32,256]{2,1,0:T(8,128)(2,1)S(1)} %shard_map.79), channel_id=1, replica_groups=mesh['groups'=2,'gx'=4,'gy'=2,'ta'=2] {'gx','gy'}, dimensions={0} | all-to-all | bytes 262144 | tf_op jit(solution)/shard_map/all_to_all | solution.py:274
  36.8 0.0 copy-done.1
  36.8 1.0 %shard_map.80 = (bf16[32,4,2,512]{3,2,1,0:T(2,128)(2,1)}, f32[32,4,2,256]{3,2,1,0:T(2,128)}) custom-call(bf16[8,32,256]{2,1,0:T(8,128)(2,1)S(1)} %all_to_all.5.state_ref, bf16[512,512]{1,0:T(8,128)(2,1)S(1)} %copy-done.1), custom_call_target="tpu_custom_call" | custom-call | tf_op jit(solution)/shard_map/pallas_call | solution.py:255
Async XLA Ops:
  1.9 21.5 %copy-start = (bf16[8,256,256]{2,1,0:T(8,128)(2,1)S(1)}, bf16[8,256,256]{2,1,0:T(8,128)(2,1)}, u32[]{:S(2)}) copy-start(bf16[8,256,256]{2,1,0:T(8,128)(2,1)} %refs_8_.1) | copy-start | bytes 3145732
  1.9 14.1 %collective-permute-start = (bf16[168,256]{1,0:T(8,128)(2,1)S(1)}, bf16[168,256]{1,0:T(8,128)(2,1)S(1)}, u32[]{:S(2)}, u32[]{:S(2)}) collective-permute-start(bf16[168,256]{1,0:T(8,128)(2,1)S(1)} %shard_map.77), channel_id=1, source_target_pairs={{0,14},{2,12},{4,10},{6,8},{8,6},{10,4},{12,2},{14,0},{1,15},{3,13... | collective-permute-start | bytes 258056 | tf_op jit(solution)/shard_map/ppermute | solution.py:113
  10.6 7.3 %collective-permute-start.1 = (bf16[168,256]{1,0:T(8,128)(2,1)S(1)}, bf16[168,256]{1,0:T(8,128)(2,1)S(1)}, u32[]{:S(2)}, u32[]{:S(2)}) collective-permute-start(bf16[168,256]{1,0:T(8,128)(2,1)S(1)} %get-tuple-element.15), channel_id=1, source_target_pairs={{0,12},{2,14},{4,8},{6,10},{8,4},{10,6},{12,0},{14,2},{1,13},{3,15... | collective-permute-start | bytes 258056 | tf_op jit(solution)/shard_map/ppermute | solution.py:113
  10.9 10.4 %collective-permute-start.2 = (bf16[168,256]{1,0:T(8,128)(2,1)S(1)}, bf16[168,256]{1,0:T(8,128)(2,1)S(1)}, u32[]{:S(2)}, u32[]{:S(2)}) collective-permute-start(bf16[168,256]{1,0:T(8,128)(2,1)S(1)} %get-tuple-element.16), channel_id=1, source_target_pairs={{0,10},{2,8},{4,14},{6,12},{8,2},{10,0},{12,6},{14,4},{1,11},{3,9}... | collective-permute-start | bytes 258056 | tf_op jit(solution)/shard_map/ppermute | solution.py:113
  11.6 10.1 %collective-permute-start.3 = (bf16[168,256]{1,0:T(8,128)(2,1)S(1)}, bf16[168,256]{1,0:T(8,128)(2,1)S(1)}, u32[]{:S(2)}, u32[]{:S(2)}) collective-permute-start(bf16[168,256]{1,0:T(8,128)(2,1)S(1)} %get-tuple-element.17), channel_id=1, source_target_pairs={{0,6},{2,4},{4,2},{6,0},{8,14},{10,12},{12,10},{14,8},{1,7},{3,5},... | collective-permute-start | bytes 258056 | tf_op jit(solution)/shard_map/ppermute | solution.py:113
  15.9 7.4 %collective-permute-start.4 = (bf16[168,256]{1,0:T(8,128)(2,1)S(1)}, bf16[168,256]{1,0:T(8,128)(2,1)S(1)}, u32[]{:S(2)}, u32[]{:S(2)}) collective-permute-start(bf16[168,256]{1,0:T(8,128)(2,1)S(1)} %get-tuple-element.18), channel_id=1, source_target_pairs={{0,8},{2,10},{4,12},{6,14},{8,0},{10,2},{12,4},{14,6},{1,9},{3,11}... | collective-permute-start | bytes 258056 | tf_op jit(solution)/shard_map/ppermute | solution.py:113
  16.0 7.4 %collective-permute-start.5 = (bf16[168,256]{1,0:T(8,128)(2,1)S(1)}, bf16[168,256]{1,0:T(8,128)(2,1)S(1)}, u32[]{:S(2)}, u32[]{:S(2)}) collective-permute-start(bf16[168,256]{1,0:T(8,128)(2,1)S(1)} %get-tuple-element.19), channel_id=1, source_target_pairs={{0,4},{2,6},{4,0},{6,2},{8,12},{10,14},{12,8},{14,10},{1,5},{3,7},... | collective-permute-start | bytes 258056 | tf_op jit(solution)/shard_map/ppermute | solution.py:113
  17.9 5.5 %collective-permute-start.6 = (bf16[168,256]{1,0:T(8,128)(2,1)S(1)}, bf16[168,256]{1,0:T(8,128)(2,1)S(1)}, u32[]{:S(2)}, u32[]{:S(2)}) collective-permute-start(bf16[168,256]{1,0:T(8,128)(2,1)S(1)} %get-tuple-element.20), channel_id=1, source_target_pairs={{0,2},{2,0},{4,6},{6,4},{8,10},{10,8},{12,14},{14,12},{1,3},{3,1},... | collective-permute-start | bytes 258056 | tf_op jit(solution)/shard_map/ppermute | solution.py:113
  23.4 13.4 %copy-start.1 = (bf16[512,512]{1,0:T(8,128)(2,1)S(1)}, bf16[512,512]{1,0:T(8,128)(2,1)}, u32[]{:S(2)}) copy-start(bf16[512,512]{1,0:T(8,128)(2,1)} %readout_ref.1) | copy-start | bytes 1572868

commit v5 on v4

--- a/solution.py
+++ b/solution.py
@@ -103,9 +103,8 @@
 
 def exchange(frames, start_state, tile_index, inlet_coupler, peers):
     order = partners(peers)
-    first = 1
     got = []
-    for part in (order[:first], order[first:]):
+    for part in (order[:1], order[1:-1], order[-1:]):
         packed = list(pack_for_peers(frames, start_state, tile_index, inlet_coupler, peers, part))
         tile_index, packed[0] = lax.optimization_barrier((tile_index, packed[0]))
         for k, block in zip(part, packed):
@@ -149,7 +148,12 @@
                 ),
             ]
         )
-    return own, [[v - first_other for v in choices] for choices in other], low
+
+    def bits(choice):
+        choice = choice.astype(jnp.int32)
+        return [(choice >> bit) & 1 == 1 for bit in range(first_other.bit_length() - 1)]
+
+    return [bits(v) for v in own], [[bits(v - first_other) for v in c] for c in other], low
 
 
 def steps_kernel(count_x, count_y, torus_rows, *refs):
@@ -166,62 +170,61 @@
     groups = [(j, t) for j in range(count_y) for t in range(trajectories)]
 
     def choose(index, products):
-        chosen = products[-1]
-        for tile in range(halves - 2, -1, -1):
-            chosen = jnp.where(index == tile, products[tile], chosen)
-        return chosen
+        level = list(products)
+        for index_bit in index:
+            level = [
+                jnp.where(index_bit, odd, even) for even, odd in zip(level[::2], level[1::2])
+            ]
+        return level[0]
 
     own_index, other_index, low = neighbour_choices(
         packed_ref, drive_rows + state_rows, count_x, count_y, halves
     )
-    state = []
+    state = {}
     for j, t in groups:
+        pieces = []
         for i in range(count_x):
             piece = packed_ref[i * count_y + j, drive_rows : drive_rows + state_rows, :]
-            piece = piece.astype(jnp.float32)
-            state.append(piece[t * home_rows : (t + 1) * home_rows])
-    state = jnp.concatenate(state, axis=0)
+            pieces.append(piece.astype(jnp.float32)[t * home_rows : (t + 1) * home_rows])
+        state[j, t] = jnp.concatenate(pieces, axis=0)
+    parts = min(2, trajectories)
     for step in range(count_x):
-        state_half = state.astype(jnp.bfloat16)
-        products = [
-            jnp.dot(state_half, bank_ref[tile], preferred_element_type=jnp.float32)
-            for tile in range(2 * halves)
-        ]
-        kept, left, right = {}, {}, {}
-        for g, (j, t) in enumerate(groups):
-            span = slice(g * torus_rows, (g + 1) * torus_rows)
-            others = [product[span] for product in products[halves:]]
-            total = choose(own_index[j], [product[span] for product in products[:halves]])
-            total += pltpu.roll(choose(other_index[j][0], others), 2, axis=0)
-            total += pltpu.roll(choose(other_index[j][1], others), torus_rows - 2, axis=0)
-            kept[j, t] = total
-            left[j, t] = choose(other_index[j][2], others)
-            right[j, t] = choose(other_index[j][3], others)
-        fresh = []
-        for j, t in groups:
-            before, behind = (j - 1) % count_y, (j + 1) % count_y
-            total = kept[j, t]
-            total += jnp.where(
-                low,
-                pltpu.roll(left[before, t], torus_rows - 1, axis=0),
-                pltpu.roll(left[j, t], 1, axis=0),
-            )
-            total += jnp.where(
-                low,
-                pltpu.roll(right[j, t], torus_rows - 1, axis=0),
-                pltpu.roll(right[behind, t], 1, axis=0),
-            )
-            drive = packed_ref[
-                step * count_y + j, t * torus_rows : (t + 1) * torus_rows, :
-            ].astype(jnp.float32)
-            fresh.append(jnp.tanh(total + drive))
-        state = jnp.concatenate(fresh, axis=0)
+        for part in range(parts):
+            members = [(j, t) for j, t in groups if t % parts == part]
+            state_half = jnp.concatenate([state[g].astype(jnp.bfloat16) for g in members], axis=0)
+            products = [
+                jnp.dot(state_half, bank_ref[tile], preferred_element_type=jnp.float32)
+                for tile in range(2 * halves)
+            ]
+            kept, left, right = {}, {}, {}
+            for g, (j, t) in enumerate(members):
+                span = slice(g * torus_rows, (g + 1) * torus_rows)
+                others = [product[span] for product in products[halves:]]
+                total = choose(own_index[j], [product[span] for product in products[:halves]])
+                total += pltpu.roll(choose(other_index[j][0], others), 2, axis=0)
+                total += pltpu.roll(choose(other_index[j][1], others), torus_rows - 2, axis=0)
+                kept[j, t] = total
+                left[j, t] = choose(other_index[j][2], others)
+                right[j, t] = choose(other_index[j][3], others)
+            for j, t in members:
+                before, behind = (j - 1) % count_y, (j + 1) % count_y
+                crossing = jnp.where(
+                    low, left[j, t] + right[behind, t], left[before, t] + right[j, t]
+                )
+                total = kept[j, t] + jnp.where(
+                    low,
+                    pltpu.roll(crossing, torus_rows - 1, axis=0),
+                    pltpu.roll(crossing, 1, axis=0),
+                )
+                drive = packed_ref[
+                    step * count_y + j, t * torus_rows : (t + 1) * torus_rows, :
+                ].astype(jnp.float32)
+                state[j, t] = jnp.tanh(total + drive)
     for i in range(count_x):
         for j in range(count_y):
             pieces = []
             for t in range(trajectories):
-                base = (j * trajectories + t) * torus_rows + i * home_rows
-                pieces.append(state[base : base + home_rows])
+                pieces.append(state[j, t][i * home_rows : (i + 1) * home_rows])
             sent_ref[i * count_y + j] = jnp.concatenate(pieces, axis=0).astype(jnp.bfloat16)
 
 

time: 38 us -> 37.4 us (0.984)
  waiting for transfers between devices: 6.02 us -> 4.78 us
  Pallas kernels: 7.91 us -> 8.43 us
    ppermute x7, waiting for transfers between devices: 6.02 us -> 4.78 us  [exchange(): block = lax.ppermute(block, PLANE, [(p, p ^ k) for p in range(peers)])]
    pallas_call x2 -> x3, Pallas kernels: 3.9 us -> 4.9 us  [pack_for_peers(): pl.pallas_call(kernel, in_specs=[pl.BlockSpec(memory_space=pltpu.HBM)] *...]
    pallas_call x1, Pallas kernels: 3 us -> 2.52 us  [run_steps(): pl.pallas_call(kernel, out_shape=jax.ShapeDtypeStruct((peers, home_rows,...]
  transfers between devices with their start and end apart: 7 -> 7, of which waited for: 4 -> 4; matrix products, arithmetic and copies ran while one was open for 0% -> 0% of each run, Pallas kernels for 7% -> 10%
where the time goes in v5:
time: 37.4 us; the launch traced here: 37.2 us
  starting transfers between devices  12.8 us (34%)
  blocking collectives  10.4 us (28%)
  Pallas kernels  8.43 us (23%)
  waiting for transfers between devices  4.78 us (13%)
  between operations  0.69 us (2%)
    ppermute x7, starting transfers between devices, exchange(): block = lax.ppermute(block, PLANE, [(p, p ^ k) for p in range(peers)])  12.8 us
    all_to_all x1, blocking collectives, by_trajectory(): state = lax.all_to_all(sent, PLANE, 0, 0, tiled=True)  10.4 us
    pallas_call x3, Pallas kernels, pack_for_peers(): pl.pallas_call(kernel, in_specs=[pl.BlockSpec(memory_space=pltpu.HBM)] *...  4.9 us
    ppermute x7, waiting for transfers between devices, exchange(): block = lax.ppermute(block, PLANE, [(p, p ^ k) for p in range(peers)])  4.78 us
    pallas_call x1, Pallas kernels, run_steps(): pl.pallas_call(kernel, out_shape=jax.ShapeDtypeStruct((peers, home_rows,...  2.52 us
    pallas_call x1, Pallas kernels, read_out(): pl.pallas_call(readout_kernel, out_shape=(jax.ShapeDtypeStruct(block_shap...  1.01 us
  transfers between devices with their start and end apart: 7, of which 4 were waited for; matrix products, arithmetic and copies ran while one was open for 0% of the time, Pallas kernels for 10%

profile of v5, /device:TPU:0, one launch (start us, length us, event | category | flops | bytes accessed | tf_op | source)
XLA Modules:
  0.0 37.2 jit_solution(636942420609483060)
XLA Ops:
  0.6 1.2 %shard_map.77 = bf16[168,256]{1,0:T(8,128)(2,1)S(1)} custom-call(bf16[1,32,16,2,512]{4,3,2,1,0:T(2,128)(2,1)} %refs_0_.5, f32[32,4,2,256]{3,2,1,0:T(2,128)} %refs_1_.5, s32[8,5]{1,0:T(8,128)} %bitcast.3, bf16[512,256]{1,0:T(8,128)(2,1)} %refs_3_.5), custom_call_target="tpu_custom_call" | custom-call | tf_op jit(solution)/shard_map/pallas_call | solution.py:88
  1.9 6.0 %collective-permute-start = (bf16[168,256]{1,0:T(8,128)(2,1)S(1)}, bf16[168,256]{1,0:T(8,128)(2,1)S(1)}, u32[]{:S(2)}, u32[]{:S(2)}) collective-permute-start(bf16[168,256]{1,0:T(8,128)(2,1)S(1)} %shard_map.77), channel_id=1, source_target_pairs={{0,14},{2,12},{4,10},{6,8},{8,6},{10,4},{12,2},{14,0},{1,15},{3,13... | collective-permute-start | bytes 258056 | tf_op jit(solution)/shard_map/ppermute | solution.py:112
  7.9 2.5 %shard_map.78 = (bf16[168,256]{1,0:T(8,128)(2,1)S(1)}, bf16[168,256]{1,0:T(8,128)(2,1)S(1)}, bf16[168,256]{1,0:T(8,128)(2,1)S(1)}, bf16[168,256]{1,0:T(8,128)(2,...) custom-call(bf16[1,32,16,2,512]{4,3,2,1,0:T(2,128)(2,1)} %refs_0_.5, f32[32,4,2,256]{3,2,1,0:T(2,128)} %refs_1_.5, ...), custom_call_target="tpu_custom_call" | custom-call | tf_op jit(solution)/shard_map/pallas_call | solution.py:88
  10.4 0.0 copy-start
  10.4 0.3 collective-permute-start.1
  10.7 0.8 %collective-permute-start.2 = (bf16[168,256]{1,0:T(8,128)(2,1)S(1)}, bf16[168,256]{1,0:T(8,128)(2,1)S(1)}, u32[]{:S(2)}, u32[]{:S(2)}) collective-permute-start(bf16[168,256]{1,0:T(8,128)(2,1)S(1)} %get-tuple-element.17), channel_id=1, source_target_pairs={{0,10},{2,8},{4,14},{6,12},{8,2},{10,0},{12,6},{14,4},{1,11},{3,9}... | collective-permute-start | bytes 258056 | tf_op jit(solution)/shard_map/ppermute | solution.py:112
  11.4 4.3 %collective-permute-start.3 = (bf16[168,256]{1,0:T(8,128)(2,1)S(1)}, bf16[168,256]{1,0:T(8,128)(2,1)S(1)}, u32[]{:S(2)}, u32[]{:S(2)}) collective-permute-start(bf16[168,256]{1,0:T(8,128)(2,1)S(1)} %get-tuple-element.18), channel_id=1, source_target_pairs={{0,6},{2,4},{4,2},{6,0},{8,14},{10,12},{12,10},{14,8},{1,7},{3,5},... | collective-permute-start | bytes 258056 | tf_op jit(solution)/shard_map/ppermute | solution.py:112
  15.7 0.0 collective-permute-start.4
  15.7 0.0 collective-permute-done.refs_0_
  15.7 0.8 %collective-permute-start.5 = (bf16[168,256]{1,0:T(8,128)(2,1)S(1)}, bf16[168,256]{1,0:T(8,128)(2,1)S(1)}, u32[]{:S(2)}, u32[]{:S(2)}) collective-permute-start(bf16[168,256]{1,0:T(8,128)(2,1)S(1)} %get-tuple-element.20), channel_id=1, source_target_pairs={{0,4},{2,6},{4,0},{6,2},{8,12},{10,14},{12,8},{14,10},{1,5},{3,7},... | collective-permute-start | bytes 258056 | tf_op jit(solution)/shard_map/ppermute | solution.py:112
  16.5 1.2 %collective-permute-done.1.refs_1_ = bf16[168,256]{1,0:T(8,128)(2,1)S(1)} collective-permute-done((bf16[168,256]{1,0:T(8,128)(2,1)S(1)}, bf16[168,256]{1,0:T(8,128)(2,1)S(1)}, u32[]{:S(2)}, u32[]{:S(2)}) %collective-permute-start.1) | collective-permute-done | bytes 86048 | tf_op jit(solution)/shard_map/ppermute | solution.py:112
  17.7 0.6 %collective-permute-start.6 = (bf16[168,256]{1,0:T(8,128)(2,1)S(1)}, bf16[168,256]{1,0:T(8,128)(2,1)S(1)}, u32[]{:S(2)}, u32[]{:S(2)}) collective-permute-start(bf16[168,256]{1,0:T(8,128)(2,1)S(1)} %get-tuple-element.21), channel_id=1, source_target_pairs={{0,2},{2,0},{4,6},{6,4},{8,10},{10,8},{12,14},{14,12},{1,3},{3,1},... | collective-permute-start | bytes 258056 | tf_op jit(solution)/shard_map/ppermute | solution.py:112
  18.3 1.2 %shard_map.79.refs_7_ = bf16[168,256]{1,0:T(8,128)(2,1)S(1)} custom-call(bf16[1,32,16,2,512]{4,3,2,1,0:T(2,128)(2,1)} %refs_0_.5, f32[32,4,2,256]{3,2,1,0:T(2,128)} %refs_1_.5, s32[8,5]{1,0:T(8,128)} %bitcast.5, bf16[512,256]{1,0:T(8,128)(2,1)} %refs_3_.5), custom_call_target="tpu_custom_call" | custom-call | tf_op jit(solution)/shard_map/pallas_call | solution.py:88
  19.6 1.5 %collective-permute-done.2.refs_2_ = bf16[168,256]{1,0:T(8,128)(2,1)S(1)} collective-permute-done((bf16[168,256]{1,0:T(8,128)(2,1)S(1)}, bf16[168,256]{1,0:T(8,128)(2,1)S(1)}, u32[]{:S(2)}, u32[]{:S(2)}) %collective-permute-start.2) | collective-permute-done | bytes 86048 | tf_op jit(solution)/shard_map/ppermute | solution.py:112
  21.1 0.5 %collective-permute-done.3.refs_3_ = bf16[168,256]{1,0:T(8,128)(2,1)S(1)} collective-permute-done((bf16[168,256]{1,0:T(8,128)(2,1)S(1)}, bf16[168,256]{1,0:T(8,128)(2,1)S(1)}, u32[]{:S(2)}, u32[]{:S(2)}) %collective-permute-start.3) | collective-permute-done | bytes 86048 | tf_op jit(solution)/shard_map/ppermute | solution.py:112
  21.5 1.6 %collective-permute-done.4.refs_4_ = bf16[168,256]{1,0:T(8,128)(2,1)S(1)} collective-permute-done((bf16[168,256]{1,0:T(8,128)(2,1)S(1)}, bf16[168,256]{1,0:T(8,128)(2,1)S(1)}, u32[]{:S(2)}, u32[]{:S(2)}) %collective-permute-start.4) | collective-permute-done | bytes 86048 | tf_op jit(solution)/shard_map/ppermute | solution.py:112
  23.2 0.0 collective-permute-done.5.refs_5_
  23.2 0.0 collective-permute-done.6.refs_6_
  23.2 0.0 copy-done
  23.2 0.0 copy-start.1
  23.2 2.5 %shard_map.80 = bf16[8,32,256]{2,1,0:T(8,128)(2,1)S(1)} custom-call(bf16[168,256]{1,0:T(8,128)(2,1)S(1)} %collective-permute-done.refs_0_, bf16[168,256]{1,0:T(8,128)(2,1)S(1)} %collective-permute-done.1.refs_1_, bf16[168,256]{1,0:T(8,128)(2,1)S(1)} %collective-permute-done.2.refs_2_, bf16[168,256]{1,0:T(8,128)(2,1)S(1)} %collective-permute-done.3.refs_3_, ...), custom_call_target="tpu_custom_call" | custom-call | tf_op jit(solution)/shard_map/pallas_call | solution.py:238
  25.7 10.4 %all_to_all.5.state_ref = bf16[8,32,256]{2,1,0:T(8,128)(2,1)S(1)} all-to-all(bf16[8,32,256]{2,1,0:T(8,128)(2,1)S(1)} %shard_map.80), channel_id=1, replica_groups=mesh['groups'=2,'gx'=4,'gy'=2,'ta'=2] {'gx','gy'}, dimensions={0} | all-to-all | bytes 262144 | tf_op jit(solution)/shard_map/all_to_all | solution.py:277
  36.2 0.0 copy-done.1
  36.2 1.0 %shard_map.81 = (bf16[32,4,2,512]{3,2,1,0:T(2,128)(2,1)}, f32[32,4,2,256]{3,2,1,0:T(2,128)}) custom-call(bf16[8,32,256]{2,1,0:T(8,128)(2,1)S(1)} %all_to_all.5.state_ref, bf16[512,512]{1,0:T(8,128)(2,1)S(1)} %copy-done.1), custom_call_target="tpu_custom_call" | custom-call | tf_op jit(solution)/shard_map/pallas_call | solution.py:258
Async XLA Ops:
  1.9 13.9 %collective-permute-start = (bf16[168,256]{1,0:T(8,128)(2,1)S(1)}, bf16[168,256]{1,0:T(8,128)(2,1)S(1)}, u32[]{:S(2)}, u32[]{:S(2)}) collective-permute-start(bf16[168,256]{1,0:T(8,128)(2,1)S(1)} %shard_map.77), channel_id=1, source_target_pairs={{0,14},{2,12},{4,10},{6,8},{8,6},{10,4},{12,2},{14,0},{1,15},{3,13... | collective-permute-start | bytes 258056 | tf_op jit(solution)/shard_map/ppermute | solution.py:112
  10.4 12.8 %copy-start = (bf16[8,256,256]{2,1,0:T(8,128)(2,1)S(1)}, bf16[8,256,256]{2,1,0:T(8,128)(2,1)}, u32[]{:S(2)}) copy-start(bf16[8,256,256]{2,1,0:T(8,128)(2,1)} %refs_8_.1) | copy-start | bytes 3145732
  10.4 7.3 %collective-permute-start.1 = (bf16[168,256]{1,0:T(8,128)(2,1)S(1)}, bf16[168,256]{1,0:T(8,128)(2,1)S(1)}, u32[]{:S(2)}, u32[]{:S(2)}) collective-permute-start(bf16[168,256]{1,0:T(8,128)(2,1)S(1)} %get-tuple-element.16), channel_id=1, source_target_pairs={{0,12},{2,14},{4,8},{6,10},{8,4},{10,6},{12,0},{14,2},{1,13},{3,15... | collective-permute-start | bytes 258056 | tf_op jit(solution)/shard_map/ppermute | solution.py:112
  10.7 10.4 %collective-permute-start.2 = (bf16[168,256]{1,0:T(8,128)(2,1)S(1)}, bf16[168,256]{1,0:T(8,128)(2,1)S(1)}, u32[]{:S(2)}, u32[]{:S(2)}) collective-permute-start(bf16[168,256]{1,0:T(8,128)(2,1)S(1)} %get-tuple-element.17), channel_id=1, source_target_pairs={{0,10},{2,8},{4,14},{6,12},{8,2},{10,0},{12,6},{14,4},{1,11},{3,9}... | collective-permute-start | bytes 258056 | tf_op jit(solution)/shard_map/ppermute | solution.py:112
  11.4 10.1 %collective-permute-start.3 = (bf16[168,256]{1,0:T(8,128)(2,1)S(1)}, bf16[168,256]{1,0:T(8,128)(2,1)S(1)}, u32[]{:S(2)}, u32[]{:S(2)}) collective-permute-start(bf16[168,256]{1,0:T(8,128)(2,1)S(1)} %get-tuple-element.18), channel_id=1, source_target_pairs={{0,6},{2,4},{4,2},{6,0},{8,14},{10,12},{12,10},{14,8},{1,7},{3,5},... | collective-permute-start | bytes 258056 | tf_op jit(solution)/shard_map/ppermute | solution.py:112
  15.7 7.4 %collective-permute-start.4 = (bf16[168,256]{1,0:T(8,128)(2,1)S(1)}, bf16[168,256]{1,0:T(8,128)(2,1)S(1)}, u32[]{:S(2)}, u32[]{:S(2)}) collective-permute-start(bf16[168,256]{1,0:T(8,128)(2,1)S(1)} %get-tuple-element.19), channel_id=1, source_target_pairs={{0,8},{2,10},{4,12},{6,14},{8,0},{10,2},{12,4},{14,6},{1,9},{3,11}... | collective-permute-start | bytes 258056 | tf_op jit(solution)/shard_map/ppermute | solution.py:112
  15.7 7.4 %collective-permute-start.5 = (bf16[168,256]{1,0:T(8,128)(2,1)S(1)}, bf16[168,256]{1,0:T(8,128)(2,1)S(1)}, u32[]{:S(2)}, u32[]{:S(2)}) collective-permute-start(bf16[168,256]{1,0:T(8,128)(2,1)S(1)} %get-tuple-element.20), channel_id=1, source_target_pairs={{0,4},{2,6},{4,0},{6,2},{8,12},{10,14},{12,8},{14,10},{1,5},{3,7},... | collective-permute-start | bytes 258056 | tf_op jit(solution)/shard_map/ppermute | solution.py:112
  17.7 5.5 %collective-permute-start.6 = (bf16[168,256]{1,0:T(8,128)(2,1)S(1)}, bf16[168,256]{1,0:T(8,128)(2,1)S(1)}, u32[]{:S(2)}, u32[]{:S(2)}) collective-permute-start(bf16[168,256]{1,0:T(8,128)(2,1)S(1)} %get-tuple-element.21), channel_id=1, source_target_pairs={{0,2},{2,0},{4,6},{6,4},{8,10},{10,8},{12,14},{14,12},{1,3},{3,1},... | collective-permute-start | bytes 258056 | tf_op jit(solution)/shard_map/ppermute | solution.py:112
  23.2 13.0 %copy-start.1 = (bf16[512,512]{1,0:T(8,128)(2,1)S(1)}, bf16[512,512]{1,0:T(8,128)(2,1)}, u32[]{:S(2)}) copy-start(bf16[512,512]{1,0:T(8,128)(2,1)} %readout_ref.1) | copy-start | bytes 1572868

commit v6 on v5

--- a/solution.py
+++ b/solution.py
@@ -6,6 +6,7 @@
 from jax.sharding import PartitionSpec as P
 
 PLANE = ("gx", "gy")
+LANES = 128
 VMEM_LIMIT = 24 * 1024 * 1024
 
 
@@ -23,6 +24,25 @@
 
 def partners(peers):
     return sorted(range(peers), key=lambda k: (-k.bit_count(), -k))
+
+
+def return_flip(peers):
+    return peers // 2 + 1 if peers > 2 else 0
+
+
+def store_rows(ref, at, rows):
+    for piece in range(rows.shape[1] // LANES):
+        ref[at : at + rows.shape[0], :] = rows[:, piece * LANES : (piece + 1) * LANES]
+        at += rows.shape[0]
+    return at
+
+
+def load_rows(ref, block, at, first, count, rows, units):
+    pieces = []
+    for piece in range(units // LANES):
+        start = at + piece * rows + first
+        pieces.append(ref[block, start : start + count, :])
+    return jnp.concatenate(pieces, axis=1)
 
 
 def inlet_kernel(order, frames_hbm, start_hbm, index_hbm, inlet_hbm, *refs):
@@ -54,16 +74,14 @@
         cell_copies[slot].wait()
         cells = frames_ref[slot].reshape(-1, frames_ref.shape[-1])
         drive = jnp.dot(cells, inlet_ref[...], preferred_element_type=jnp.float32)
-        drive_rows = drive.shape[0]
-        packed_ref[:drive_rows, :] = drive.astype(jnp.bfloat16)
+        after = store_rows(packed_ref, 0, drive.astype(jnp.bfloat16))
         if slot == 0:
             index_copy.wait()
             index = index_ref[...].astype(jnp.bfloat16)
-            blank = jnp.zeros((index.shape[0], units), jnp.bfloat16)
+            blank = jnp.zeros((index.shape[0], packed_ref.shape[1]), jnp.bfloat16)
         state_copies[slot].wait()
         state = start_ref[slot].reshape(-1, units)
-        after = drive_rows + state.shape[0]
-        packed_ref[drive_rows:after, :] = state.astype(jnp.bfloat16)
+        after = store_rows(packed_ref, after, state.astype(jnp.bfloat16))
         packed_ref[after:, :] = blank
         packed_ref[after:, :entries] = index
 
@@ -74,7 +92,7 @@
     drive_rows = frames.size // frames.shape[-1] // peers
     state_rows = start_state.size // units // peers
     index = tile_index.reshape(blocks, -1)
-    out_shape = (drive_rows + state_rows + blocks, units)
+    out_shape = ((drive_rows + state_rows) * units // LANES + blocks, LANES)
     share = frames.shape[1] // peers
     count = len(order)
     operands = [
@@ -114,9 +132,7 @@
     return got
 
 
-def neighbour_choices(packed_ref, base, count_x, count_y, first_other):
-    units = packed_ref.shape[-1]
-
+def neighbour_choices(packed_ref, base, units, count_x, count_y, first_other):
     def entry(j, k):
         parts = []
         for i in range(count_x):
@@ -158,7 +174,7 @@
 
 def steps_kernel(count_x, count_y, torus_rows, *refs):
     got_refs, (bank_ref, sent_ref, packed_ref) = refs[:-3], refs[-3:]
-    peers, rows, units = packed_ref.shape
+    peers, units = packed_ref.shape[0], bank_ref.shape[-1]
     place = place_in_plane()
     for k, got_ref in zip(partners(peers), got_refs):
         packed_ref[place ^ k] = got_ref[...]
@@ -178,13 +194,15 @@
         return level[0]
 
     own_index, other_index, low = neighbour_choices(
-        packed_ref, drive_rows + state_rows, count_x, count_y, halves
+        packed_ref, (drive_rows + state_rows) * units // LANES, units, count_x, count_y, halves
     )
     state = {}
     for j, t in groups:
         pieces = []
         for i in range(count_x):
-            piece = packed_ref[i * count_y + j, drive_rows : drive_rows + state_rows, :]
+            piece = load_rows(
+                packed_ref, i * count_y + j, drive_rows * units // LANES, 0, state_rows, state_rows, units
+            )
             pieces.append(piece.astype(jnp.float32)[t * home_rows : (t + 1) * home_rows])
         state[j, t] = jnp.concatenate(pieces, axis=0)
     parts = min(2, trajectories)
@@ -216,21 +234,20 @@
                     pltpu.roll(crossing, torus_rows - 1, axis=0),
                     pltpu.roll(crossing, 1, axis=0),
                 )
-                drive = packed_ref[
-                    step * count_y + j, t * torus_rows : (t + 1) * torus_rows, :
-                ].astype(jnp.float32)
-                state[j, t] = jnp.tanh(total + drive)
+                drive = load_rows(
+                    packed_ref, step * count_y + j, 0, t * torus_rows, torus_rows, drive_rows, units
+                )
+                state[j, t] = jnp.tanh(total + drive.astype(jnp.float32))
     for i in range(count_x):
         for j in range(count_y):
             pieces = []
             for t in range(trajectories):
                 pieces.append(state[j, t][i * home_rows : (i + 1) * home_rows])
-            sent_ref[i * count_y + j] = jnp.concatenate(pieces, axis=0).astype(jnp.bfloat16)
+            sent_ref[(i * count_y + j) ^ return_flip(peers)] = jnp.concatenate(pieces, axis=0).astype(jnp.bfloat16)
 
 
 def run_steps(packed, tile_bank, count_x, count_y, torus_rows, home_rows):
-    peers = len(packed)
-    rows, units = packed[0].shape
+    peers, units = len(packed), tile_bank.shape[-1]
 
     def kernel(*refs):
         steps_kernel(count_x, count_y, torus_rows, *refs)
@@ -238,14 +255,15 @@
     return pl.pallas_call(
         kernel,
         out_shape=jax.ShapeDtypeStruct((peers, home_rows, units), jnp.bfloat16),
-        scratch_shapes=[pltpu.VMEM((peers, rows, units), jnp.bfloat16)],
+        scratch_shapes=[pltpu.VMEM((peers,) + packed[0].shape, jnp.bfloat16)],
         compiler_params=pltpu.CompilerParams(vmem_limit_bytes=VMEM_LIMIT),
     )(*packed, tile_bank)
 
 
 def readout_kernel(state_ref, readout_ref, field_ref, final_ref):
     units = state_ref.shape[-1]
-    half = state_ref[...].reshape(-1, units)
+    peers = state_ref.shape[0]
+    half = jnp.concatenate([state_ref[p ^ return_flip(peers)] for p in range(peers)], axis=0)
     final = half.astype(jnp.float32)
     squares = (final * final).astype(jnp.bfloat16)
     field = jnp.dot(half, readout_ref[:units], preferred_element_type=jnp.float32)
@@ -274,7 +292,8 @@
     torus_rows = frames.shape[2] * frames.shape[3]
     home_rows = start_state.size // units // peers
     sent = run_steps(packed, tile_bank, count_x, count_y, torus_rows, home_rows)
-    state = lax.all_to_all(sent, PLANE, 0, 0, tiled=True)
+    group = [p ^ return_flip(peers) for p in range(peers)]
+    state = lax.all_to_all(sent, PLANE, 0, 0, tiled=True, axis_index_groups=[group])
     return read_out(state, readout_operator, block_shape)
 
 

time: 37.4 us -> 35.4 us (0.947)
  blocking collectives: 10.4 us -> 8.63 us
    all_to_all x1, blocking collectives: 10.4 us -> 8.63 us  [by_trajectory(): lax.all_to_all(sent, PLANE, 0, 0, tiled=True, axis_index_groups=[group])]
where the time goes in v6:
time: 35.4 us; the launch traced here: 35.2 us
  starting transfers between devices  12.7 us (36%)
  blocking collectives  8.63 us (24%)
  Pallas kernels  8.45 us (24%)
  waiting for transfers between devices  4.69 us (13%)
  between operations  0.69 us (2%)
    ppermute x7, starting transfers between devices, exchange(): block = lax.ppermute(block, PLANE, [(p, p ^ k) for p in range(peers)])  12.7 us
    all_to_all x1, blocking collectives, by_trajectory(): lax.all_to_all(sent, PLANE, 0, 0, tiled=True, axis_index_groups=[group])  8.63 us
    pallas_call x3, Pallas kernels, pack_for_peers(): pl.pallas_call(kernel, in_specs=[pl.BlockSpec(memory_space=pltpu.HBM)] *...  4.9 us
    ppermute x7, waiting for transfers between devices, exchange(): block = lax.ppermute(block, PLANE, [(p, p ^ k) for p in range(peers)])  4.69 us
    pallas_call x1, Pallas kernels, run_steps(): pl.pallas_call(kernel, out_shape=jax.ShapeDtypeStruct((peers, home_rows,...  2.53 us
    pallas_call x1, Pallas kernels, read_out(): pl.pallas_call(readout_kernel, out_shape=(jax.ShapeDtypeStruct(block_shap...  1.01 us
  transfers between devices with their start and end apart: 7, of which 4 were waited for; matrix products, arithmetic and copies ran while one was open for 0% of the time, Pallas kernels for 10%

profile of v6, /device:TPU:0, one launch (start us, length us, event | category | flops | bytes accessed | tf_op | source)
XLA Modules:
  0.0 35.2 jit_solution(12658575708581891255)
XLA Ops:
  0.6 1.2 %shard_map.77 = bf16[328,128]{1,0:T(8,128)(2,1)S(1)} custom-call(bf16[1,32,16,2,512]{4,3,2,1,0:T(2,128)(2,1)} %refs_0_.5, f32[32,4,2,256]{3,2,1,0:T(2,128)} %refs_1_.5, s32[8,5]{1,0:T(8,128)} %bitcast.3, bf16[512,256]{1,0:T(8,128)(2,1)} %refs_3_.5), custom_call_target="tpu_custom_call" | custom-call | tf_op jit(solution)/shard_map/pallas_call | solution.py:106
  1.9 6.0 %collective-permute-start = (bf16[328,128]{1,0:T(8,128)(2,1)S(1)}, bf16[328,128]{1,0:T(8,128)(2,1)S(1)}, u32[]{:S(2)}, u32[]{:S(2)}) collective-permute-start(bf16[328,128]{1,0:T(8,128)(2,1)S(1)} %shard_map.77), channel_id=1, source_target_pairs={{0,14},{2,12},{4,10},{6,8},{8,6},{10,4},{12,2},{14,0},{1,15},{3,13... | collective-permute-start | bytes 251912 | tf_op jit(solution)/shard_map/ppermute | solution.py:130
  7.9 2.5 %shard_map.78 = (bf16[328,128]{1,0:T(8,128)(2,1)S(1)}, bf16[328,128]{1,0:T(8,128)(2,1)S(1)}, bf16[328,128]{1,0:T(8,128)(2,1)S(1)}, bf16[328,128]{1,0:T(8,128)(2,...) custom-call(bf16[1,32,16,2,512]{4,3,2,1,0:T(2,128)(2,1)} %refs_0_.5, f32[32,4,2,256]{3,2,1,0:T(2,128)} %refs_1_.5, ...), custom_call_target="tpu_custom_call" | custom-call | tf_op jit(solution)/shard_map/pallas_call | solution.py:106
  10.4 0.0 copy-start
  10.4 0.3 collective-permute-start.1
  10.7 0.8 %collective-permute-start.2 = (bf16[328,128]{1,0:T(8,128)(2,1)S(1)}, bf16[328,128]{1,0:T(8,128)(2,1)S(1)}, u32[]{:S(2)}, u32[]{:S(2)}) collective-permute-start(bf16[328,128]{1,0:T(8,128)(2,1)S(1)} %get-tuple-element.17), channel_id=1, source_target_pairs={{0,10},{2,8},{4,14},{6,12},{8,2},{10,0},{12,6},{14,4},{1,11},{3,9}... | collective-permute-start | bytes 251912 | tf_op jit(solution)/shard_map/ppermute | solution.py:130
  11.4 4.3 %collective-permute-start.3 = (bf16[328,128]{1,0:T(8,128)(2,1)S(1)}, bf16[328,128]{1,0:T(8,128)(2,1)S(1)}, u32[]{:S(2)}, u32[]{:S(2)}) collective-permute-start(bf16[328,128]{1,0:T(8,128)(2,1)S(1)} %get-tuple-element.18), channel_id=1, source_target_pairs={{0,6},{2,4},{4,2},{6,0},{8,14},{10,12},{12,10},{14,8},{1,7},{3,5},... | collective-permute-start | bytes 251912 | tf_op jit(solution)/shard_map/ppermute | solution.py:130
  15.7 0.0 collective-permute-start.4
  15.7 0.0 collective-permute-done.refs_0_
  15.7 0.8 %collective-permute-start.5 = (bf16[328,128]{1,0:T(8,128)(2,1)S(1)}, bf16[328,128]{1,0:T(8,128)(2,1)S(1)}, u32[]{:S(2)}, u32[]{:S(2)}) collective-permute-start(bf16[328,128]{1,0:T(8,128)(2,1)S(1)} %get-tuple-element.20), channel_id=1, source_target_pairs={{0,4},{2,6},{4,0},{6,2},{8,12},{10,14},{12,8},{14,10},{1,5},{3,7},... | collective-permute-start | bytes 251912 | tf_op jit(solution)/shard_map/ppermute | solution.py:130
  16.5 1.2 %collective-permute-done.1.refs_1_ = bf16[328,128]{1,0:T(8,128)(2,1)S(1)} collective-permute-done((bf16[328,128]{1,0:T(8,128)(2,1)S(1)}, bf16[328,128]{1,0:T(8,128)(2,1)S(1)}, u32[]{:S(2)}, u32[]{:S(2)}) %collective-permute-start.1) | collective-permute-done | bytes 84000 | tf_op jit(solution)/shard_map/ppermute | solution.py:130
  17.7 0.5 %collective-permute-start.6 = (bf16[328,128]{1,0:T(8,128)(2,1)S(1)}, bf16[328,128]{1,0:T(8,128)(2,1)S(1)}, u32[]{:S(2)}, u32[]{:S(2)}) collective-permute-start(bf16[328,128]{1,0:T(8,128)(2,1)S(1)} %get-tuple-element.21), channel_id=1, source_target_pairs={{0,2},{2,0},{4,6},{6,4},{8,10},{10,8},{12,14},{14,12},{1,3},{3,1},... | collective-permute-start | bytes 251912 | tf_op jit(solution)/shard_map/ppermute | solution.py:130
  18.3 1.2 %shard_map.79.refs_7_ = bf16[328,128]{1,0:T(8,128)(2,1)S(1)} custom-call(bf16[1,32,16,2,512]{4,3,2,1,0:T(2,128)(2,1)} %refs_0_.5, f32[32,4,2,256]{3,2,1,0:T(2,128)} %refs_1_.5, s32[8,5]{1,0:T(8,128)} %bitcast.5, bf16[512,256]{1,0:T(8,128)(2,1)} %refs_3_.5), custom_call_target="tpu_custom_call" | custom-call | tf_op jit(solution)/shard_map/pallas_call | solution.py:106
  19.5 1.4 %collective-permute-done.2.refs_2_ = bf16[328,128]{1,0:T(8,128)(2,1)S(1)} collective-permute-done((bf16[328,128]{1,0:T(8,128)(2,1)S(1)}, bf16[328,128]{1,0:T(8,128)(2,1)S(1)}, u32[]{:S(2)}, u32[]{:S(2)}) %collective-permute-start.2) | collective-permute-done | bytes 84000 | tf_op jit(solution)/shard_map/ppermute | solution.py:130
  20.9 0.5 %collective-permute-done.3.refs_3_ = bf16[328,128]{1,0:T(8,128)(2,1)S(1)} collective-permute-done((bf16[328,128]{1,0:T(8,128)(2,1)S(1)}, bf16[328,128]{1,0:T(8,128)(2,1)S(1)}, u32[]{:S(2)}, u32[]{:S(2)}) %collective-permute-start.3) | collective-permute-done | bytes 84000 | tf_op jit(solution)/shard_map/ppermute | solution.py:130
  21.4 1.6 %collective-permute-done.4.refs_4_ = bf16[328,128]{1,0:T(8,128)(2,1)S(1)} collective-permute-done((bf16[328,128]{1,0:T(8,128)(2,1)S(1)}, bf16[328,128]{1,0:T(8,128)(2,1)S(1)}, u32[]{:S(2)}, u32[]{:S(2)}) %collective-permute-start.4) | collective-permute-done | bytes 84000 | tf_op jit(solution)/shard_map/ppermute | solution.py:130
  23.0 0.0 collective-permute-done.5.refs_5_
  23.0 0.0 collective-permute-done.6.refs_6_
  23.0 0.0 copy-done
  23.0 0.0 copy-start.1
  23.0 2.5 %shard_map.80 = bf16[8,32,256]{2,1,0:T(8,128)(2,1)S(1)} custom-call(bf16[328,128]{1,0:T(8,128)(2,1)S(1)} %collective-permute-done.refs_0_, bf16[328,128]{1,0:T(8,128)(2,1)S(1)} %collective-permute-done.1.refs_1_, bf16[328,128]{1,0:T(8,128)(2,1)S(1)} %collective-permute-done.2.refs_2_, bf16[328,128]{1,0:T(8,128)(2,1)S(1)} %collective-permute-done.3.refs_3_, ...), custom_call_target="tpu_custom_call" | custom-call | tf_op jit(solution)/shard_map/pallas_call | solution.py:255
  25.5 8.6 %all_to_all.5.state_ref = bf16[8,32,256]{2,1,0:T(8,128)(2,1)S(1)} all-to-all(bf16[8,32,256]{2,1,0:T(8,128)(2,1)S(1)} %shard_map.80), channel_id=1, replica_groups={{10,8,14,12,2,0,6,4},{11,9,15,13,3,1,7,5},{26,24,30,28,18,16,22,20},{27..., dimensions={0} | all-to-all | bytes 262144 | tf_op jit(solution)/shard_map/all_to_all | solution.py:296
  34.2 0.0 copy-done.1
  34.2 1.0 %shard_map.81 = (bf16[32,4,2,512]{3,2,1,0:T(2,128)(2,1)}, f32[32,4,2,256]{3,2,1,0:T(2,128)}) custom-call(bf16[8,32,256]{2,1,0:T(8,128)(2,1)S(1)} %all_to_all.5.state_ref, bf16[512,512]{1,0:T(8,128)(2,1)S(1)} %copy-done.1), custom_call_target="tpu_custom_call" | custom-call | tf_op jit(solution)/shard_map/pallas_call | solution.py:276
Async XLA Ops:
  1.9 13.9 %collective-permute-start = (bf16[328,128]{1,0:T(8,128)(2,1)S(1)}, bf16[328,128]{1,0:T(8,128)(2,1)S(1)}, u32[]{:S(2)}, u32[]{:S(2)}) collective-permute-start(bf16[328,128]{1,0:T(8,128)(2,1)S(1)} %shard_map.77), channel_id=1, source_target_pairs={{0,14},{2,12},{4,10},{6,8},{8,6},{10,4},{12,2},{14,0},{1,15},{3,13... | collective-permute-start | bytes 251912 | tf_op jit(solution)/shard_map/ppermute | solution.py:130
  10.4 12.6 %copy-start = (bf16[8,256,256]{2,1,0:T(8,128)(2,1)S(1)}, bf16[8,256,256]{2,1,0:T(8,128)(2,1)}, u32[]{:S(2)}) copy-start(bf16[8,256,256]{2,1,0:T(8,128)(2,1)} %refs_8_.1) | copy-start | bytes 3145732
  10.4 7.4 %collective-permute-start.1 = (bf16[328,128]{1,0:T(8,128)(2,1)S(1)}, bf16[328,128]{1,0:T(8,128)(2,1)S(1)}, u32[]{:S(2)}, u32[]{:S(2)}) collective-permute-start(bf16[328,128]{1,0:T(8,128)(2,1)S(1)} %get-tuple-element.16), channel_id=1, source_target_pairs={{0,12},{2,14},{4,8},{6,10},{8,4},{10,6},{12,0},{14,2},{1,13},{3,15... | collective-permute-start | bytes 251912 | tf_op jit(solution)/shard_map/ppermute | solution.py:130
  10.7 10.2 %collective-permute-start.2 = (bf16[328,128]{1,0:T(8,128)(2,1)S(1)}, bf16[328,128]{1,0:T(8,128)(2,1)S(1)}, u32[]{:S(2)}, u32[]{:S(2)}) collective-permute-start(bf16[328,128]{1,0:T(8,128)(2,1)S(1)} %get-tuple-element.17), channel_id=1, source_target_pairs={{0,10},{2,8},{4,14},{6,12},{8,2},{10,0},{12,6},{14,4},{1,11},{3,9}... | collective-permute-start | bytes 251912 | tf_op jit(solution)/shard_map/ppermute | solution.py:130
  11.4 10.0 %collective-permute-start.3 = (bf16[328,128]{1,0:T(8,128)(2,1)S(1)}, bf16[328,128]{1,0:T(8,128)(2,1)S(1)}, u32[]{:S(2)}, u32[]{:S(2)}) collective-permute-start(bf16[328,128]{1,0:T(8,128)(2,1)S(1)} %get-tuple-element.18), channel_id=1, source_target_pairs={{0,6},{2,4},{4,2},{6,0},{8,14},{10,12},{12,10},{14,8},{1,7},{3,5},... | collective-permute-start | bytes 251912 | tf_op jit(solution)/shard_map/ppermute | solution.py:130
  15.7 7.2 %collective-permute-start.4 = (bf16[328,128]{1,0:T(8,128)(2,1)S(1)}, bf16[328,128]{1,0:T(8,128)(2,1)S(1)}, u32[]{:S(2)}, u32[]{:S(2)}) collective-permute-start(bf16[328,128]{1,0:T(8,128)(2,1)S(1)} %get-tuple-element.19), channel_id=1, source_target_pairs={{0,8},{2,10},{4,12},{6,14},{8,0},{10,2},{12,4},{14,6},{1,9},{3,11}... | collective-permute-start | bytes 251912 | tf_op jit(solution)/shard_map/ppermute | solution.py:130
  15.7 7.2 %collective-permute-start.5 = (bf16[328,128]{1,0:T(8,128)(2,1)S(1)}, bf16[328,128]{1,0:T(8,128)(2,1)S(1)}, u32[]{:S(2)}, u32[]{:S(2)}) collective-permute-start(bf16[328,128]{1,0:T(8,128)(2,1)S(1)} %get-tuple-element.20), channel_id=1, source_target_pairs={{0,4},{2,6},{4,0},{6,2},{8,12},{10,14},{12,8},{14,10},{1,5},{3,7},... | collective-permute-start | bytes 251912 | tf_op jit(solution)/shard_map/ppermute | solution.py:130
  17.7 5.2 %collective-permute-start.6 = (bf16[328,128]{1,0:T(8,128)(2,1)S(1)}, bf16[328,128]{1,0:T(8,128)(2,1)S(1)}, u32[]{:S(2)}, u32[]{:S(2)}) collective-permute-start(bf16[328,128]{1,0:T(8,128)(2,1)S(1)} %get-tuple-element.21), channel_id=1, source_target_pairs={{0,2},{2,0},{4,6},{6,4},{8,10},{10,8},{12,14},{14,12},{1,3},{3,1},... | collective-permute-start | bytes 251912 | tf_op jit(solution)/shard_map/ppermute | solution.py:130
  23.0 11.2 %copy-start.1 = (bf16[512,512]{1,0:T(8,128)(2,1)S(1)}, bf16[512,512]{1,0:T(8,128)(2,1)}, u32[]{:S(2)}) copy-start(bf16[512,512]{1,0:T(8,128)(2,1)} %readout_ref.1) | copy-start | bytes 1572868

commit v7 on v6

--- a/solution.py
+++ b/solution.py
@@ -23,7 +23,8 @@
 
 
 def partners(peers):
-    return sorted(range(peers), key=lambda k: (-k.bit_count(), -k))
+    served = (6, 7, 2, 5, 3, 4, 1)
+    return sorted(range(1, peers), key=lambda k: served.index(k) if k in served else k) + [0]
 
 
 def return_flip(peers):
@@ -132,12 +133,12 @@
     return got
 
 
-def neighbour_choices(packed_ref, base, units, count_x, count_y, first_other):
+def neighbour_choices(packed_ref, base, count_x, count_y, first_other):
     def entry(j, k):
         parts = []
         for i in range(count_x):
             rows = packed_ref[i * count_y + j, base:, :].astype(jnp.float32)
-            parts.append(jnp.broadcast_to(rows[:, k : k + 1], (rows.shape[0], units)))
+            parts.append(jnp.broadcast_to(rows[:, k : k + 1], (rows.shape[0], LANES)))
         return jnp.concatenate(parts, axis=0)
 
     columns = range(count_y)
@@ -169,7 +170,8 @@
         choice = choice.astype(jnp.int32)
         return [(choice >> bit) & 1 == 1 for bit in range(first_other.bit_length() - 1)]
 
-    return [bits(v) for v in own], [[bits(v - first_other) for v in c] for c in other], low
+    shares = [[(v == tile).astype(jnp.bfloat16) for tile in range(first_other)] for v in own]
+    return shares, [[bits(v - first_other) for v in c] for c in other]
 
 
 def steps_kernel(count_x, count_y, torus_rows, *refs):
@@ -186,15 +188,23 @@
     groups = [(j, t) for j in range(count_y) for t in range(trajectories)]
 
     def choose(index, products):
-        level = list(products)
-        for index_bit in index:
-            level = [
-                jnp.where(index_bit, odd, even) for even, odd in zip(level[::2], level[1::2])
-            ]
-        return level[0]
-
-    own_index, other_index, low = neighbour_choices(
-        packed_ref, (drive_rows + state_rows) * units // LANES, units, count_x, count_y, halves
+        chosen = []
+        for piece in range(units // LANES):
+            level = [product[:, piece * LANES : (piece + 1) * LANES] for product in products]
+            for index_bit in index:
+                level = [
+                    jnp.where(index_bit, odd, even) for even, odd in zip(level[::2], level[1::2])
+                ]
+            chosen.append(level[0])
+        return jnp.concatenate(chosen, axis=1)
+
+    low = lax.broadcasted_iota(jnp.int32, (torus_rows, units), 0) % 2 == 0
+
+    def share_of(rows, share):
+        return rows.astype(jnp.bfloat16) * jnp.concatenate([share] * (units // LANES), axis=1)
+
+    own_share, other_index = neighbour_choices(
+        packed_ref, (drive_rows + state_rows) * units // LANES, count_x, count_y, halves
     )
     state = {}
     for j, t in groups:
@@ -210,15 +220,24 @@
         for part in range(parts):
             members = [(j, t) for j, t in groups if t % parts == part]
             state_half = jnp.concatenate([state[g].astype(jnp.bfloat16) for g in members], axis=0)
+            masked = [
+                jnp.concatenate([share_of(state[j, t], own_share[j][tile]) for j, t in members], axis=0)
+                for tile in range(halves)
+            ]
+            own = jnp.dot(
+                jnp.concatenate(masked, axis=1),
+                bank_ref[:halves].reshape(halves * units, units),
+                preferred_element_type=jnp.float32,
+            )
             products = [
-                jnp.dot(state_half, bank_ref[tile], preferred_element_type=jnp.float32)
-                for tile in range(2 * halves)
+                jnp.dot(state_half, bank_ref[halves + tile], preferred_element_type=jnp.float32)
+                for tile in range(halves)
             ]
             kept, left, right = {}, {}, {}
             for g, (j, t) in enumerate(members):
                 span = slice(g * torus_rows, (g + 1) * torus_rows)
-                others = [product[span] for product in products[halves:]]
-                total = choose(own_index[j], [product[span] for product in products[:halves]])
+                others = [product[span] for product in products]
+                total = own[span]
                 total += pltpu.roll(choose(other_index[j][0], others), 2, axis=0)
                 total += pltpu.roll(choose(other_index[j][1], others), torus_rows - 2, axis=0)
                 kept[j, t] = total
@@ -368,12 +387,14 @@
         P(),
         P(),
     )
-    def shards(frames, start_state, *rest):
+    def shards(frames, start_state, tile_index, tile_bank, *rest):
         peers = mesh.shape["gx"] * mesh.shape["gy"]
-        fits = start_state.shape[0] % peers == 0 and peers & (peers - 1) == 0 and start_state.shape[2] == 2
-        fits = fits and start_state.shape[1] % 4 == 0
+        halves = tile_bank.shape[0] // 2
+        fits = all(v & (v - 1) == 0 for v in (peers, halves))
+        fits = fits and start_state.shape[0] % peers == 0 and start_state.shape[1] % 4 == 0
+        fits = fits and start_state.shape[2] == 2 and start_state.shape[3] % LANES == 0
         body = by_trajectory if fits and frames.shape[0] == 1 else by_block
-        return body(frames, start_state, *rest)
+        return body(frames, start_state, tile_index, tile_bank, *rest)
 
     return jax.shard_map(
         shards,

time: 35.4 us -> 34.6 us (0.977)
  waiting for transfers between devices: 4.69 us -> 3.29 us
  starting transfers between devices: 12.7 us -> 13.7 us
    ppermute x7, waiting for transfers between devices: 4.69 us -> 3.29 us  [exchange(): block = lax.ppermute(block, PLANE, [(p, p ^ k) for p in range(peers)])]
    ppermute x7, starting transfers between devices: 12.7 us -> 13.7 us  [exchange(): block = lax.ppermute(block, PLANE, [(p, p ^ k) for p in range(peers)])]
  transfers between devices with their start and end apart: 7 -> 7, of which waited for: 4 -> 3; matrix products, arithmetic and copies ran while one was open for 0% -> 0% of each run, Pallas kernels for 10% -> 11%
where the time goes in v7:
time: 34.6 us; the launch traced here: 34.4 us
  starting transfers between devices  13.7 us (40%)
  blocking collectives  8.63 us (25%)
  Pallas kernels  8.14 us (24%)
  waiting for transfers between devices  3.29 us (10%)
  between operations  0.69 us (2%)
    ppermute x7, starting transfers between devices, exchange(): block = lax.ppermute(block, PLANE, [(p, p ^ k) for p in range(peers)])  13.7 us
    all_to_all x1, blocking collectives, by_trajectory(): lax.all_to_all(sent, PLANE, 0, 0, tiled=True, axis_index_groups=[group])  8.63 us
    pallas_call x3, Pallas kernels, pack_for_peers(): pl.pallas_call(kernel, in_specs=[pl.BlockSpec(memory_space=pltpu.HBM)] *...  4.9 us
    ppermute x7, waiting for transfers between devices, exchange(): block = lax.ppermute(block, PLANE, [(p, p ^ k) for p in range(peers)])  3.29 us
    pallas_call x1, Pallas kernels, run_steps(): pl.pallas_call(kernel, out_shape=jax.ShapeDtypeStruct((peers, home_rows,...  2.23 us
    pallas_call x1, Pallas kernels, read_out(): pl.pallas_call(readout_kernel, out_shape=(jax.ShapeDtypeStruct(block_shap...  1.01 us
  transfers between devices with their start and end apart: 7, of which 3 were waited for; matrix products, arithmetic and copies ran while one was open for 0% of the time, Pallas kernels for 11%

profile of v7, /device:TPU:0, one launch (start us, length us, event | category | flops | bytes accessed | tf_op | source)
XLA Modules:
  0.0 34.4 jit_solution(11742479660937711961)
XLA Ops:
  0.6 1.2 %shard_map.77 = bf16[328,128]{1,0:T(8,128)(2,1)S(1)} custom-call(bf16[1,32,16,2,512]{4,3,2,1,0:T(2,128)(2,1)} %refs_0_.5, f32[32,4,2,256]{3,2,1,0:T(2,128)} %refs_1_.5, s32[8,5]{1,0:T(8,128)} %bitcast.3, bf16[512,256]{1,0:T(8,128)(2,1)} %refs_3_.5), custom_call_target="tpu_custom_call" | custom-call | tf_op jit(solution)/shard_map/pallas_call | solution.py:107
  1.9 5.1 %collective-permute-start = (bf16[328,128]{1,0:T(8,128)(2,1)S(1)}, bf16[328,128]{1,0:T(8,128)(2,1)S(1)}, u32[]{:S(2)}, u32[]{:S(2)}) collective-permute-start(bf16[328,128]{1,0:T(8,128)(2,1)S(1)} %shard_map.77), channel_id=1, source_target_pairs={{0,12},{2,14},{4,8},{6,10},{8,4},{10,6},{12,0},{14,2},{1,13},{3,15... | collective-permute-start | bytes 251912 | tf_op jit(solution)/shard_map/ppermute | solution.py:131
  7.0 2.5 %shard_map.78 = (bf16[328,128]{1,0:T(8,128)(2,1)S(1)}, bf16[328,128]{1,0:T(8,128)(2,1)S(1)}, bf16[328,128]{1,0:T(8,128)(2,1)S(1)}, bf16[328,128]{1,0:T(8,128)(2,...) custom-call(bf16[1,32,16,2,512]{4,3,2,1,0:T(2,128)(2,1)} %refs_0_.5, f32[32,4,2,256]{3,2,1,0:T(2,128)} %refs_1_.5, ...), custom_call_target="tpu_custom_call" | custom-call | tf_op jit(solution)/shard_map/pallas_call | solution.py:107
  9.4 0.0 copy-start
  9.5 1.2 %collective-permute-start.1 = (bf16[328,128]{1,0:T(8,128)(2,1)S(1)}, bf16[328,128]{1,0:T(8,128)(2,1)S(1)}, u32[]{:S(2)}, u32[]{:S(2)}) collective-permute-start(bf16[328,128]{1,0:T(8,128)(2,1)S(1)} %get-tuple-element.16), channel_id=1, source_target_pairs={{0,14},{2,12},{4,10},{6,8},{8,6},{10,4},{12,2},{14,0},{1,15},{3,13... | collective-permute-start | bytes 251912 | tf_op jit(solution)/shard_map/ppermute | solution.py:131
  10.7 0.0 collective-permute-start.2
  10.7 4.1 %collective-permute-start.3 = (bf16[328,128]{1,0:T(8,128)(2,1)S(1)}, bf16[328,128]{1,0:T(8,128)(2,1)S(1)}, u32[]{:S(2)}, u32[]{:S(2)}) collective-permute-start(bf16[328,128]{1,0:T(8,128)(2,1)S(1)} %get-tuple-element.18), channel_id=1, source_target_pairs={{0,10},{2,8},{4,14},{6,12},{8,2},{10,0},{12,6},{14,4},{1,11},{3,9}... | collective-permute-start | bytes 251912 | tf_op jit(solution)/shard_map/ppermute | solution.py:131
  14.8 0.9 %collective-permute-start.4 = (bf16[328,128]{1,0:T(8,128)(2,1)S(1)}, bf16[328,128]{1,0:T(8,128)(2,1)S(1)}, u32[]{:S(2)}, u32[]{:S(2)}) collective-permute-start(bf16[328,128]{1,0:T(8,128)(2,1)S(1)} %get-tuple-element.19), channel_id=1, source_target_pairs={{0,6},{2,4},{4,2},{6,0},{8,14},{10,12},{12,10},{14,8},{1,7},{3,5},... | collective-permute-start | bytes 251912 | tf_op jit(solution)/shard_map/ppermute | solution.py:131
  15.7 0.0 collective-permute-done.refs_0_
  15.7 0.8 %collective-permute-start.5 = (bf16[328,128]{1,0:T(8,128)(2,1)S(1)}, bf16[328,128]{1,0:T(8,128)(2,1)S(1)}, u32[]{:S(2)}, u32[]{:S(2)}) collective-permute-start(bf16[328,128]{1,0:T(8,128)(2,1)S(1)} %get-tuple-element.20), channel_id=1, source_target_pairs={{0,8},{2,10},{4,12},{6,14},{8,0},{10,2},{12,4},{14,6},{1,9},{3,11}... | collective-permute-start | bytes 251912 | tf_op jit(solution)/shard_map/ppermute | solution.py:131
  16.5 1.2 %collective-permute-done.1.refs_1_ = bf16[328,128]{1,0:T(8,128)(2,1)S(1)} collective-permute-done((bf16[328,128]{1,0:T(8,128)(2,1)S(1)}, bf16[328,128]{1,0:T(8,128)(2,1)S(1)}, u32[]{:S(2)}, u32[]{:S(2)}) %collective-permute-start.1) | collective-permute-done | bytes 84000 | tf_op jit(solution)/shard_map/ppermute | solution.py:131
  17.7 1.5 %collective-permute-start.6 = (bf16[328,128]{1,0:T(8,128)(2,1)S(1)}, bf16[328,128]{1,0:T(8,128)(2,1)S(1)}, u32[]{:S(2)}, u32[]{:S(2)}) collective-permute-start(bf16[328,128]{1,0:T(8,128)(2,1)S(1)} %get-tuple-element.21), channel_id=1, source_target_pairs={{0,2},{2,0},{4,6},{6,4},{8,10},{10,8},{12,14},{14,12},{1,3},{3,1},... | collective-permute-start | bytes 251912 | tf_op jit(solution)/shard_map/ppermute | solution.py:131
  19.2 1.2 %shard_map.79.refs_7_ = bf16[328,128]{1,0:T(8,128)(2,1)S(1)} custom-call(bf16[1,32,16,2,512]{4,3,2,1,0:T(2,128)(2,1)} %refs_0_.5, f32[32,4,2,256]{3,2,1,0:T(2,128)} %refs_1_.5, s32[8,5]{1,0:T(8,128)} %bitcast.5, bf16[512,256]{1,0:T(8,128)(2,1)} %refs_3_.5), custom_call_target="tpu_custom_call" | custom-call | tf_op jit(solution)/shard_map/pallas_call | solution.py:107
  20.4 0.0 collective-permute-done.2.refs_2_
  20.5 0.0 collective-permute-done.3.refs_3_
  20.5 0.9 %collective-permute-done.4.refs_4_ = bf16[328,128]{1,0:T(8,128)(2,1)S(1)} collective-permute-done((bf16[328,128]{1,0:T(8,128)(2,1)S(1)}, bf16[328,128]{1,0:T(8,128)(2,1)S(1)}, u32[]{:S(2)}, u32[]{:S(2)}) %collective-permute-start.4) | collective-permute-done | bytes 84000 | tf_op jit(solution)/shard_map/ppermute | solution.py:131
  21.4 1.1 %collective-permute-done.5.refs_5_ = bf16[328,128]{1,0:T(8,128)(2,1)S(1)} collective-permute-done((bf16[328,128]{1,0:T(8,128)(2,1)S(1)}, bf16[328,128]{1,0:T(8,128)(2,1)S(1)}, u32[]{:S(2)}, u32[]{:S(2)}) %collective-permute-start.5) | collective-permute-done | bytes 84000 | tf_op jit(solution)/shard_map/ppermute | solution.py:131
  22.5 0.0 collective-permute-done.6.refs_6_
  22.5 0.0 copy-done
  22.5 0.0 copy-start.1
  22.5 2.2 %shard_map.80 = bf16[8,32,256]{2,1,0:T(8,128)(2,1)S(1)} custom-call(bf16[328,128]{1,0:T(8,128)(2,1)S(1)} %collective-permute-done.refs_0_, bf16[328,128]{1,0:T(8,128)(2,1)S(1)} %collective-permute-done.1.refs_1_, bf16[328,128]{1,0:T(8,128)(2,1)S(1)} %collective-permute-done.2.refs_2_, bf16[328,128]{1,0:T(8,128)(2,1)S(1)} %collective-permute-done.3.refs_3_, ...), custom_call_target="tpu_custom_call" | custom-call | tf_op jit(solution)/shard_map/pallas_call | solution.py:274
  24.8 8.6 %all_to_all.5.state_ref = bf16[8,32,256]{2,1,0:T(8,128)(2,1)S(1)} all-to-all(bf16[8,32,256]{2,1,0:T(8,128)(2,1)S(1)} %shard_map.80), channel_id=1, replica_groups={{10,8,14,12,2,0,6,4},{11,9,15,13,3,1,7,5},{26,24,30,28,18,16,22,20},{27..., dimensions={0} | all-to-all | bytes 262144 | tf_op jit(solution)/shard_map/all_to_all | solution.py:315
  33.4 0.0 copy-done.1
  33.4 1.0 %shard_map.81 = (bf16[32,4,2,512]{3,2,1,0:T(2,128)(2,1)}, f32[32,4,2,256]{3,2,1,0:T(2,128)}) custom-call(bf16[8,32,256]{2,1,0:T(8,128)(2,1)S(1)} %all_to_all.5.state_ref, bf16[512,512]{1,0:T(8,128)(2,1)S(1)} %copy-done.1), custom_call_target="tpu_custom_call" | custom-call | tf_op jit(solution)/shard_map/pallas_call | solution.py:295
Async XLA Ops:
  1.9 13.9 %collective-permute-start = (bf16[328,128]{1,0:T(8,128)(2,1)S(1)}, bf16[328,128]{1,0:T(8,128)(2,1)S(1)}, u32[]{:S(2)}, u32[]{:S(2)}) collective-permute-start(bf16[328,128]{1,0:T(8,128)(2,1)S(1)} %shard_map.77), channel_id=1, source_target_pairs={{0,12},{2,14},{4,8},{6,10},{8,4},{10,6},{12,0},{14,2},{1,13},{3,15... | collective-permute-start | bytes 251912 | tf_op jit(solution)/shard_map/ppermute | solution.py:131
  9.4 13.1 %copy-start = (bf16[8,256,256]{2,1,0:T(8,128)(2,1)S(1)}, bf16[8,256,256]{2,1,0:T(8,128)(2,1)}, u32[]{:S(2)}) copy-start(bf16[8,256,256]{2,1,0:T(8,128)(2,1)} %refs_8_.1) | copy-start | bytes 3145732
  9.5 8.3 %collective-permute-start.1 = (bf16[328,128]{1,0:T(8,128)(2,1)S(1)}, bf16[328,128]{1,0:T(8,128)(2,1)S(1)}, u32[]{:S(2)}, u32[]{:S(2)}) collective-permute-start(bf16[328,128]{1,0:T(8,128)(2,1)S(1)} %get-tuple-element.16), channel_id=1, source_target_pairs={{0,14},{2,12},{4,10},{6,8},{8,6},{10,4},{12,2},{14,0},{1,15},{3,13... | collective-permute-start | bytes 251912 | tf_op jit(solution)/shard_map/ppermute | solution.py:131
  10.7 9.8 %collective-permute-start.2 = (bf16[328,128]{1,0:T(8,128)(2,1)S(1)}, bf16[328,128]{1,0:T(8,128)(2,1)S(1)}, u32[]{:S(2)}, u32[]{:S(2)}) collective-permute-start(bf16[328,128]{1,0:T(8,128)(2,1)S(1)} %get-tuple-element.17), channel_id=1, source_target_pairs={{0,4},{2,6},{4,0},{6,2},{8,12},{10,14},{12,8},{14,10},{1,5},{3,7},... | collective-permute-start | bytes 251912 | tf_op jit(solution)/shard_map/ppermute | solution.py:131
  10.7 9.8 %collective-permute-start.3 = (bf16[328,128]{1,0:T(8,128)(2,1)S(1)}, bf16[328,128]{1,0:T(8,128)(2,1)S(1)}, u32[]{:S(2)}, u32[]{:S(2)}) collective-permute-start(bf16[328,128]{1,0:T(8,128)(2,1)S(1)} %get-tuple-element.18), channel_id=1, source_target_pairs={{0,10},{2,8},{4,14},{6,12},{8,2},{10,0},{12,6},{14,4},{1,11},{3,9}... | collective-permute-start | bytes 251912 | tf_op jit(solution)/shard_map/ppermute | solution.py:131
  14.8 6.6 %collective-permute-start.4 = (bf16[328,128]{1,0:T(8,128)(2,1)S(1)}, bf16[328,128]{1,0:T(8,128)(2,1)S(1)}, u32[]{:S(2)}, u32[]{:S(2)}) collective-permute-start(bf16[328,128]{1,0:T(8,128)(2,1)S(1)} %get-tuple-element.19), channel_id=1, source_target_pairs={{0,6},{2,4},{4,2},{6,0},{8,14},{10,12},{12,10},{14,8},{1,7},{3,5},... | collective-permute-start | bytes 251912 | tf_op jit(solution)/shard_map/ppermute | solution.py:131
  15.7 6.8 %collective-permute-start.5 = (bf16[328,128]{1,0:T(8,128)(2,1)S(1)}, bf16[328,128]{1,0:T(8,128)(2,1)S(1)}, u32[]{:S(2)}, u32[]{:S(2)}) collective-permute-start(bf16[328,128]{1,0:T(8,128)(2,1)S(1)} %get-tuple-element.20), channel_id=1, source_target_pairs={{0,8},{2,10},{4,12},{6,14},{8,0},{10,2},{12,4},{14,6},{1,9},{3,11}... | collective-permute-start | bytes 251912 | tf_op jit(solution)/shard_map/ppermute | solution.py:131
  17.7 4.8 %collective-permute-start.6 = (bf16[328,128]{1,0:T(8,128)(2,1)S(1)}, bf16[328,128]{1,0:T(8,128)(2,1)S(1)}, u32[]{:S(2)}, u32[]{:S(2)}) collective-permute-start(bf16[328,128]{1,0:T(8,128)(2,1)S(1)} %get-tuple-element.21), channel_id=1, source_target_pairs={{0,2},{2,0},{4,6},{6,4},{8,10},{10,8},{12,14},{14,12},{1,3},{3,1},... | collective-permute-start | bytes 251912 | tf_op jit(solution)/shard_map/ppermute | solution.py:131
  22.5 10.9 %copy-start.1 = (bf16[512,512]{1,0:T(8,128)(2,1)S(1)}, bf16[512,512]{1,0:T(8,128)(2,1)}, u32[]{:S(2)}) copy-start(bf16[512,512]{1,0:T(8,128)(2,1)} %readout_ref.1) | copy-start | bytes 1572868

commit v8 on v7

--- a/solution.py
+++ b/solution.py
@@ -123,7 +123,7 @@
 def exchange(frames, start_state, tile_index, inlet_coupler, peers):
     order = partners(peers)
     got = []
-    for part in (order[:1], order[1:-1], order[-1:]):
+    for part in (order[:2], order[2:-1], order[-1:]):
         packed = list(pack_for_peers(frames, start_state, tile_index, inlet_coupler, peers, part))
         tile_index, packed[0] = lax.optimization_barrier((tile_index, packed[0]))
         for k, block in zip(part, packed):

time: 34.6 us -> 34.3 us (level)
  starting transfers between devices: 13.7 us -> 12.6 us
  blocking collectives: 8.63 us -> 9.32 us
    ppermute x7, starting transfers between devices: 13.7 us -> 12.6 us  [exchange(): block = lax.ppermute(block, PLANE, [(p, p ^ k) for p in range(peers)])]
    all_to_all x1, blocking collectives: 8.63 us -> 9.32 us  [by_trajectory(): lax.all_to_all(sent, PLANE, 0, 0, tiled=True, axis_index_groups=[group])]
  transfers between devices with their start and end apart: 7 -> 7, of which waited for: 3 -> 2; matrix products, arithmetic and copies ran while one was open for 0% -> 0% of each run, Pallas kernels for 11% -> 10%
where the time goes in v8:
time: 34.3 us; the launch traced here: 34.1 us
  starting transfers between devices  12.6 us (37%)
  blocking collectives  9.32 us (27%)
  Pallas kernels  8.14 us (24%)
  waiting for transfers between devices  3.39 us (10%)
  between operations  0.69 us (2%)
    ppermute x7, starting transfers between devices, exchange(): block = lax.ppermute(block, PLANE, [(p, p ^ k) for p in range(peers)])  12.6 us
    all_to_all x1, blocking collectives, by_trajectory(): lax.all_to_all(sent, PLANE, 0, 0, tiled=True, axis_index_groups=[group])  9.32 us
    pallas_call x3, Pallas kernels, pack_for_peers(): pl.pallas_call(kernel, in_specs=[pl.BlockSpec(memory_space=pltpu.HBM)] *...  4.9 us
    ppermute x7, waiting for transfers between devices, exchange(): block = lax.ppermute(block, PLANE, [(p, p ^ k) for p in range(peers)])  3.39 us
    pallas_call x1, Pallas kernels, run_steps(): pl.pallas_call(kernel, out_shape=jax.ShapeDtypeStruct((peers, home_rows,...  2.22 us
    pallas_call x1, Pallas kernels, read_out(): pl.pallas_call(readout_kernel, out_shape=(jax.ShapeDtypeStruct(block_shap...  1.01 us
  transfers between devices with their start and end apart: 7, of which 2 were waited for; matrix products, arithmetic and copies ran while one was open for 0% of the time, Pallas kernels for 10%

profile of v8, /device:TPU:0, one launch (start us, length us, event | category | flops | bytes accessed | tf_op | source)
XLA Modules:
  0.0 34.1 jit_solution(899388577139260057)
XLA Ops:
  0.6 1.5 %shard_map.77 = (bf16[328,128]{1,0:T(8,128)(2,1)S(1)}, bf16[328,128]{1,0:T(8,128)(2,1)S(1)}) custom-call(bf16[1,32,16,2,512]{4,3,2,1,0:T(2,128)(2,1)} %refs_0_.5, f32[32,4,2,256]{3,2,1,0:T(2,128)} %refs_1_.5, s32[8,5]{1,0:T(8,128)} %bitcast.3, bf16[512,256]{1,0:T(8,128)(2,1)} %refs_3_.5), custom_call_target="tpu_custom_call" | custom-call | tf_op jit(solution)/shard_map/pallas_call | solution.py:107
  2.1 5.1 %collective-permute-start = (bf16[328,128]{1,0:T(8,128)(2,1)S(1)}, bf16[328,128]{1,0:T(8,128)(2,1)S(1)}, u32[]{:S(2)}, u32[]{:S(2)}) collective-permute-start(bf16[328,128]{1,0:T(8,128)(2,1)S(1)} %get-tuple-element.15), channel_id=1, source_target_pairs={{0,12},{2,14},{4,8},{6,10},{8,4},{10,6},{12,0},{14,2},{1,13},{3,15... | collective-permute-start | bytes 251912 | tf_op jit(solution)/shard_map/ppermute | solution.py:131
  7.2 1.1 %collective-permute-start.1 = (bf16[328,128]{1,0:T(8,128)(2,1)S(1)}, bf16[328,128]{1,0:T(8,128)(2,1)S(1)}, u32[]{:S(2)}, u32[]{:S(2)}) collective-permute-start(bf16[328,128]{1,0:T(8,128)(2,1)S(1)} %get-tuple-element.16), channel_id=1, source_target_pairs={{0,14},{2,12},{4,10},{6,8},{8,6},{10,4},{12,2},{14,0},{1,15},{3,13... | collective-permute-start | bytes 251912 | tf_op jit(solution)/shard_map/ppermute | solution.py:131
  8.4 2.2 %shard_map.78 = (bf16[328,128]{1,0:T(8,128)(2,1)S(1)}, bf16[328,128]{1,0:T(8,128)(2,1)S(1)}, bf16[328,128]{1,0:T(8,128)(2,1)S(1)}, bf16[328,128]{1,0:T(8,128)(2,1)S(1)}, bf16[328,128]{1,0:T(8,128)(2,1)S(1)}) custom-call(bf16[1,32,16,2,512]{4,3,2,1,0:T(2,128)(2,1)} %refs_0_.5, f32[32,4,2,256]{3,2,1,0:T(2,128)} %refs_1_.5, s32[8,5]{1,0:T(8,128)} %bitcast.4, ...), custom_call_target="tpu_custom_call" | custom-call | tf_op jit(solution)/shard_map/pallas_call | solution.py:107
  10.6 0.0 copy-start
  10.6 0.1 collective-permute-start.2
  10.7 4.1 %collective-permute-start.3 = (bf16[328,128]{1,0:T(8,128)(2,1)S(1)}, bf16[328,128]{1,0:T(8,128)(2,1)S(1)}, u32[]{:S(2)}, u32[]{:S(2)}) collective-permute-start(bf16[328,128]{1,0:T(8,128)(2,1)S(1)} %get-tuple-element.20), channel_id=1, source_target_pairs={{0,10},{2,8},{4,14},{6,12},{8,2},{10,0},{12,6},{14,4},{1,11},{3,9}... | collective-permute-start | bytes 251912 | tf_op jit(solution)/shard_map/ppermute | solution.py:131
  14.8 1.0 %collective-permute-start.4 = (bf16[328,128]{1,0:T(8,128)(2,1)S(1)}, bf16[328,128]{1,0:T(8,128)(2,1)S(1)}, u32[]{:S(2)}, u32[]{:S(2)}) collective-permute-start(bf16[328,128]{1,0:T(8,128)(2,1)S(1)} %get-tuple-element.21), channel_id=1, source_target_pairs={{0,6},{2,4},{4,2},{6,0},{8,14},{10,12},{12,10},{14,8},{1,7},{3,5},... | collective-permute-start | bytes 251912 | tf_op jit(solution)/shard_map/ppermute | solution.py:131
  15.8 0.0 collective-permute-done.refs_0_
  15.8 0.7 %collective-permute-start.5 = (bf16[328,128]{1,0:T(8,128)(2,1)S(1)}, bf16[328,128]{1,0:T(8,128)(2,1)S(1)}, u32[]{:S(2)}, u32[]{:S(2)}) collective-permute-start(bf16[328,128]{1,0:T(8,128)(2,1)S(1)} %get-tuple-element.22), channel_id=1, source_target_pairs={{0,8},{2,10},{4,12},{6,14},{8,0},{10,2},{12,4},{14,6},{1,9},{3,11}... | collective-permute-start | bytes 251912 | tf_op jit(solution)/shard_map/ppermute | solution.py:131
  16.5 0.0 collective-permute-done.1.refs_1_
  16.5 0.4 %collective-permute-start.6 = (bf16[328,128]{1,0:T(8,128)(2,1)S(1)}, bf16[328,128]{1,0:T(8,128)(2,1)S(1)}, u32[]{:S(2)}, u32[]{:S(2)}) collective-permute-start(bf16[328,128]{1,0:T(8,128)(2,1)S(1)} %get-tuple-element.23), channel_id=1, source_target_pairs={{0,2},{2,0},{4,6},{6,4},{8,10},{10,8},{12,14},{14,12},{1,3},{3,1},... | collective-permute-start | bytes 251912 | tf_op jit(solution)/shard_map/ppermute | solution.py:131
  16.9 1.2 %shard_map.79.refs_7_ = bf16[328,128]{1,0:T(8,128)(2,1)S(1)} custom-call(bf16[1,32,16,2,512]{4,3,2,1,0:T(2,128)(2,1)} %refs_0_.5, f32[32,4,2,256]{3,2,1,0:T(2,128)} %refs_1_.5, s32[8,5]{1,0:T(8,128)} %bitcast.5, bf16[512,256]{1,0:T(8,128)(2,1)} %refs_3_.5), custom_call_target="tpu_custom_call" | custom-call | tf_op jit(solution)/shard_map/pallas_call | solution.py:107
  18.1 0.0 collective-permute-done.2.refs_2_
  18.2 0.2 collective-permute-done.3.refs_3_
  18.4 3.2 %collective-permute-done.4.refs_4_ = bf16[328,128]{1,0:T(8,128)(2,1)S(1)} collective-permute-done((bf16[328,128]{1,0:T(8,128)(2,1)S(1)}, bf16[328,128]{1,0:T(8,128)(2,1)S(1)}, u32[]{:S(2)}, u32[]{:S(2)}) %collective-permute-start.4) | collective-permute-done | bytes 84000 | tf_op jit(solution)/shard_map/ppermute | solution.py:131
  21.5 0.0 collective-permute-done.5.refs_5_
  21.5 0.0 collective-permute-done.6.refs_6_
  21.5 0.0 copy-done
  21.5 0.0 copy-start.1
  21.5 2.2 %shard_map.80 = bf16[8,32,256]{2,1,0:T(8,128)(2,1)S(1)} custom-call(bf16[328,128]{1,0:T(8,128)(2,1)S(1)} %collective-permute-done.refs_0_, bf16[328,128]{1,0:T(8,128)(2,1)S(1)} %collective-permute-done.1.refs_1_, bf16[328,128]{1,0:T(8,128)(2,1)S(1)} %collective-permute-done.2.refs_2_, bf16[328,128]{1,0:T(8,128)(2,1)S(1)} %collective-permute-done.3.refs_3_, ...), custom_call_target="tpu_custom_call" | custom-call | tf_op jit(solution)/shard_map/pallas_call | solution.py:274
  23.8 9.3 %all_to_all.5.state_ref = bf16[8,32,256]{2,1,0:T(8,128)(2,1)S(1)} all-to-all(bf16[8,32,256]{2,1,0:T(8,128)(2,1)S(1)} %shard_map.80), channel_id=1, replica_groups={{10,8,14,12,2,0,6,4},{11,9,15,13,3,1,7,5},{26,24,30,28,18,16,22,20},{27..., dimensions={0} | all-to-all | bytes 262144 | tf_op jit(solution)/shard_map/all_to_all | solution.py:315
  33.1 0.0 copy-done.1
  33.1 1.0 %shard_map.81 = (bf16[32,4,2,512]{3,2,1,0:T(2,128)(2,1)}, f32[32,4,2,256]{3,2,1,0:T(2,128)}) custom-call(bf16[8,32,256]{2,1,0:T(8,128)(2,1)S(1)} %all_to_all.5.state_ref, bf16[512,512]{1,0:T(8,128)(2,1)S(1)} %copy-done.1), custom_call_target="tpu_custom_call" | custom-call | tf_op jit(solution)/shard_map/pallas_call | solution.py:295
Async XLA Ops:
  2.1 13.7 %collective-permute-start = (bf16[328,128]{1,0:T(8,128)(2,1)S(1)}, bf16[328,128]{1,0:T(8,128)(2,1)S(1)}, u32[]{:S(2)}, u32[]{:S(2)}) collective-permute-start(bf16[328,128]{1,0:T(8,128)(2,1)S(1)} %get-tuple-element.15), channel_id=1, source_target_pairs={{0,12},{2,14},{4,8},{6,10},{8,4},{10,6},{12,0},{14,2},{1,13},{3,15... | collective-permute-start | bytes 251912 | tf_op jit(solution)/shard_map/ppermute | solution.py:131
  7.2 9.3 %collective-permute-start.1 = (bf16[328,128]{1,0:T(8,128)(2,1)S(1)}, bf16[328,128]{1,0:T(8,128)(2,1)S(1)}, u32[]{:S(2)}, u32[]{:S(2)}) collective-permute-start(bf16[328,128]{1,0:T(8,128)(2,1)S(1)} %get-tuple-element.16), channel_id=1, source_target_pairs={{0,14},{2,12},{4,10},{6,8},{8,6},{10,4},{12,2},{14,0},{1,15},{3,13... | collective-permute-start | bytes 251912 | tf_op jit(solution)/shard_map/ppermute | solution.py:131
  10.6 10.9 %copy-start = (bf16[8,256,256]{2,1,0:T(8,128)(2,1)S(1)}, bf16[8,256,256]{2,1,0:T(8,128)(2,1)}, u32[]{:S(2)}) copy-start(bf16[8,256,256]{2,1,0:T(8,128)(2,1)} %refs_8_.1) | copy-start | bytes 3145732
  10.6 7.5 %collective-permute-start.2 = (bf16[328,128]{1,0:T(8,128)(2,1)S(1)}, bf16[328,128]{1,0:T(8,128)(2,1)S(1)}, u32[]{:S(2)}, u32[]{:S(2)}) collective-permute-start(bf16[328,128]{1,0:T(8,128)(2,1)S(1)} %get-tuple-element.19), channel_id=1, source_target_pairs={{0,4},{2,6},{4,0},{6,2},{8,12},{10,14},{12,8},{14,10},{1,5},{3,7},... | collective-permute-start | bytes 251912 | tf_op jit(solution)/shard_map/ppermute | solution.py:131
  10.7 7.7 %collective-permute-start.3 = (bf16[328,128]{1,0:T(8,128)(2,1)S(1)}, bf16[328,128]{1,0:T(8,128)(2,1)S(1)}, u32[]{:S(2)}, u32[]{:S(2)}) collective-permute-start(bf16[328,128]{1,0:T(8,128)(2,1)S(1)} %get-tuple-element.20), channel_id=1, source_target_pairs={{0,10},{2,8},{4,14},{6,12},{8,2},{10,0},{12,6},{14,4},{1,11},{3,9}... | collective-permute-start | bytes 251912 | tf_op jit(solution)/shard_map/ppermute | solution.py:131
  14.8 6.7 %collective-permute-start.4 = (bf16[328,128]{1,0:T(8,128)(2,1)S(1)}, bf16[328,128]{1,0:T(8,128)(2,1)S(1)}, u32[]{:S(2)}, u32[]{:S(2)}) collective-permute-start(bf16[328,128]{1,0:T(8,128)(2,1)S(1)} %get-tuple-element.21), channel_id=1, source_target_pairs={{0,6},{2,4},{4,2},{6,0},{8,14},{10,12},{12,10},{14,8},{1,7},{3,5},... | collective-permute-start | bytes 251912 | tf_op jit(solution)/shard_map/ppermute | solution.py:131
  15.8 5.7 %collective-permute-start.5 = (bf16[328,128]{1,0:T(8,128)(2,1)S(1)}, bf16[328,128]{1,0:T(8,128)(2,1)S(1)}, u32[]{:S(2)}, u32[]{:S(2)}) collective-permute-start(bf16[328,128]{1,0:T(8,128)(2,1)S(1)} %get-tuple-element.22), channel_id=1, source_target_pairs={{0,8},{2,10},{4,12},{6,14},{8,0},{10,2},{12,4},{14,6},{1,9},{3,11}... | collective-permute-start | bytes 251912 | tf_op jit(solution)/shard_map/ppermute | solution.py:131
  16.5 5.0 %collective-permute-start.6 = (bf16[328,128]{1,0:T(8,128)(2,1)S(1)}, bf16[328,128]{1,0:T(8,128)(2,1)S(1)}, u32[]{:S(2)}, u32[]{:S(2)}) collective-permute-start(bf16[328,128]{1,0:T(8,128)(2,1)S(1)} %get-tuple-element.23), channel_id=1, source_target_pairs={{0,2},{2,0},{4,6},{6,4},{8,10},{10,8},{12,14},{14,12},{1,3},{3,1},... | collective-permute-start | bytes 251912 | tf_op jit(solution)/shard_map/ppermute | solution.py:131
  21.5 11.6 %copy-start.1 = (bf16[512,512]{1,0:T(8,128)(2,1)S(1)}, bf16[512,512]{1,0:T(8,128)(2,1)}, u32[]{:S(2)}) copy-start(bf16[512,512]{1,0:T(8,128)(2,1)} %readout_ref.1) | copy-start | bytes 1572868

commit v9 on v8

--- a/solution.py
+++ b/solution.py
@@ -27,8 +27,9 @@
     return sorted(range(1, peers), key=lambda k: served.index(k) if k in served else k) + [0]
 
 
-def return_flip(peers):
-    return peers // 2 + 1 if peers > 2 else 0
+def homeward(peers):
+    listed = (5, 4, 1, 0, 7, 6, 3, 2)
+    return sorted(range(peers), key=lambda place: listed.index(place) if place in listed else place)
 
 
 def store_rows(ref, at, rows):
@@ -220,6 +221,10 @@
         for part in range(parts):
             members = [(j, t) for j, t in groups if t % parts == part]
             state_half = jnp.concatenate([state[g].astype(jnp.bfloat16) for g in members], axis=0)
+            products = [
+                jnp.dot(state_half, bank_ref[halves + tile], preferred_element_type=jnp.float32)
+                for tile in range(halves)
+            ]
             masked = [
                 jnp.concatenate([share_of(state[j, t], own_share[j][tile]) for j, t in members], axis=0)
                 for tile in range(halves)
@@ -229,10 +234,6 @@
                 bank_ref[:halves].reshape(halves * units, units),
                 preferred_element_type=jnp.float32,
             )
-            products = [
-                jnp.dot(state_half, bank_ref[halves + tile], preferred_element_type=jnp.float32)
-                for tile in range(halves)
-            ]
             kept, left, right = {}, {}, {}
             for g, (j, t) in enumerate(members):
                 span = slice(g * torus_rows, (g + 1) * torus_rows)
@@ -262,7 +263,8 @@
             pieces = []
             for t in range(trajectories):
                 pieces.append(state[j, t][i * home_rows : (i + 1) * home_rows])
-            sent_ref[(i * count_y + j) ^ return_flip(peers)] = jnp.concatenate(pieces, axis=0).astype(jnp.bfloat16)
+            position = homeward(peers).index(i * count_y + j)
+            sent_ref[position] = jnp.concatenate(pieces, axis=0).astype(jnp.bfloat16)
 
 
 def run_steps(packed, tile_bank, count_x, count_y, torus_rows, home_rows):
@@ -282,7 +284,9 @@
 def readout_kernel(state_ref, readout_ref, field_ref, final_ref):
     units = state_ref.shape[-1]
     peers = state_ref.shape[0]
-    half = jnp.concatenate([state_ref[p ^ return_flip(peers)] for p in range(peers)], axis=0)
+    half = jnp.concatenate(
+        [state_ref[homeward(peers).index(place)] for place in range(peers)], axis=0
+    )
     final = half.astype(jnp.float32)
     squares = (final * final).astype(jnp.bfloat16)
     field = jnp.dot(half, readout_ref[:units], preferred_element_type=jnp.float32)
@@ -311,8 +315,7 @@
     torus_rows = frames.shape[2] * frames.shape[3]
     home_rows = start_state.size // units // peers
     sent = run_steps(packed, tile_bank, count_x, count_y, torus_rows, home_rows)
-    group = [p ^ return_flip(peers) for p in range(peers)]
-    state = lax.all_to_all(sent, PLANE, 0, 0, tiled=True, axis_index_groups=[group])
+    state = lax.all_to_all(sent, PLANE, 0, 0, tiled=True, axis_index_groups=[homeward(peers)])
     return read_out(state, readout_operator, block_shape)
 
 

time: 34.3 us -> 34.1 us (level)
  no operation moved by 1% of the time
where the time goes in v9:
time: 34.1 us; the launch traced here: 33.9 us
  starting transfers between devices  12.6 us (37%)
  blocking collectives  9.14 us (27%)
  Pallas kernels  8.11 us (24%)
  waiting for transfers between devices  3.39 us (10%)
  between operations  0.69 us (2%)
    ppermute x7, starting transfers between devices, exchange(): block = lax.ppermute(block, PLANE, [(p, p ^ k) for p in range(peers)])  12.6 us
    all_to_all x1, blocking collectives, by_trajectory(): lax.all_to_all(sent, PLANE, 0, 0, tiled=True, axis_index_groups=[homeward...  9.14 us
    pallas_call x3, Pallas kernels, pack_for_peers(): pl.pallas_call(kernel, in_specs=[pl.BlockSpec(memory_space=pltpu.HBM)] *...  4.9 us
    ppermute x7, waiting for transfers between devices, exchange(): block = lax.ppermute(block, PLANE, [(p, p ^ k) for p in range(peers)])  3.39 us
    pallas_call x1, Pallas kernels, run_steps(): pl.pallas_call(kernel, out_shape=jax.ShapeDtypeStruct((peers, home_rows,...  2.2 us
    pallas_call x1, Pallas kernels, read_out(): pl.pallas_call(readout_kernel, out_shape=(jax.ShapeDtypeStruct(block_shap...  1.01 us
  transfers between devices with their start and end apart: 7, of which 2 were waited for; matrix products, arithmetic and copies ran while one was open for 0% of the time, Pallas kernels for 10%

profile of v9, /device:TPU:0, one launch (start us, length us, event | category | flops | bytes accessed | tf_op | source)
XLA Modules:
  0.0 33.9 jit_solution(10891247854194568544)
XLA Ops:
  0.6 1.5 %shard_map.77 = (bf16[328,128]{1,0:T(8,128)(2,1)S(1)}, bf16[328,128]{1,0:T(8,128)(2,1)S(1)}) custom-call(bf16[1,32,16,2,512]{4,3,2,1,0:T(2,128)(2,1)} %refs_0_.5, f32[32,4,2,256]{3,2,1,0:T(2,128)} %refs_1_.5, s32[8,5]{1,0:T(8,128)} %bitcast.3, bf16[512,256]{1,0:T(8,128)(2,1)} %refs_3_.5), custom_call_target="tpu_custom_call" | custom-call | tf_op jit(solution)/shard_map/pallas_call | solution.py:108
  2.1 5.1 %collective-permute-start = (bf16[328,128]{1,0:T(8,128)(2,1)S(1)}, bf16[328,128]{1,0:T(8,128)(2,1)S(1)}, u32[]{:S(2)}, u32[]{:S(2)}) collective-permute-start(bf16[328,128]{1,0:T(8,128)(2,1)S(1)} %get-tuple-element.15), channel_id=1, source_target_pairs={{0,12},{2,14},{4,8},{6,10},{8,4},{10,6},{12,0},{14,2},{1,13},{3,15... | collective-permute-start | bytes 251912 | tf_op jit(solution)/shard_map/ppermute | solution.py:132
  7.2 1.1 %collective-permute-start.1 = (bf16[328,128]{1,0:T(8,128)(2,1)S(1)}, bf16[328,128]{1,0:T(8,128)(2,1)S(1)}, u32[]{:S(2)}, u32[]{:S(2)}) collective-permute-start(bf16[328,128]{1,0:T(8,128)(2,1)S(1)} %get-tuple-element.16), channel_id=1, source_target_pairs={{0,14},{2,12},{4,10},{6,8},{8,6},{10,4},{12,2},{14,0},{1,15},{3,13... | collective-permute-start | bytes 251912 | tf_op jit(solution)/shard_map/ppermute | solution.py:132
  8.4 2.2 %shard_map.78 = (bf16[328,128]{1,0:T(8,128)(2,1)S(1)}, bf16[328,128]{1,0:T(8,128)(2,1)S(1)}, bf16[328,128]{1,0:T(8,128)(2,1)S(1)}, bf16[328,128]{1,0:T(8,128)(2,1)S(1)}, bf16[328,128]{1,0:T(8,128)(2,1)S(1)}) custom-call(bf16[1,32,16,2,512]{4,3,2,1,0:T(2,128)(2,1)} %refs_0_.5, f32[32,4,2,256]{3,2,1,0:T(2,128)} %refs_1_.5, s32[8,5]{1,0:T(8,128)} %bitcast.4, ...), custom_call_target="tpu_custom_call" | custom-call | tf_op jit(solution)/shard_map/pallas_call | solution.py:108
  10.6 0.0 copy-start
  10.6 0.1 collective-permute-start.2
  10.7 4.1 %collective-permute-start.3 = (bf16[328,128]{1,0:T(8,128)(2,1)S(1)}, bf16[328,128]{1,0:T(8,128)(2,1)S(1)}, u32[]{:S(2)}, u32[]{:S(2)}) collective-permute-start(bf16[328,128]{1,0:T(8,128)(2,1)S(1)} %get-tuple-element.20), channel_id=1, source_target_pairs={{0,10},{2,8},{4,14},{6,12},{8,2},{10,0},{12,6},{14,4},{1,11},{3,9}... | collective-permute-start | bytes 251912 | tf_op jit(solution)/shard_map/ppermute | solution.py:132
  14.8 1.0 %collective-permute-start.4 = (bf16[328,128]{1,0:T(8,128)(2,1)S(1)}, bf16[328,128]{1,0:T(8,128)(2,1)S(1)}, u32[]{:S(2)}, u32[]{:S(2)}) collective-permute-start(bf16[328,128]{1,0:T(8,128)(2,1)S(1)} %get-tuple-element.21), channel_id=1, source_target_pairs={{0,6},{2,4},{4,2},{6,0},{8,14},{10,12},{12,10},{14,8},{1,7},{3,5},... | collective-permute-start | bytes 251912 | tf_op jit(solution)/shard_map/ppermute | solution.py:132
  15.8 0.0 collective-permute-done.refs_0_
  15.8 0.7 %collective-permute-start.5 = (bf16[328,128]{1,0:T(8,128)(2,1)S(1)}, bf16[328,128]{1,0:T(8,128)(2,1)S(1)}, u32[]{:S(2)}, u32[]{:S(2)}) collective-permute-start(bf16[328,128]{1,0:T(8,128)(2,1)S(1)} %get-tuple-element.22), channel_id=1, source_target_pairs={{0,8},{2,10},{4,12},{6,14},{8,0},{10,2},{12,4},{14,6},{1,9},{3,11}... | collective-permute-start | bytes 251912 | tf_op jit(solution)/shard_map/ppermute | solution.py:132
  16.5 0.0 collective-permute-done.1.refs_1_
  16.5 0.4 %collective-permute-start.6 = (bf16[328,128]{1,0:T(8,128)(2,1)S(1)}, bf16[328,128]{1,0:T(8,128)(2,1)S(1)}, u32[]{:S(2)}, u32[]{:S(2)}) collective-permute-start(bf16[328,128]{1,0:T(8,128)(2,1)S(1)} %get-tuple-element.23), channel_id=1, source_target_pairs={{0,2},{2,0},{4,6},{6,4},{8,10},{10,8},{12,14},{14,12},{1,3},{3,1},... | collective-permute-start | bytes 251912 | tf_op jit(solution)/shard_map/ppermute | solution.py:132
  16.9 1.2 %shard_map.79.refs_7_ = bf16[328,128]{1,0:T(8,128)(2,1)S(1)} custom-call(bf16[1,32,16,2,512]{4,3,2,1,0:T(2,128)(2,1)} %refs_0_.5, f32[32,4,2,256]{3,2,1,0:T(2,128)} %refs_1_.5, s32[8,5]{1,0:T(8,128)} %bitcast.5, bf16[512,256]{1,0:T(8,128)(2,1)} %refs_3_.5), custom_call_target="tpu_custom_call" | custom-call | tf_op jit(solution)/shard_map/pallas_call | solution.py:108
  18.1 0.0 collective-permute-done.2.refs_2_
  18.2 0.2 collective-permute-done.3.refs_3_
  18.4 3.2 %collective-permute-done.4.refs_4_ = bf16[328,128]{1,0:T(8,128)(2,1)S(1)} collective-permute-done((bf16[328,128]{1,0:T(8,128)(2,1)S(1)}, bf16[328,128]{1,0:T(8,128)(2,1)S(1)}, u32[]{:S(2)}, u32[]{:S(2)}) %collective-permute-start.4) | collective-permute-done | bytes 84000 | tf_op jit(solution)/shard_map/ppermute | solution.py:132
  21.5 0.0 collective-permute-done.5.refs_5_
  21.5 0.0 collective-permute-done.6.refs_6_
  21.5 0.0 copy-done
  21.5 0.0 copy-start.1
  21.5 2.2 %shard_map.80 = bf16[8,32,256]{2,1,0:T(8,128)(2,1)S(1)} custom-call(bf16[328,128]{1,0:T(8,128)(2,1)S(1)} %collective-permute-done.refs_0_, bf16[328,128]{1,0:T(8,128)(2,1)S(1)} %collective-permute-done.1.refs_1_, bf16[328,128]{1,0:T(8,128)(2,1)S(1)} %collective-permute-done.2.refs_2_, bf16[328,128]{1,0:T(8,128)(2,1)S(1)} %collective-permute-done.3.refs_3_, ...), custom_call_target="tpu_custom_call" | custom-call | tf_op jit(solution)/shard_map/pallas_call | solution.py:276
  23.7 9.1 %all_to_all.5.state_ref = bf16[8,32,256]{2,1,0:T(8,128)(2,1)S(1)} all-to-all(bf16[8,32,256]{2,1,0:T(8,128)(2,1)S(1)} %shard_map.80), channel_id=1, replica_groups={{10,8,2,0,14,12,6,4},{11,9,3,1,15,13,7,5},{26,24,18,16,30,28,22,20},{27..., dimensions={0} | all-to-all | bytes 262144 | tf_op jit(solution)/shard_map/all_to_all | solution.py:318
  32.9 0.0 copy-done.1
  32.9 1.0 %shard_map.81 = (bf16[32,4,2,512]{3,2,1,0:T(2,128)(2,1)}, f32[32,4,2,256]{3,2,1,0:T(2,128)}) custom-call(bf16[8,32,256]{2,1,0:T(8,128)(2,1)S(1)} %all_to_all.5.state_ref, bf16[512,512]{1,0:T(8,128)(2,1)S(1)} %copy-done.1), custom_call_target="tpu_custom_call" | custom-call | tf_op jit(solution)/shard_map/pallas_call | solution.py:299
Async XLA Ops:
  2.1 13.7 %collective-permute-start = (bf16[328,128]{1,0:T(8,128)(2,1)S(1)}, bf16[328,128]{1,0:T(8,128)(2,1)S(1)}, u32[]{:S(2)}, u32[]{:S(2)}) collective-permute-start(bf16[328,128]{1,0:T(8,128)(2,1)S(1)} %get-tuple-element.15), channel_id=1, source_target_pairs={{0,12},{2,14},{4,8},{6,10},{8,4},{10,6},{12,0},{14,2},{1,13},{3,15... | collective-permute-start | bytes 251912 | tf_op jit(solution)/shard_map/ppermute | solution.py:132
  7.2 9.3 %collective-permute-start.1 = (bf16[328,128]{1,0:T(8,128)(2,1)S(1)}, bf16[328,128]{1,0:T(8,128)(2,1)S(1)}, u32[]{:S(2)}, u32[]{:S(2)}) collective-permute-start(bf16[328,128]{1,0:T(8,128)(2,1)S(1)} %get-tuple-element.16), channel_id=1, source_target_pairs={{0,14},{2,12},{4,10},{6,8},{8,6},{10,4},{12,2},{14,0},{1,15},{3,13... | collective-permute-start | bytes 251912 | tf_op jit(solution)/shard_map/ppermute | solution.py:132
  10.6 10.9 %copy-start = (bf16[8,256,256]{2,1,0:T(8,128)(2,1)S(1)}, bf16[8,256,256]{2,1,0:T(8,128)(2,1)}, u32[]{:S(2)}) copy-start(bf16[8,256,256]{2,1,0:T(8,128)(2,1)} %refs_8_.1) | copy-start | bytes 3145732
  10.6 7.5 %collective-permute-start.2 = (bf16[328,128]{1,0:T(8,128)(2,1)S(1)}, bf16[328,128]{1,0:T(8,128)(2,1)S(1)}, u32[]{:S(2)}, u32[]{:S(2)}) collective-permute-start(bf16[328,128]{1,0:T(8,128)(2,1)S(1)} %get-tuple-element.19), channel_id=1, source_target_pairs={{0,4},{2,6},{4,0},{6,2},{8,12},{10,14},{12,8},{14,10},{1,5},{3,7},... | collective-permute-start | bytes 251912 | tf_op jit(solution)/shard_map/ppermute | solution.py:132
  10.7 7.7 %collective-permute-start.3 = (bf16[328,128]{1,0:T(8,128)(2,1)S(1)}, bf16[328,128]{1,0:T(8,128)(2,1)S(1)}, u32[]{:S(2)}, u32[]{:S(2)}) collective-permute-start(bf16[328,128]{1,0:T(8,128)(2,1)S(1)} %get-tuple-element.20), channel_id=1, source_target_pairs={{0,10},{2,8},{4,14},{6,12},{8,2},{10,0},{12,6},{14,4},{1,11},{3,9}... | collective-permute-start | bytes 251912 | tf_op jit(solution)/shard_map/ppermute | solution.py:132
  14.8 6.7 %collective-permute-start.4 = (bf16[328,128]{1,0:T(8,128)(2,1)S(1)}, bf16[328,128]{1,0:T(8,128)(2,1)S(1)}, u32[]{:S(2)}, u32[]{:S(2)}) collective-permute-start(bf16[328,128]{1,0:T(8,128)(2,1)S(1)} %get-tuple-element.21), channel_id=1, source_target_pairs={{0,6},{2,4},{4,2},{6,0},{8,14},{10,12},{12,10},{14,8},{1,7},{3,5},... | collective-permute-start | bytes 251912 | tf_op jit(solution)/shard_map/ppermute | solution.py:132
  15.8 5.7 %collective-permute-start.5 = (bf16[328,128]{1,0:T(8,128)(2,1)S(1)}, bf16[328,128]{1,0:T(8,128)(2,1)S(1)}, u32[]{:S(2)}, u32[]{:S(2)}) collective-permute-start(bf16[328,128]{1,0:T(8,128)(2,1)S(1)} %get-tuple-element.22), channel_id=1, source_target_pairs={{0,8},{2,10},{4,12},{6,14},{8,0},{10,2},{12,4},{14,6},{1,9},{3,11}... | collective-permute-start | bytes 251912 | tf_op jit(solution)/shard_map/ppermute | solution.py:132
  16.5 5.0 %collective-permute-start.6 = (bf16[328,128]{1,0:T(8,128)(2,1)S(1)}, bf16[328,128]{1,0:T(8,128)(2,1)S(1)}, u32[]{:S(2)}, u32[]{:S(2)}) collective-permute-start(bf16[328,128]{1,0:T(8,128)(2,1)S(1)} %get-tuple-element.23), channel_id=1, source_target_pairs={{0,2},{2,0},{4,6},{6,4},{8,10},{10,8},{12,14},{14,12},{1,3},{3,1},... | collective-permute-start | bytes 251912 | tf_op jit(solution)/shard_map/ppermute | solution.py:132
  21.5 11.3 %copy-start.1 = (bf16[512,512]{1,0:T(8,128)(2,1)S(1)}, bf16[512,512]{1,0:T(8,128)(2,1)}, u32[]{:S(2)}) copy-start(bf16[512,512]{1,0:T(8,128)(2,1)} %readout_ref.1) | copy-start | bytes 1572868

commit v10 on v9

--- a/solution.py
+++ b/solution.py
@@ -124,7 +124,7 @@
 def exchange(frames, start_state, tile_index, inlet_coupler, peers):
     order = partners(peers)
     got = []
-    for part in (order[:2], order[2:-1], order[-1:]):
+    for part in (order[:3], order[3:-1], order[-1:]):
         packed = list(pack_for_peers(frames, start_state, tile_index, inlet_coupler, peers, part))
         tile_index, packed[0] = lax.optimization_barrier((tile_index, packed[0]))
         for k, block in zip(part, packed):
@@ -229,10 +229,9 @@
                 jnp.concatenate([share_of(state[j, t], own_share[j][tile]) for j, t in members], axis=0)
                 for tile in range(halves)
             ]
-            own = jnp.dot(
-                jnp.concatenate(masked, axis=1),
-                bank_ref[:halves].reshape(halves * units, units),
-                preferred_element_type=jnp.float32,
+            own = sum(
+                jnp.dot(rows, bank_ref[tile], preferred_element_type=jnp.float32)
+                for tile, rows in enumerate(masked)
             )
             kept, left, right = {}, {}, {}
             for g, (j, t) in enumerate(members):

time: 34.1 us -> 34.1 us (level)
  transfers between devices with their start and end apart: 7 -> 7, of which waited for: 2 -> 2; matrix products, arithmetic and copies ran while one was open for 0% -> 0% of each run, Pallas kernels for 10% -> 9%
where the time goes in v10:
time: 34.1 us; the launch traced here: 33.9 us
  starting transfers between devices  12.6 us (37%)
  blocking collectives  8.85 us (26%)
  Pallas kernels  8.11 us (24%)
  waiting for transfers between devices  3.66 us (11%)
  between operations  0.69 us (2%)
    ppermute x7, starting transfers between devices, exchange(): block = lax.ppermute(block, PLANE, [(p, p ^ k) for p in range(peers)])  12.6 us
    all_to_all x1, blocking collectives, by_trajectory(): lax.all_to_all(sent, PLANE, 0, 0, tiled=True, axis_index_groups=[homeward...  8.85 us
    pallas_call x3, Pallas kernels, pack_for_peers(): pl.pallas_call(kernel, in_specs=[pl.BlockSpec(memory_space=pltpu.HBM)] *...  4.9 us
    ppermute x7, waiting for transfers between devices, exchange(): block = lax.ppermute(block, PLANE, [(p, p ^ k) for p in range(peers)])  3.66 us
    pallas_call x1, Pallas kernels, run_steps(): pl.pallas_call(kernel, out_shape=jax.ShapeDtypeStruct((peers, home_rows,...  2.19 us
    pallas_call x1, Pallas kernels, read_out(): pl.pallas_call(readout_kernel, out_shape=(jax.ShapeDtypeStruct(block_shap...  1.01 us
  transfers between devices with their start and end apart: 7, of which 2 were waited for; matrix products, arithmetic and copies ran while one was open for 0% of the time, Pallas kernels for 9%

profile of v10, /device:TPU:0, one launch (start us, length us, event | category | flops | bytes accessed | tf_op | source)
XLA Modules:
  0.0 33.9 jit_solution(3214616190353520941)
XLA Ops:
  0.6 1.7 %shard_map.77 = (bf16[328,128]{1,0:T(8,128)(2,1)S(1)}, bf16[328,128]{1,0:T(8,128)(2,1)S(1)}, bf16[328,128]{1,0:T(8,128)(2,1)S(1)}) custom-call(bf16[1,32,16,2,512]{4,3,2,1,0:T(2,128)(2,1)} %refs_0_.5, f32[32,4,2,256]{3,2,1,0:T(2,128)} %refs_1_.5, s32[8,5]{1,0:T(8,128)} %bitcast.3, bf16[512,256]{1,0:T(8,128)(2,1)} %refs_3_.5), custom_call_target="tpu_custom_call" | custom-call | tf_op jit(solution)/shard_map/pallas_call | solution.py:108
  2.3 5.1 %collective-permute-start = (bf16[328,128]{1,0:T(8,128)(2,1)S(1)}, bf16[328,128]{1,0:T(8,128)(2,1)S(1)}, u32[]{:S(2)}, u32[]{:S(2)}) collective-permute-start(bf16[328,128]{1,0:T(8,128)(2,1)S(1)} %get-tuple-element.15), channel_id=1, source_target_pairs={{0,12},{2,14},{4,8},{6,10},{8,4},{10,6},{12,0},{14,2},{1,13},{3,15... | collective-permute-start | bytes 251912 | tf_op jit(solution)/shard_map/ppermute | solution.py:132
  7.5 1.1 %collective-permute-start.1 = (bf16[328,128]{1,0:T(8,128)(2,1)S(1)}, bf16[328,128]{1,0:T(8,128)(2,1)S(1)}, u32[]{:S(2)}, u32[]{:S(2)}) collective-permute-start(bf16[328,128]{1,0:T(8,128)(2,1)S(1)} %get-tuple-element.16), channel_id=1, source_target_pairs={{0,14},{2,12},{4,10},{6,8},{8,6},{10,4},{12,2},{14,0},{1,15},{3,13... | collective-permute-start | bytes 251912 | tf_op jit(solution)/shard_map/ppermute | solution.py:132
  8.6 0.0 collective-permute-start.2
  8.6 2.0 %shard_map.78 = (bf16[328,128]{1,0:T(8,128)(2,1)S(1)}, bf16[328,128]{1,0:T(8,128)(2,1)S(1)}, bf16[328,128]{1,0:T(8,128)(2,1)S(1)}, bf16[328,128]{1,0:T(8,128)(2,1)S(1)}) custom-call(bf16[1,32,16,2,512]{4,3,2,1,0:T(2,128)(2,1)} %refs_0_.5, f32[32,4,2,256]{3,2,1,0:T(2,128)} %refs_1_.5, s32[8,5]{1,0:T(8,128)} %bitcast.4, bf16[512,256]{1,0:T(8,128)(2,1)} %refs_3_.5), custom_call_target="tpu_custom_call" | custom-call | tf_op jit(solution)/shard_map/pallas_call | solution.py:108
  10.6 0.0 copy-start
  10.6 4.2 %collective-permute-start.3 = (bf16[328,128]{1,0:T(8,128)(2,1)S(1)}, bf16[328,128]{1,0:T(8,128)(2,1)S(1)}, u32[]{:S(2)}, u32[]{:S(2)}) collective-permute-start(bf16[328,128]{1,0:T(8,128)(2,1)S(1)} %get-tuple-element.20), channel_id=1, source_target_pairs={{0,10},{2,8},{4,14},{6,12},{8,2},{10,0},{12,6},{14,4},{1,11},{3,9}... | collective-permute-start | bytes 251912 | tf_op jit(solution)/shard_map/ppermute | solution.py:132
  14.8 0.9 %collective-permute-start.4 = (bf16[328,128]{1,0:T(8,128)(2,1)S(1)}, bf16[328,128]{1,0:T(8,128)(2,1)S(1)}, u32[]{:S(2)}, u32[]{:S(2)}) collective-permute-start(bf16[328,128]{1,0:T(8,128)(2,1)S(1)} %get-tuple-element.21), channel_id=1, source_target_pairs={{0,6},{2,4},{4,2},{6,0},{8,14},{10,12},{12,10},{14,8},{1,7},{3,5},... | collective-permute-start | bytes 251912 | tf_op jit(solution)/shard_map/ppermute | solution.py:132
  15.7 0.0 collective-permute-done.refs_0_
  15.7 0.8 %collective-permute-start.5 = (bf16[328,128]{1,0:T(8,128)(2,1)S(1)}, bf16[328,128]{1,0:T(8,128)(2,1)S(1)}, u32[]{:S(2)}, u32[]{:S(2)}) collective-permute-start(bf16[328,128]{1,0:T(8,128)(2,1)S(1)} %get-tuple-element.22), channel_id=1, source_target_pairs={{0,8},{2,10},{4,12},{6,14},{8,0},{10,2},{12,4},{14,6},{1,9},{3,11}... | collective-permute-start | bytes 251912 | tf_op jit(solution)/shard_map/ppermute | solution.py:132
  16.5 0.0 collective-permute-done.1.refs_1_
  16.5 0.4 %collective-permute-start.6 = (bf16[328,128]{1,0:T(8,128)(2,1)S(1)}, bf16[328,128]{1,0:T(8,128)(2,1)S(1)}, u32[]{:S(2)}, u32[]{:S(2)}) collective-permute-start(bf16[328,128]{1,0:T(8,128)(2,1)S(1)} %get-tuple-element.23), channel_id=1, source_target_pairs={{0,2},{2,0},{4,6},{6,4},{8,10},{10,8},{12,14},{14,12},{1,3},{3,1},... | collective-permute-start | bytes 251912 | tf_op jit(solution)/shard_map/ppermute | solution.py:132
  16.9 1.2 %shard_map.79.refs_7_ = bf16[328,128]{1,0:T(8,128)(2,1)S(1)} custom-call(bf16[1,32,16,2,512]{4,3,2,1,0:T(2,128)(2,1)} %refs_0_.5, f32[32,4,2,256]{3,2,1,0:T(2,128)} %refs_1_.5, s32[8,5]{1,0:T(8,128)} %bitcast.5, bf16[512,256]{1,0:T(8,128)(2,1)} %refs_3_.5), custom_call_target="tpu_custom_call" | custom-call | tf_op jit(solution)/shard_map/pallas_call | solution.py:108
  18.1 0.0 collective-permute-done.2.refs_2_
  18.2 1.5 %collective-permute-done.3.refs_3_ = bf16[328,128]{1,0:T(8,128)(2,1)S(1)} collective-permute-done((bf16[328,128]{1,0:T(8,128)(2,1)S(1)}, bf16[328,128]{1,0:T(8,128)(2,1)S(1)}, u32[]{:S(2)}, u32[]{:S(2)}) %collective-permute-start.3) | collective-permute-done | bytes 84000 | tf_op jit(solution)/shard_map/ppermute | solution.py:132
  19.7 2.1 %collective-permute-done.4.refs_4_ = bf16[328,128]{1,0:T(8,128)(2,1)S(1)} collective-permute-done((bf16[328,128]{1,0:T(8,128)(2,1)S(1)}, bf16[328,128]{1,0:T(8,128)(2,1)S(1)}, u32[]{:S(2)}, u32[]{:S(2)}) %collective-permute-start.4) | collective-permute-done | bytes 84000 | tf_op jit(solution)/shard_map/ppermute | solution.py:132
  21.8 0.0 collective-permute-done.5.refs_5_
  21.8 0.0 collective-permute-done.6.refs_6_
  21.8 0.0 copy-done
  21.8 0.0 copy-start.1
  21.8 2.2 %shard_map.80 = bf16[8,32,256]{2,1,0:T(8,128)(2,1)S(1)} custom-call(bf16[328,128]{1,0:T(8,128)(2,1)S(1)} %collective-permute-done.refs_0_, bf16[328,128]{1,0:T(8,128)(2,1)S(1)} %collective-permute-done.1.refs_1_, bf16[328,128]{1,0:T(8,128)(2,1)S(1)} %collective-permute-done.2.refs_2_, bf16[328,128]{1,0:T(8,128)(2,1)S(1)} %collective-permute-done.3.refs_3_, ...), custom_call_target="tpu_custom_call" | custom-call | tf_op jit(solution)/shard_map/pallas_call | solution.py:275
  24.0 8.9 %all_to_all.5.state_ref = bf16[8,32,256]{2,1,0:T(8,128)(2,1)S(1)} all-to-all(bf16[8,32,256]{2,1,0:T(8,128)(2,1)S(1)} %shard_map.80), channel_id=1, replica_groups={{10,8,2,0,14,12,6,4},{11,9,3,1,15,13,7,5},{26,24,18,16,30,28,22,20},{27..., dimensions={0} | all-to-all | bytes 262144 | tf_op jit(solution)/shard_map/all_to_all | solution.py:317
  32.9 0.0 copy-done.1
  32.9 1.0 %shard_map.81 = (bf16[32,4,2,512]{3,2,1,0:T(2,128)(2,1)}, f32[32,4,2,256]{3,2,1,0:T(2,128)}) custom-call(bf16[8,32,256]{2,1,0:T(8,128)(2,1)S(1)} %all_to_all.5.state_ref, bf16[512,512]{1,0:T(8,128)(2,1)S(1)} %copy-done.1), custom_call_target="tpu_custom_call" | custom-call | tf_op jit(solution)/shard_map/pallas_call | solution.py:298
Async XLA Ops:
  2.3 13.4 %collective-permute-start = (bf16[328,128]{1,0:T(8,128)(2,1)S(1)}, bf16[328,128]{1,0:T(8,128)(2,1)S(1)}, u32[]{:S(2)}, u32[]{:S(2)}) collective-permute-start(bf16[328,128]{1,0:T(8,128)(2,1)S(1)} %get-tuple-element.15), channel_id=1, source_target_pairs={{0,12},{2,14},{4,8},{6,10},{8,4},{10,6},{12,0},{14,2},{1,13},{3,15... | collective-permute-start | bytes 251912 | tf_op jit(solution)/shard_map/ppermute | solution.py:132
  7.5 9.1 %collective-permute-start.1 = (bf16[328,128]{1,0:T(8,128)(2,1)S(1)}, bf16[328,128]{1,0:T(8,128)(2,1)S(1)}, u32[]{:S(2)}, u32[]{:S(2)}) collective-permute-start(bf16[328,128]{1,0:T(8,128)(2,1)S(1)} %get-tuple-element.16), channel_id=1, source_target_pairs={{0,14},{2,12},{4,10},{6,8},{8,6},{10,4},{12,2},{14,0},{1,15},{3,13... | collective-permute-start | bytes 251912 | tf_op jit(solution)/shard_map/ppermute | solution.py:132
  8.6 9.5 %collective-permute-start.2 = (bf16[328,128]{1,0:T(8,128)(2,1)S(1)}, bf16[328,128]{1,0:T(8,128)(2,1)S(1)}, u32[]{:S(2)}, u32[]{:S(2)}) collective-permute-start(bf16[328,128]{1,0:T(8,128)(2,1)S(1)} %get-tuple-element.17), channel_id=1, source_target_pairs={{0,4},{2,6},{4,0},{6,2},{8,12},{10,14},{12,8},{14,10},{1,5},{3,7},... | collective-permute-start | bytes 251912 | tf_op jit(solution)/shard_map/ppermute | solution.py:132
  10.6 11.2 %copy-start = (bf16[8,256,256]{2,1,0:T(8,128)(2,1)S(1)}, bf16[8,256,256]{2,1,0:T(8,128)(2,1)}, u32[]{:S(2)}) copy-start(bf16[8,256,256]{2,1,0:T(8,128)(2,1)} %refs_8_.1) | copy-start | bytes 3145732
  10.6 9.1 %collective-permute-start.3 = (bf16[328,128]{1,0:T(8,128)(2,1)S(1)}, bf16[328,128]{1,0:T(8,128)(2,1)S(1)}, u32[]{:S(2)}, u32[]{:S(2)}) collective-permute-start(bf16[328,128]{1,0:T(8,128)(2,1)S(1)} %get-tuple-element.20), channel_id=1, source_target_pairs={{0,10},{2,8},{4,14},{6,12},{8,2},{10,0},{12,6},{14,4},{1,11},{3,9}... | collective-permute-start | bytes 251912 | tf_op jit(solution)/shard_map/ppermute | solution.py:132
  14.8 7.0 %collective-permute-start.4 = (bf16[328,128]{1,0:T(8,128)(2,1)S(1)}, bf16[328,128]{1,0:T(8,128)(2,1)S(1)}, u32[]{:S(2)}, u32[]{:S(2)}) collective-permute-start(bf16[328,128]{1,0:T(8,128)(2,1)S(1)} %get-tuple-element.21), channel_id=1, source_target_pairs={{0,6},{2,4},{4,2},{6,0},{8,14},{10,12},{12,10},{14,8},{1,7},{3,5},... | collective-permute-start | bytes 251912 | tf_op jit(solution)/shard_map/ppermute | solution.py:132
  15.7 6.1 %collective-permute-start.5 = (bf16[328,128]{1,0:T(8,128)(2,1)S(1)}, bf16[328,128]{1,0:T(8,128)(2,1)S(1)}, u32[]{:S(2)}, u32[]{:S(2)}) collective-permute-start(bf16[328,128]{1,0:T(8,128)(2,1)S(1)} %get-tuple-element.22), channel_id=1, source_target_pairs={{0,8},{2,10},{4,12},{6,14},{8,0},{10,2},{12,4},{14,6},{1,9},{3,11}... | collective-permute-start | bytes 251912 | tf_op jit(solution)/shard_map/ppermute | solution.py:132
  16.5 5.3 %collective-permute-start.6 = (bf16[328,128]{1,0:T(8,128)(2,1)S(1)}, bf16[328,128]{1,0:T(8,128)(2,1)S(1)}, u32[]{:S(2)}, u32[]{:S(2)}) collective-permute-start(bf16[328,128]{1,0:T(8,128)(2,1)S(1)} %get-tuple-element.23), channel_id=1, source_target_pairs={{0,2},{2,0},{4,6},{6,4},{8,10},{10,8},{12,14},{14,12},{1,3},{3,1},... | collective-permute-start | bytes 251912 | tf_op jit(solution)/shard_map/ppermute | solution.py:132
  21.8 11.1 %copy-start.1 = (bf16[512,512]{1,0:T(8,128)(2,1)S(1)}, bf16[512,512]{1,0:T(8,128)(2,1)}, u32[]{:S(2)}) copy-start(bf16[512,512]{1,0:T(8,128)(2,1)} %readout_ref.1) | copy-start | bytes 1572868
